TPU v7x, 32 devices: a whole 2x2x4 slice. The times are simulated.
32 devices in a mesh: dp: 4 (over z), mp: 8 (over y, x, core).
Axes of the slice: x: 2, y: 2, z: 4, core: 2. Of those that a mesh axis runs over, the one named last changes fastest.
Arguments:
- tokens: bfloat16 [32768, 2048], P(('dp', 'mp')), may hold values from -6 to 6
- cotangent: bfloat16 [32768, 2048], P(('dp', 'mp')), may hold values from -0.015625 to 0.015625
- lengths: int32 [4], P('dp'), may hold values from 1024 to 8192, as said below
- inner_weight: float32 [2048, 64, 128], P('dp', 'mp'), may hold values from -0.125 to 0.125
- step_weight: float32 [2048, 64], P('dp', 'mp'), may hold values from -0.0625 to 0.0625
- state_weight: float32 [2048, 256], P('dp'), may hold values from -0.125 to 0.125
- output_weight: float32 [2048, 4096], P('dp', 'mp'), may hold values from -0.09375 to 0.09375
- inner_filter: float32 [5, 4096], P(None, 'mp'), may hold values from -3 to 3
- state_filter: float32 [5, 256], replicated, may hold values from -3 to 3
- head_params: float32 [3, 64], P(None, 'mp'), may hold values from -4 to 2.5
- norm_gain: float32 [4096], P('mp'), may hold values from 0.5 to 1.5
- inner_moments: float32 [2, 2048, 64, 128], P(None, 'dp', 'mp'), as said below
- step_moments: float32 [2, 2048, 64], P(None, 'dp', 'mp'), as said below
- state_moments: float32 [2, 2048, 256], P(None, 'dp'), as said below
- output_moments: float32 [2, 2048, 4096], P(None, 'dp', 'mp'), as said below
- inner_filter_moments: float32 [2, 5, 4096], P(None, None, 'mp'), as said below
- state_filter_moments: float32 [2, 5, 256], replicated, as said below
- head_moments: float32 [2, 3, 64], P(None, None, 'mp'), as said below
- gain_moments: float32 [2, 4096], P(None, 'mp'), as said below
Outputs:
- mixed: bfloat16 [32768, 2048], P(('dp', 'mp'))
- tokens_gradient: bfloat16 [32768, 2048], P(('dp', 'mp'))
- inner_gradient: float32 [2048, 64, 128], P('dp', 'mp')
- step_gradient: float32 [2048, 64], P('dp', 'mp')
- state_gradient: float32 [2048, 256], P('dp')
- output_gradient: float32 [2048, 4096], P('dp', 'mp')
- inner_filter_gradient: float32 [5, 4096], P(None, 'mp')
- state_filter_gradient: float32 [5, 256], replicated
- head_gradient: float32 [3, 64], P(None, 'mp')
- gain_gradient: float32 [4096], P('mp')
- inner_update: float32 [3, 2048, 64, 128], P(None, 'dp', 'mp')
- step_update: float32 [3, 2048, 64], P(None, 'dp', 'mp')
- state_update: float32 [3, 2048, 256], P(None, 'dp')
- output_update: float32 [3, 2048, 4096], P(None, 'dp', 'mp')
- inner_filter_update: float32 [3, 5, 4096], P(None, None, 'mp')
- state_filter_update: float32 [3, 5, 256], replicated
- head_update: float32 [3, 3, 64], P(None, None, 'mp')
- gain_update: float32 [3, 4096], P(None, 'mp')
Inputs may be any that keep to these rules, and one draw needn't show every extreme that they name: `lengths`: one sequence in every draw has all 8192 positions valid. `inner_moments`: row 1 (second moments) is positive. `step_moments`: row 1 (second moments) is positive. `state_moments`: row 1 (second moments) is positive. `output_moments`: row 1 (second moments) is positive. `inner_filter_moments`: row 1 (second moments) is positive. `state_filter_moments`: row 1 (second moments) is positive. `head_moments`: row 1 (second moments) is positive. `gain_moments`: row 1 (second moments) is positive.
All inputs are finite; a program needn't handle non-finite values.
Results may differ from a plain program's by a relative error of at most 0.012.
Values may be sent and summed in bfloat16 or wider, within the bound.
No kernel may reach another device: no remote copies, remote signals or barrier semaphores. Data moves between devices by JAX's collectives and lax.ppermute only.
A program may use at most 576 MiB of HBM per device.

v0:
```python
import jax
import jax.numpy as jnp
from jax import lax
from jax.sharding import PartitionSpec as P

HEAD_DIM = 64
STATE = 128
CONV = 4
BLOCK = 256
STEP = 100
INNER = 4096


highest = lax.Precision.HIGHEST
eps_norm = 1e-05
beta_one = 0.9
beta_two = 0.95
adam_eps = 1e-08
decay_rate = 0.1


def causal_filter(signal, filter_taps):
    length_now = signal.shape[0]
    padded = jnp.concatenate([jnp.zeros((CONV - 1, signal.shape[1]), jnp.float32), signal], axis=0)
    result = filter_taps[CONV]
    for offset in range(CONV):
        result = result + filter_taps[offset] * padded[offset : offset + length_now]
    return result


def block_step(state_now, inputs):
    values, step_sizes, log_decay, writer, reader = inputs
    cumulative = jnp.cumsum(log_decay, axis=0)
    causal = (jnp.arange(BLOCK)[:, None] >= jnp.arange(BLOCK)[None, :])[:, :, None]
    decay_mask = jnp.exp(
        jnp.where(causal, cumulative[:, None, :] - cumulative[None, :, :], -jnp.inf)
    )
    scores = jnp.dot(reader, writer.T, precision=highest, preferred_element_type=jnp.float32)
    weights = scores[:, :, None] * decay_mask * step_sizes[None, :, :]
    within = jnp.einsum("tsh,shp->thp", weights, values, precision=highest)
    carried = (
        jnp.einsum("tn,hnp->thp", reader, state_now, precision=highest)
        * jnp.exp(cumulative)[:, :, None]
    )
    tail_weight = jnp.exp(cumulative[-1][None, :] - cumulative) * step_sizes
    state_next = jnp.exp(cumulative[-1])[:, None, None] * state_now + jnp.einsum(
        "sn,shp->hnp", writer, tail_weight[:, :, None] * values, precision=highest
    )
    return (state_next, within + carried)


def scan_heads(values, step_sizes, log_decay, writer, reader):
    blocks = values.shape[0] // BLOCK

    def blocked(array):
        return array.reshape((blocks, BLOCK) + array.shape[1:])

    initial = jnp.zeros((values.shape[1], STATE, values.shape[2]), jnp.float32)
    last_state, outputs = lax.scan(
        jax.checkpoint(block_step),
        initial,
        (
            blocked(values),
            blocked(step_sizes),
            blocked(log_decay),
            blocked(writer),
            blocked(reader),
        ),
    )
    return outputs.reshape(values.shape)


def mixer_core(main_part, step_raw, state_raw, inner_filter, state_filter, head_params):
    positions = main_part.shape[0]
    heads_here = main_part.shape[1]
    gate_raw = main_part[:, :, :HEAD_DIM]
    signal = main_part[:, :, HEAD_DIM:].reshape(positions, heads_here * HEAD_DIM)
    signal = jax.nn.silu(causal_filter(signal, inner_filter)).reshape(
        positions, heads_here, HEAD_DIM
    )
    state_signal = jax.nn.silu(causal_filter(state_raw, state_filter))
    writer = state_signal[:, :STATE]
    reader = state_signal[:, STATE:]
    step_sizes = jax.nn.softplus(step_raw + head_params[0])
    log_decay = -step_sizes * jnp.exp(head_params[1])
    scanned = (
        scan_heads(signal, step_sizes, log_decay, writer, reader)
        + head_params[2][None, :, None] * signal
    )
    return (scanned * jax.nn.silu(gate_raw)).reshape(positions, heads_here * HEAD_DIM)


def adam_rows(weight_now, gradient, moments, decayed):
    first_moment = beta_one * moments[0] + (1.0 - beta_one) * gradient
    second_moment = beta_two * moments[1] + (1.0 - beta_two) * gradient * gradient
    direction = (
        first_moment
        / (1.0 - beta_one**STEP)
        / (jnp.sqrt(second_moment / (1.0 - beta_two**STEP)) + adam_eps)
    )
    if decayed:
        direction = direction + decay_rate * weight_now
    return jnp.stack([first_moment, second_moment, direction])


def contract_rows(left, right):
    return lax.dot_general(
        left, right, (((0,), (0,)), ((), ())), preferred_element_type=jnp.float32
    )


def contract_cols(left, right):
    return lax.dot_general(
        left, right, (((1,), (1,)), ((), ())), preferred_element_type=jnp.float32
    )


def local(
    tokens,
    cotangent,
    lengths,
    inner_weight,
    step_weight,
    state_weight,
    output_weight,
    inner_filter,
    state_filter,
    head_params,
    norm_gain,
    inner_moments,
    step_moments,
    state_moments,
    output_moments,
    inner_filter_moments,
    state_filter_moments,
    head_moments,
    gain_moments,
):
    heads_here = inner_weight.shape[1]
    main_width = heads_here * 2 * HEAD_DIM
    own_rows = tokens.shape[0]
    group_rows = own_rows * lax.axis_size("mp")
    inner_full, step_full, state_full, output_full = (
        lax.all_gather(inner_weight.astype(jnp.bfloat16), "dp", axis=0, tiled=True),
        lax.all_gather(step_weight.astype(jnp.bfloat16), "dp", axis=0, tiled=True),
        lax.all_gather(state_weight.astype(jnp.bfloat16), "dp", axis=0, tiled=True),
        lax.all_gather(output_weight.astype(jnp.bfloat16), "dp", axis=0, tiled=True),
    )
    model_width = inner_full.shape[0]
    main_columns = jnp.concatenate([inner_full.reshape(model_width, main_width), step_full], axis=1)
    columns = jnp.concatenate([main_columns, state_full], axis=1)
    gathered = lax.all_gather(tokens, "mp", axis=0, tiled=True)
    projected = jnp.dot(gathered, columns, preferred_element_type=jnp.float32)
    state_raw = projected[:, main_width + heads_here :]
    main_part = projected[:, :main_width].reshape(group_rows, heads_here, 2 * HEAD_DIM)
    step_raw = projected[:, main_width : main_width + heads_here]
    gated_out, pullback = jax.vjp(
        mixer_core, main_part, step_raw, state_raw, inner_filter, state_filter, head_params
    )
    squares = lax.psum(jnp.sum(gated_out * gated_out, axis=1), "mp")
    norm_scale = lax.rsqrt(squares[:, None] / INNER + eps_norm)
    normed = (gated_out * norm_scale * norm_gain).astype(jnp.bfloat16)
    row_block = normed
    branch = lax.psum_scatter(
        contract_cols(row_block, output_full), "mp", scatter_dimension=0, tiled=True
    )
    my_index = lax.axis_index("mp")
    positions = my_index * own_rows + jnp.arange(own_rows)
    live_mask = (positions < lengths[0]).astype(jnp.float32)
    mixed = (tokens.astype(jnp.float32) + live_mask[:, None] * branch).astype(jnp.bfloat16)
    masked_cot = (cotangent.astype(jnp.float32) * live_mask[:, None]).astype(jnp.bfloat16)
    cotangent_group = lax.all_gather(masked_cot, "mp", axis=0, tiled=True)
    normed_grad = jnp.dot(cotangent_group, output_full, preferred_element_type=jnp.float32)
    output_grad = contract_rows(cotangent_group, normed)
    scaled = normed_grad * norm_gain
    inner_sum = lax.psum(jnp.sum(scaled * gated_out, axis=1), "mp")
    gated_grad = scaled * norm_scale - gated_out * norm_scale**3 * inner_sum[:, None] / INNER
    gain_grad = jnp.sum(normed_grad * gated_out * norm_scale, axis=0)
    main_grad, step_grad, state_partial, inner_filter_grad, state_filter_partial, head_grad = (
        pullback(gated_grad)
    )
    state_grad, state_filter_grad = lax.psum((state_partial, state_filter_partial), "mp")
    state_low = state_grad.astype(jnp.bfloat16)
    main_back = jnp.concatenate(
        [main_grad.reshape(group_rows, main_width), step_grad], axis=1
    ).astype(jnp.bfloat16)
    row_block = main_back
    input_part = lax.psum_scatter(
        contract_cols(row_block, main_columns), "mp", scatter_dimension=0, tiled=True
    )
    own_state_grad = lax.dynamic_slice_in_dim(state_low, my_index * own_rows, own_rows, 0)
    tokens_gradient = (
        cotangent.astype(jnp.float32) + input_part + contract_cols(own_state_grad, state_full)
    ).astype(jnp.bfloat16)
    main_weight_grad = contract_rows(gathered, main_back)
    state_weight_grad = contract_rows(gathered, state_low)
    inner_grad_full = main_weight_grad[:, :main_width].reshape(
        model_width, heads_here, 2 * HEAD_DIM
    )
    step_grad_full = main_weight_grad[:, main_width:]
    inner_gradient, step_gradient, state_gradient, output_gradient = (
        lax.psum_scatter(inner_grad_full, "dp", scatter_dimension=0, tiled=True),
        lax.psum_scatter(step_grad_full, "dp", scatter_dimension=0, tiled=True),
        lax.psum_scatter(state_weight_grad, "dp", scatter_dimension=0, tiled=True),
        lax.psum_scatter(output_grad, "dp", scatter_dimension=0, tiled=True),
    )
    inner_filter_gradient, state_filter_gradient, head_gradient, gain_gradient = lax.psum(
        (inner_filter_grad, state_filter_grad, head_grad, gain_grad), "dp"
    )
    inner_update = adam_rows(inner_weight, inner_gradient, inner_moments, True)
    step_update = adam_rows(step_weight, step_gradient, step_moments, True)
    state_update = adam_rows(state_weight, state_gradient, state_moments, True)
    output_update = adam_rows(output_weight, output_gradient, output_moments, True)
    inner_filter_update = adam_rows(inner_filter, inner_filter_gradient, inner_filter_moments, True)
    state_filter_update = adam_rows(state_filter, state_filter_gradient, state_filter_moments, True)
    head_update = adam_rows(head_params, head_gradient, head_moments, False)
    gain_update = adam_rows(norm_gain, gain_gradient, gain_moments, False)
    return (
        mixed,
        tokens_gradient,
        inner_gradient,
        step_gradient,
        state_gradient,
        output_gradient,
        inner_filter_gradient,
        state_filter_gradient,
        head_gradient,
        gain_gradient,
        inner_update,
        step_update,
        state_update,
        output_update,
        inner_filter_update,
        state_filter_update,
        head_update,
        gain_update,
    )


def solution(mesh):
    return jax.shard_map(
        local,
        mesh=mesh,
        in_specs=(
            P(("dp", "mp"), None),
            P(("dp", "mp"), None),
            P("dp"),
            P("dp", "mp", None),
            P("dp", "mp"),
            P("dp", None),
            P("dp", "mp"),
            P(None, "mp"),
            P(),
            P(None, "mp"),
            P("mp"),
            P(None, "dp", "mp", None),
            P(None, "dp", "mp"),
            P(None, "dp", None),
            P(None, "dp", "mp"),
            P(None, None, "mp"),
            P(),
            P(None, None, "mp"),
            P(None, "mp"),
        ),
        out_specs=(
            P(("dp", "mp"), None),
            P(("dp", "mp"), None),
            P("dp", "mp", None),
            P("dp", "mp"),
            P("dp", None),
            P("dp", "mp"),
            P(None, "mp"),
            P(),
            P(None, "mp"),
            P("mp"),
            P(None, "dp", "mp", None),
            P(None, "dp", "mp"),
            P(None, "dp", None),
            P(None, "dp", "mp"),
            P(None, None, "mp"),
            P(),
            P(None, None, "mp"),
            P(None, "mp"),
        ),
        check_vma=False,
    )
```

profile of v0, /device:TPU:0, one launch (start us, length us, event | category | flops | bytes accessed | tf_op | source)
XLA Modules:
  0.0 4202.8 jit_solution(6419928798441403018)
XLA Ops:
  20.5 15.0 all_gather.19
  37.2 56.9 %all-gather.6.cloned.1.call-done = bf16[2048,8,128]{2,1,0:T(8,128)(2,1)} async-done(((bf16[512,8,128]{2,1,0:T(8,128)(2,1)}), bf16[2048,8,128]{2,1,0:T(8,128)(2,1)}) %all-gather.6.cloned.1.call-update) | async-done | bytes 4194320 | tf_op jit(solution)/shard_map/all_gather | solution.py:144
  99.4 23.4 all-gather.8.cloned.1.call-done
  132.4 152.6 %all-gather.10.cloned.1.call-done = bf16[8192,2048]{1,0:T(8,128)(2,1)} async-done(((bf16[1024,2048]{1,0:T(8,128)(2,1)}), bf16[8192,2048]{1,0:T(8,128)(2,1)}) %all-gather.10.cloned.1.call-update) | async-done | bytes 33554448 | tf_op jit(solution)/shard_map/all_gather | solution.py:152
  285.0 57.3 %convolution_bitcast_fusion.4 = f32[8192,1288]{0,1:T(8,128)} fusion(bf16[2048,1288]{1,0:T(8,128)(2,1)} %concatenate.17, bf16[8192,2048]{1,0:T(8,128)(2,1)} %all-gather.10.cloned.1.call-done), kind=kOutput, calls=%fused_computation.116 | convolution fusion | flops 43218108416 | bytes 81035264 | tf_op jit(solution)/shard_map/dot_general | solution.py:153
  342.3 24.1 slice.252
  385.6 39.0 fusion.101
  435.9 19.3 copy.131
  455.2 21.9 fusion.110
  505.8 768.4 %while.41 = (s32[]{:T(128)}, f32[8,128,64]{1,2,0:T(8,128)S(1)}, f32[32,256,8,64]{1,0,3,2:T(8,128)}, f32[32,8,128,64]{2,3,1,0:T(8,128)}, f32[32,256,8]{1,2,0:T(8,...) while((s32[]{:T(128)}, f32[8,128,64]{1,2,0:T(8,128)S(1)}, ...), condition=%wide.region_3.4_spmd.clone, body=%wide.region_0.3_spmd.clone.sunk | while | flops 908922880 | bytes 7541051 | solution.py:59
  1115.5 12.9 dynamic_update_slice.79
  1187.6 12.9 dynamic_update_slice.79
  1259.7 12.9 dynamic_update_slice.79
  1274.3 18.2 reshape.397
  1292.5 23.5 multiply_reduce_fusion.9
  1316.1 24.1 psum.56
  1340.3 29.6 fusion.99
  1369.9 22.5 psum.57
  1392.4 19.1 fusion.96
  1411.6 41.1 multiply_reduce_fusion.4
  1452.6 15.9 copy.217
  1482.2 1210.9 %while.42 = (s32[]{:T(128)}, f32[8,128,64]{1,2,0:T(8,128)S(1)}, f32[32,256,8,64]{1,0,3,2:T(8,128)}, f32[32,256,8]{1,2,0:T(8,128)S(1)}, f32[32,256,8]{1,2,0:T(8,1...) while((s32[]{:T(128)}, f32[8,128,64]{1,2,0:T(8,128)S(1)}, ...), condition=%wide.region_22.23_spmd.clone, body=%wide.region_9.22_spmd.clone.sunk | while | flops 2124961792 | bytes 18491572 | solution.py:59
  1507.0 12.9 dynamic_update_slice.84
  1544.8 12.9 dynamic_update_slice.84
  1582.7 12.9 dynamic_update_slice.84
  1620.5 12.9 dynamic_update_slice.84
  1658.3 12.9 dynamic_update_slice.84
  1696.2 12.9 dynamic_update_slice.84
  1734.0 12.9 dynamic_update_slice.84
  1771.9 12.9 dynamic_update_slice.84
  2693.1 18.3 reshape.402
  2711.4 18.1 multiply_add_fusion
  2729.5 44.2 %multiply_reduce_fusion.8 = (f32[512]{0:T(512)}, f32[512]{0:T(512)}, f32[512]{0:T(512)}, f32[512]{0:T(512)}, f32[512]{0:T(512)}, /*index=5*/f32[8192,512]{0,1:T(8,128)}) fusion(f32[8192,8,64]{0,2,1:T(8,128)} %slice.253, f32[8192,512]{0,1:T(8,128)} %bitcast.521, f32[8192,512]{0,1:T(8,128)} %get-tuple-element.756, f32[8192,8,64]{0,2,1:T(8,128)} %multiply_add_fusion), kind=kLoop, calls=%fused_computation.146 | loop fusion | flops 75494912 | bytes 83896320 | tf_op jit(solution)/shard_map/transpose(jvp())/reduce_sum | solution.py:27
  2784.9 19.4 multiply_reduce_fusion.13
  2815.9 17.2 pad_add_fusion.3
  2833.2 26.3 broadcast_multiply_fusion
  2861.4 29.7 pad_add_fusion
  2891.1 17.3 add_convert_fusion
  2908.4 41.3 fusion.104
  2953.8 168.9 %all-reduce.32 = (bf16[8192,256]{0,1:T(8,128)(2,1)}, f32[5,256]{1,0:T(8,128)}) all-reduce(f32[8192,256]{0,1:T(8,128)} %pad_add_fusion.3, f32[5,256]{1,0:T(8,128)S(1)} %pad_add_fusion.7), channel_id=1, replica_groups=mesh['dp'=4,'mp'=8] {'mp'}, use_global_device_ids=true, to_apply=%region_24.25 | all-reduce | flops 2098432 | bytes 12593152 | tf_op jit(solution)/shard_map/psum | solution.py:182
  3122.6 17.2 convolution_bitcast_fusion.5
  3139.9 25.2 fusion.172
  3183.9 30.0 fusion.171
  3215.0 51.6 %fusion.103 = f32[8192,2048]{1,0:T(8,128)} fusion(bf16[8192,8]{0,1:T(8,128)(2,1)S(1)} %get-tuple-element.748, bf16[8192,1024]{0,1:T(8,128)(2,1)} %bitcast.536, bf16[2048,8]{1,0:T(8,128)(2,1)S(1)} %copy-done.8, bf16[2048,1024]{1,0:T(8,128)(2,1)} %bitcast.540), kind=kOutput, calls=%fused_computation.159 | convolution fusion | flops 34670444544 | bytes 88244224 | tf_op jit(solution)/shard_map/dot_general | solution.py:113
  3270.5 20.7 all-reduce.30
  3307.7 104.6 %reduce-scatter.11.cloned.1.call-done = f32[512,8,128]{2,1,0:T(8,128)} async-done(((f32[2048,8,128]{2,1,0:T(8,128)}), f32[512,8,128]{2,1,0:T(8,128)}) %reduce-scatter.11.cloned.1.call-update) | async-done | bytes 2097168 | tf_op jit(solution)/shard_map/reduce_scatter | solution.py:202
  3419.7 380.9 %reduce-scatter.7.cloned.1.call-done = f32[1024,2048]{1,0:T(8,128)} async-done(((f32[8192,2048]{1,0:T(8,128)}), f32[1024,2048]{1,0:T(8,128)}) %reduce-scatter.7.cloned.1.call-update) | async-done | bytes 8388624 | tf_op jit(solution)/shard_map/reduce_scatter | solution.py:164
  3808.2 379.7 %reduce-scatter.9.cloned.1.call-done = f32[1024,2048]{1,0:T(8,128)} async-done(((f32[8192,2048]{1,0:T(8,128)}), f32[1024,2048]{1,0:T(8,128)}) %reduce-scatter.9.cloned.1.call-update) | async-done | bytes 8388624 | tf_op jit(solution)/shard_map/reduce_scatter | solution.py:188
  (1923 shorter events, 2025.2 us)
Async XLA Ops:
  7.2 86.9 %all-gather.6.cloned.1.call-start = ((), (), s32[]{:S(2)}) async-start(), calls=%async_computation.6 | async-start | bytes 5242880 | tf_op jit(solution)/shard_map/all_gather | solution.py:144
  10.0 112.8 %all-gather.8.cloned.1.call-start = ((), (), s32[]{:S(2)}) async-start(), calls=%async_computation.7 | async-start | bytes 1310720 | tf_op jit(solution)/shard_map/all_gather | solution.py:146
  11.9 273.1 %all-gather.10.cloned.1.call-start = ((), (), s32[]{:S(2)}) async-start(), calls=%async_computation.8 | async-start | bytes 37748736 | tf_op jit(solution)/shard_map/all_gather | solution.py:152
  12.6 23.2 copy-start.14
  12.6 23.3 copy-start.19
  12.6 24.0 copy-start.67
  12.6 1327.6 %all-gather.12.cloned.1.call-start = ((), (), s32[]{:S(2)}) async-start(), calls=%async_computation.9 | async-start | bytes 2621440 | tf_op jit(solution)/shard_map/all_gather | solution.py:147
  13.6 1326.7 %all-gather.14.cloned.1.call-start = ((), (), s32[]{:S(2)}) async-start(), calls=%async_computation.11 | async-start | bytes 37748736 | tf_op jit(solution)/shard_map/all_gather | solution.py:172
  19.8 3274.0 %reduce-scatter.13.cloned.1.call-start = ((), (), s32[]{:S(2)}) async-start(), calls=%async_computation.14 | async-start | bytes 81920 | tf_op jit(solution)/shard_map/reduce_scatter | solution.py:203
  35.8 96.5 %copy-start.7 = (bf16[2048,8]{1,0:T(8,128)(2,1)}, bf16[2048,8]{1,0:T(8,128)(2,1)S(1)}, u32[]{:S(2)}) copy-start(bf16[2048,8]{1,0:T(8,128)(2,1)S(1)} %copy.130) | copy-start | bytes 98308
  35.9 349.7 %copy-start.22 = (f32[1,512]{1,0:T(1,128)}, f32[1,512]{1,0:T(1,128)S(1)}, u32[]{:S(2)}) copy-start(f32[1,512]{1,0:T(1,128)S(1)} %get-tuple-element.806) | copy-start | bytes 6148
  35.9 349.7 %copy-start.24 = (f32[1,512]{1,0:T(1,128)}, f32[1,512]{1,0:T(1,128)S(1)}, u32[]{:S(2)}) copy-start(f32[1,512]{1,0:T(1,128)S(1)} %get-tuple-element.807) | copy-start | bytes 6148
  35.9 349.7 %copy-start.26 = (f32[1,512]{1,0:T(1,128)}, f32[1,512]{1,0:T(1,128)S(1)}, u32[]{:S(2)}) copy-start(f32[1,512]{1,0:T(1,128)S(1)} %get-tuple-element.808) | copy-start | bytes 6148
  35.9 349.7 %copy-start.28 = (f32[1,512]{1,0:T(1,128)}, f32[1,512]{1,0:T(1,128)S(1)}, u32[]{:S(2)}) copy-start(f32[1,512]{1,0:T(1,128)S(1)} %get-tuple-element.809) | copy-start | bytes 6148
  435.9 19.3 copy-start.32
  435.9 19.3 copy-start.34
  435.9 19.3 copy-start.36
  435.9 19.3 copy-start.38
  435.9 19.3 copy-start.58
  1274.3 18.3 copy-start.45
  1292.5 47.8 %copy-start.61 = (f32[512]{0:T(512)S(1)}, f32[512]{0:T(512)}, u32[]{:S(2)}) copy-start(f32[512]{0:T(512)} %param.33) | copy-start | bytes 6148
  2693.1 18.3 copy-start.46
  2784.9 19.5 copy-start.33
  2784.9 19.5 copy-start.35
  2784.9 19.5 copy-start.37
  2784.9 19.5 copy-start.39
  2815.9 17.3 copy-start.29
  2833.2 26.4 copy-start.10
  2833.2 26.4 copy-start.50
  2833.2 26.4 copy-start.52
  2908.4 45.3 %copy-start.53 = (f32[256]{0:T(256)S(1)}, f32[256]{0:T(256)}, u32[]{:S(2)}) copy-start(f32[256]{0:T(256)} %get-tuple-element.673) | copy-start | bytes 3076
  2908.4 45.4 %copy-start.54 = (f32[256]{0:T(256)S(1)}, f32[256]{0:T(256)}, u32[]{:S(2)}) copy-start(f32[256]{0:T(256)} %get-tuple-element.674) | copy-start | bytes 3076
  2908.4 45.4 %copy-start.55 = (f32[256]{0:T(256)S(1)}, f32[256]{0:T(256)}, u32[]{:S(2)}) copy-start(f32[256]{0:T(256)} %get-tuple-element.675) | copy-start | bytes 3076
  2908.4 45.4 %copy-start.56 = (f32[256]{0:T(256)S(1)}, f32[256]{0:T(256)}, u32[]{:S(2)}) copy-start(f32[256]{0:T(256)} %get-tuple-element.676) | copy-start | bytes 3076
  2908.4 45.4 %copy-start.57 = (f32[256]{0:T(256)S(1)}, f32[256]{0:T(256)}, u32[]{:S(2)}) copy-start(f32[256]{0:T(256)} %get-tuple-element.677) | copy-start | bytes 3076
  2953.6 341.5 %reduce-scatter.15.cloned.1.call-start = ((), (), s32[]{:S(2)}) async-start(), calls=%async_computation.15 | async-start | bytes 2621440 | tf_op jit(solution)/shard_map/reduce_scatter | solution.py:204
  3139.9 163.2 %reduce-scatter.17.cloned.1.call-start = ((), (), s32[]{:S(2)}) async-start(), calls=%async_computation.16 | async-start | bytes 5242880 | tf_op jit(solution)/shard_map/reduce_scatter | solution.py:205
  3165.1 247.2 %reduce-scatter.11.cloned.1.call-start = ((), (), s32[]{:S(2)}) async-start(), calls=%async_computation.13 | async-start | bytes 10485760 | tf_op jit(solution)/shard_map/reduce_scatter | solution.py:202
  3182.3 618.3 %reduce-scatter.7.cloned.1.call-start = ((), (), s32[]{:S(2)}) async-start(), calls=%async_computation.10 | async-start | bytes 75497472 | tf_op jit(solution)/shard_map/reduce_scatter | solution.py:164
  3213.9 974.0 %reduce-scatter.9.cloned.1.call-start = ((), (), s32[]{:S(2)}) async-start(), calls=%async_computation.12 | async-start | bytes 75497472 | tf_op jit(solution)/shard_map/reduce_scatter | solution.py:188
  3266.7 24.5 copy-start.20
  3266.7 25.2 copy-start.15
  3266.7 27.1 copy-start.12
  3266.7 27.1 copy-start.18
  3267.6 35.5 copy-start.5
  3297.9 114.4 %copy-start.1 = (f32[512,8,128]{2,1,0:T(8,128)S(1)}, f32[512,8,128]{2,1,0:T(8,128)}, u32[]{:S(2)}) copy-start(f32[512,8,128]{2,1,0:T(8,128)} %param.26) | copy-start | bytes 6291460
  3416.6 384.0 %copy-start.17 = (f32[1024]{0:T(1024)S(1)}, f32[1024]{0:T(1024)}, u32[]{:S(2)}) copy-start(f32[1024]{0:T(1024)} %copy-done.16) | copy-start | bytes 12292
  3419.7 768.3 %copy-start.6 = (bf16[2048,256]{1,0:T(8,128)(2,1)S(1)}, bf16[2048,256]{1,0:T(8,128)(2,1)}, u32[]{:S(2)}) copy-start(bf16[2048,256]{1,0:T(8,128)(2,1)} %all-gather.8.cloned.1.call-done) | copy-start | bytes 3145732
  (33 other events, 224.2 us)
Sparse Core Ops, SparseCore 0:
  10.2 83.8 all-gather.5
  96.3 26.4 all-gather.7
  124.7 160.2 all-gather.9
  287.0 45.9 all-gather.11
  334.7 159.4 all-gather.13
  2953.8 19.1 reduce-scatter.12
  3140.0 44.3 reduce-scatter.14
  3187.2 76.0 reduce-scatter.16
  3266.4 145.8 reduce-scatter.10
  3416.1 384.4 reduce-scatter.6
  3804.2 383.7 reduce-scatter.8
where the time goes:
time: 4240 us; the launch traced here: 4200 us
  local copies, waits for them, and re-layouts  1360 us (32%)
  waiting for transfers between devices  1100 us (26%)
  matrix products  892 us (21%)
  other arithmetic  582 us (14%)
  blocking collectives  251 us (6%)
    dynamic_update_slice x128, local copies, waits for them, and re-layouts, scan_heads(): lax.scan(jax.checkpoint(block_step), initial, (blocked(values), blocked(s...  855 us
    reduce_scatter x1, waiting for transfers between devices, local(): lax.psum_scatter(contract_cols(row_block, output_full), 'mp', scatter_dim...  381 us
    reduce_scatter x1, waiting for transfers between devices, local(): lax.psum_scatter(contract_cols(row_block, main_columns), 'mp', scatter_di...  380 us
    dot_general x96, matrix products, block_step(): within = jnp.einsum('tsh,shp->thp', weights, values, precision=highest)  283 us
    psum x1, blocking collectives, local(): lax.psum((state_partial, state_filter_partial), 'mp')  169 us
    all_gather x1, waiting for transfers between devices, local(): gathered = lax.all_gather(tokens, 'mp', axis=0, tiled=True)  153 us
    another operation x225, other arithmetic  140 us
    dot_general x128, matrix products, block_step(): jnp.dot(reader, writer.T, precision=highest, preferred_element_type=jnp.f...  129 us
  transfers between devices with their start and end apart: 11, of which 6 were waited for; matrix products, arithmetic and copies ran while one was open for 29% of the time, Pallas kernels for 0%

commit v1 on v0

v1 whole, which is shorter than its diff:
```python
import functools

import jax
import jax.numpy as jnp
from jax import lax
from jax.experimental import pallas as pl
from jax.experimental.pallas import tpu as pltpu
from jax.sharding import PartitionSpec as P

HEAD_DIM = 64
STATE = 128
CONV = 4
BLOCK = 256
STEP = 100
INNER = 4096

highest = lax.Precision.HIGHEST
eps_norm = 1e-05
beta_one = 0.9
beta_two = 0.95
adam_eps = 1e-08
decay_rate = 0.1

f32 = jnp.float32
bf16 = jnp.bfloat16

KINDS = 5
A_COL, EA_COL, W_COL, WDEV_COL, EADEV_COL = range(KINDS)


def dot(left, right, dims=((1,), (0,))):
    return lax.dot_general(left, right, (dims, ((), ())), preferred_element_type=f32)


NT = ((1,), (1,))


def exact_dot(left, right, dims=((1,), (0,))):
    return lax.dot_general(
        left, right, (dims, ((), ())), precision=highest, preferred_element_type=f32
    )


def sigmoid(value):
    return 1.0 / (1.0 + jnp.exp(-value))


def expand(cols, kind, heads):
    rows = cols.shape[0]
    first = lax.broadcasted_iota(jnp.int32, (rows, 128), 1) < HEAD_DIM
    tiles = []
    for pair in range(heads // 2):
        at = kind * heads + 2 * pair
        tiles.append(jnp.where(first, cols[:, at : at + 1], cols[:, at + 1 : at + 2]))
    return tiles[0] if len(tiles) == 1 else jnp.concatenate(tiles, axis=1)


def head_sums(value, heads):
    first = lax.broadcasted_iota(jnp.int32, (value.shape[0], 128), 1) < HEAD_DIM
    sums = []
    for pair in range(heads // 2):
        tile = value[:, 128 * pair : 128 * (pair + 1)]
        sums.append(jnp.sum(jnp.where(first, tile, 0.0), axis=1, keepdims=True))
        sums.append(jnp.sum(jnp.where(first, 0.0, tile), axis=1, keepdims=True))
    return sums


def head_mask(width, head):
    lanes = lax.broadcasted_iota(jnp.int32, (1, width), 1)
    return jnp.where(lanes // HEAD_DIM == head, 1.0, 0.0).astype(bf16)


def block_rows(index):
    return pl.ds(pl.multiple_of(index * BLOCK, BLOCK), BLOCK)


def filtered(extended, taps, base):
    result = taps[CONV : CONV + 1]
    for offset in range(CONV):
        begin = base + 8 - (CONV - 1) + offset
        result = result + taps[offset : offset + 1] * extended[begin : begin + BLOCK]
    return result


def decay_of(cols_block, arow_ref, block, head, heads, causal):
    column = cols_block[:, A_COL * heads + head : A_COL * heads + head + 1]
    row = arow_ref[0, block, head : head + 1, :]
    return jnp.exp(jnp.where(causal, column - row, -jnp.inf))


def causal_mask():
    rows = lax.broadcasted_iota(jnp.int32, (BLOCK, BLOCK), 0)
    return rows >= lax.broadcasted_iota(jnp.int32, (BLOCK, BLOCK), 1)


def load_signal(part_ref, halo_ref, xext, width):
    rows = part_ref.shape[1]
    xext[0:8] = halo_ref[0, :, width:].astype(f32)
    xext[8 : 8 + rows] = part_ref[0, :, width:].astype(f32)


def state_kernel(width, part_ref, halo_ref, par_ref, cols_ref, bt_ref, state_ref, xext, weighted):
    heads = width // HEAD_DIM
    rows = part_ref.shape[1]
    load_signal(part_ref, halo_ref, xext, width)
    taps = par_ref[0, :, width:]
    for block in range(rows // BLOCK):
        at = pl.ds(block * BLOCK, BLOCK)
        u = filtered(xext, taps, block * BLOCK)
        weight = expand(cols_ref[0, at, :], WDEV_COL, heads)
        weighted[at] = (u * sigmoid(u) * weight).astype(bf16)
    state_ref[0] = dot(bt_ref[...], weighted[...])


def forward_kernel(
    width, part_ref, halo_ref, par_ref, cols_ref, arow_ref, b_ref, c_ref, bt_ref, sin_ref,
    gated_ref, sq_ref, xext, signal, scores, state, squares,
):
    heads = width // HEAD_DIM
    rows = part_ref.shape[1]
    blocks = rows // BLOCK

    @pl.when(pl.program_id(0) == 0)
    def _():
        squares[...] = jnp.zeros_like(squares)
        for block in range(blocks):
            at = pl.ds(block * BLOCK, BLOCK)
            scores[block] = exact_dot(c_ref[at], b_ref[at], NT)

    load_signal(part_ref, halo_ref, xext, width)
    taps = par_ref[0, :, width:]
    gain = par_ref[0, 5:6, width:]
    skip = par_ref[0, 6:7, width:]
    for block in range(blocks):
        u = filtered(xext, taps, block * BLOCK)
        signal[pl.ds(block * BLOCK, BLOCK)] = u * sigmoid(u)
    state[...] = sin_ref[0]

    def body(block, carry):
        at = block_rows(block)
        causal = causal_mask()
        cols = cols_ref[0, at, :]
        x = signal[at]
        xl = x.astype(bf16)
        s = state[...].astype(bf16)
        ea = expand(cols, EA_COL, heads)
        y = ea * dot(c_ref[at].astype(bf16), s)
        g = scores[block]
        for head in range(heads):
            m = (g * decay_of(cols, arow_ref, block, head, heads, causal)).astype(bf16)
            y = y + dot(m, xl * head_mask(width, head))
        z = part_ref[0, at, :width].astype(f32)
        gated = (y + skip * x) * (z * sigmoid(z))
        gated_ref[0, at, :] = (gated * gain).astype(bf16)
        sq = gated * gated
        total = sq[:, :128]
        for tile in range(1, width // 128):
            total = total + sq[:, 128 * tile : 128 * (tile + 1)]
        squares[at] += total
        weight = expand(cols, W_COL, heads)
        bt = bt_ref[block]
        state[...] = ea[BLOCK - 1 :] * state[...] + dot(bt, (weight * x).astype(bf16))
        return carry

    lax.fori_loop(0, blocks, body, 0)

    @pl.when(pl.program_id(0) == pl.num_programs(0) - 1)
    def _():
        sq_ref[...] = jnp.sum(squares[...], axis=1, keepdims=True)


def gate_grads(part, normed_grad, gained, par, rowcols, width):
    z = part[:, :width].astype(f32)
    gain = par[5:6, width:]
    gated = gained.astype(f32) * (1.0 / gain)
    grad = rowcols[:, 0:1] * (normed_grad.astype(f32) * gain) - rowcols[:, 1:2] * gated
    sz = sigmoid(z)
    return grad, z * sz, sz * (1.0 + z * (1.0 - sz))


def back_state_kernel(
    width, part_ref, ngrad_ref, gated_ref, par_ref, cols_ref, row_ref, ct_ref,
    dstate_ref, gain_ref, weighted,
):
    heads = width // HEAD_DIM
    rows = part_ref.shape[1]
    gain_sum = jnp.zeros((8, width), f32)
    for block in range(rows // BLOCK):
        at = pl.ds(block * BLOCK, BLOCK)
        ngrad = ngrad_ref[0, at, :]
        gated = gated_ref[0, at, :]
        grad, silu_z, _ = gate_grads(
            part_ref[0, at, :], ngrad, gated, par_ref[0], row_ref[at], width
        )
        weight = expand(cols_ref[0, at, :], EADEV_COL, heads)
        weighted[at] = (grad * silu_z * weight).astype(bf16)
        prod = ngrad.astype(f32) * gated.astype(f32) * row_ref[at, 0:1]
        gain_sum = gain_sum + jnp.sum(prod.reshape(BLOCK // 8, 8, width), axis=0)
    dstate_ref[0] = dot(ct_ref[...], weighted[...])
    gain_ref[0] = gain_sum * (1.0 / par_ref[0, 5:6, width:])


def product_terms(left, right):
    lane = lax.broadcasted_iota(jnp.int32, (left.shape[0], 128), 1)
    first = lane < HEAD_DIM
    terms = []
    for pair in range(left.shape[1] // 128):
        tile = slice(128 * pair, 128 * (pair + 1))
        value = left[:, tile]
        other = right[:, tile]
        value_high = value.astype(bf16).astype(f32)
        other_high = other.astype(bf16).astype(f32)
        value_low = value - value_high
        other_low = (other - other_high).astype(bf16)
        turned_high = pltpu.roll(value_high, HEAD_DIM, 1)
        turned_low = pltpu.roll(value_low, HEAD_DIM, 1)
        other_turned = pltpu.roll(other_high, HEAD_DIM, 1)
        for even in (True, False):
            if even:
                one = jnp.where(first, value_high, turned_low)
                two = jnp.where(first, value_high, 0.0)
                both = jnp.where(first, other_high, other_turned)
            else:
                one = jnp.where(first, turned_high, value_low)
                two = jnp.where(first, 0.0, value_high)
                both = jnp.where(first, other_turned, other_high)
            terms.append(
                (
                    jnp.concatenate([one.astype(bf16), two.astype(bf16)], axis=1),
                    jnp.concatenate([both.astype(bf16), other_low], axis=1),
                )
            )
    return terms


def fold_rows(value):
    return jnp.sum(value.reshape(value.shape[0] // 8, 8, value.shape[1]), axis=0)


def backward_kernel(
    width, part_ref, halo_ref, ngrad_ref, gated_ref, par_ref, cols_ref, arow_ref, row_ref,
    b_ref, c_ref, bt_ref, ct_ref, sin_ref, din_ref,
    dpart_ref, tail_ref, head_ref, sums_ref, dcols_ref, dbc_ref,
    xext, uval, scores, dscores, states, dstate, duext, skip_sum, dbacc, dcacc,
):
    heads = width // HEAD_DIM
    rows = part_ref.shape[1]
    blocks = rows // BLOCK
    step = pl.program_id(0)

    @pl.when(step == 0)
    def _():
        dscores[...] = jnp.zeros_like(dscores)
        dbacc[...] = jnp.zeros_like(dbacc)
        dcacc[...] = jnp.zeros_like(dcacc)
        for block in range(blocks):
            at = pl.ds(block * BLOCK, BLOCK)
            scores[block] = exact_dot(c_ref[at], b_ref[at], NT)

    load_signal(part_ref, halo_ref, xext, width)
    taps = par_ref[0, :, width:]
    skip = par_ref[0, 6:7, width:]
    for block in range(blocks):
        uval[pl.ds(block * BLOCK, BLOCK)] = filtered(xext, taps, block * BLOCK)
    states[0] = sin_ref[0]
    dstate[...] = din_ref[0]
    skip_sum[...] = jnp.zeros_like(skip_sum)

    def state_body(block, carry):
        at = block_rows(block)
        cols = cols_ref[0, at, :]
        u = uval[at]
        weight = expand(cols, W_COL, heads)
        last = expand(cols[BLOCK - 8 :], EA_COL, heads)[7:8]
        states[block + 1] = last * states[block] + dot(
            bt_ref[block], (weight * (u * sigmoid(u))).astype(bf16)
        )
        return carry

    lax.fori_loop(0, blocks, state_body, 0)

    def body(count, carry):
        block = blocks - 1 - count
        at = block_rows(block)
        causal = causal_mask()
        cols = cols_ref[0, at, :]
        part = part_ref[0, at, :]
        grad, silu_z, slope_z = gate_grads(
            part, ngrad_ref[0, at, :], gated_ref[0, at, :], par_ref[0], row_ref[at], width
        )
        u = uval[at]
        su = sigmoid(u)
        x = u * su
        xl = x.astype(bf16)
        dy = grad * silu_z
        dyl = dy.astype(bf16)
        dyt = dy.T.astype(bf16)
        s = states[block].astype(bf16)
        d = dstate[...]
        dl = d.astype(bf16)
        ea = expand(cols, EA_COL, heads)
        weight = expand(cols, W_COL, heads)
        b = b_ref[at].astype(bf16)
        c = c_ref[at].astype(bf16)
        g = scores[block]
        y = ea * dot(c, s)
        dg = dscores[block]
        terms = product_terms(dy, x)
        dxt = []
        for head in range(heads):
            decay = decay_of(cols, arow_ref, block, head, heads, causal)
            m = (g * decay).astype(bf16)
            keep = head_mask(width, head)
            y = y + dot(m, xl * keep)
            dm = dot(terms[head][0], terms[head][1], NT)
            dg = dg + dm * decay
            dxt.append(dot(dyt[HEAD_DIM * head : HEAD_DIM * (head + 1)], m))
        dscores[block] = dg
        dx = jnp.concatenate(dxt, axis=0).T + weight * dot(b, dl)
        xf = xl.astype(f32)
        zz = xf * dx
        da = dyl.astype(f32) * y - zz
        ends = jnp.sum(states[block + 1] * d, axis=0, keepdims=True)
        is_last = lax.broadcasted_iota(jnp.int32, (BLOCK, 1), 0) == BLOCK - 1
        da = da + jnp.where(is_last, ends, 0.0)
        columns = head_sums(da, heads) + head_sums(zz, heads)
        lanes = lax.broadcasted_iota(jnp.int32, (BLOCK, 2 * heads), 1)
        packed = jnp.broadcast_to(columns[0], (BLOCK, 2 * heads))
        for at_lane in range(1, 2 * heads):
            packed = jnp.where(lanes == at_lane, columns[at_lane], packed)
        dcols_ref[0, at, :] = packed
        edy = (ea * dy).astype(bf16)
        dcacc[at] += dot(edy, s, NT)
        dbacc[at] += dot((weight * x).astype(bf16), dl, NT)
        dstate[...] = ea[BLOCK - 1 :] * d + dot(ct_ref[block], edy)
        du = (dx + skip * dy) * (su * (1.0 + u * (1.0 - su)))
        duext[at] = du
        skip_sum[...] += fold_rows(dy * x)
        dz = grad * (y + skip * x) * slope_z
        dpart_ref[0, at, :width] = dz.astype(bf16)
        return carry

    lax.fori_loop(0, blocks, body, 0)
    duext[rows : rows + 8] = jnp.zeros((8, width), f32)

    tap_sums = [jnp.zeros((8, width), f32) for _ in range(CONV + 1)]
    for block in range(blocks):
        base = block * BLOCK
        du = duext[base : base + BLOCK]
        dx = taps[CONV - 1 : CONV] * du
        tap_sums[CONV] = tap_sums[CONV] + fold_rows(du)
        for offset in range(CONV):
            begin = base + 8 - (CONV - 1) + offset
            tap_sums[offset] = tap_sums[offset] + fold_rows(du * xext[begin : begin + BLOCK])
            if offset < CONV - 1:
                ahead = base + CONV - 1 - offset
                dx = dx + taps[offset : offset + 1] * duext[ahead : ahead + BLOCK]
        dpart_ref[0, base : base + BLOCK, width:] = dx.astype(bf16)
        if block == blocks - 1:
            tail_ref[0, :, width:] = dx[BLOCK - 16 :]
    tail_ref[0, :, :width] = dpart_ref[0, rows - 16 : rows, :width].astype(f32)
    head_ref[0, :, :width] = jnp.zeros((8, width), f32)
    head_ref[0, :, width:] = duext[0:8]
    lines = tap_sums + [jnp.zeros((8, width), f32), skip_sum[...]]
    out_rows = [jnp.sum(line, axis=0, keepdims=True) for line in lines]
    sums_ref[0] = jnp.concatenate(out_rows + [jnp.zeros((1, width), f32)], axis=0)

    @pl.when(step == pl.num_programs(0) - 1)
    def _():
        for block in range(blocks):
            at = pl.ds(block * BLOCK, BLOCK)
            dg = dscores[block]
            dbc_ref[at, :STATE] = dbacc[at] + exact_dot(dg.T, c_ref[at])
            dbc_ref[at, STATE:] = dcacc[at] + exact_dot(dg, b_ref[at])


def run_kernels(rows, shards, width):
    heads = width // HEAD_DIM
    steps = shards
    blocks = rows // BLOCK
    chans = width

    def over(rows_here, lanes):
        return pl.BlockSpec((1, rows_here, lanes), lambda i: (i, 0, 0))

    def each(*dims):
        return pl.BlockSpec((1,) + dims, lambda i: (i,) + (0,) * len(dims))

    def whole(*dims):
        return pl.BlockSpec(dims, lambda i: (0,) * len(dims))

    part = over(rows, 2 * width)
    halo = over(8, 2 * width)
    par = over(8, 2 * width)
    chan = over(rows, width)
    cols = each(rows, KINDS * heads)
    arow = each(blocks, heads, BLOCK)
    state = over(STATE, width)
    bc = whole(rows, STATE)
    bct = whole(blocks, STATE, BLOCK)
    bct_flat = whole(STATE, rows)
    rowcols = whole(rows, 2)
    shape = jax.ShapeDtypeStruct
    params = pltpu.CompilerParams(
        dimension_semantics=("arbitrary",), vmem_limit_bytes=56 * 1024 * 1024
    )
    elements = rows * shards * chans

    def cost(per_element, reads):
        return pl.CostEstimate(
            flops=elements * per_element, bytes_accessed=elements * reads, transcendentals=0
        )

    local_state = pl.pallas_call(
        functools.partial(state_kernel, width),
        grid=(steps,),
        in_specs=[part, halo, par, cols, bct_flat],
        out_specs=state,
        out_shape=shape((shards, STATE, chans), f32),
        scratch_shapes=[pltpu.VMEM((rows + 8, width), f32), pltpu.VMEM((rows, width), bf16)],
        compiler_params=params,
        cost_estimate=cost(7000, 8),
        name="local_state",
    )
    forward = pl.pallas_call(
        functools.partial(forward_kernel, width),
        grid=(steps,),
        in_specs=[part, halo, par, cols, arow, bc, bc, bct, state],
        out_specs=[chan, whole(rows, 1)],
        out_shape=[shape((shards, rows, chans), bf16), shape((rows, 1), f32)],
        scratch_shapes=[
            pltpu.VMEM((rows + 8, width), f32),
            pltpu.VMEM((rows, width), f32),
            pltpu.VMEM((blocks, BLOCK, BLOCK), f32),
            pltpu.VMEM((STATE, width), f32),
            pltpu.VMEM((rows, 128), f32),
        ],
        compiler_params=params,
        cost_estimate=cost(17000, 10),
        name="forward_scan",
    )
    back_state = pl.pallas_call(
        functools.partial(back_state_kernel, width),
        grid=(steps,),
        in_specs=[part, chan, chan, par, cols, rowcols, bct_flat],
        out_specs=[state, over(8, width)],
        out_shape=[shape((shards, STATE, chans), f32), shape((shards, 8, chans), f32)],
        scratch_shapes=[pltpu.VMEM((rows, width), bf16)],
        compiler_params=params,
        cost_estimate=cost(8000, 14),
        name="back_state",
    )
    backward = pl.pallas_call(
        functools.partial(backward_kernel, width),
        grid=(steps,),
        in_specs=[
            part, halo, chan, chan, par, cols, arow, rowcols, bc, bc, bct, bct, state, state
        ],
        out_specs=[
            part, over(16, 2 * width), over(8, 2 * width), over(8, width),
            each(rows, 2 * heads), whole(rows, 2 * STATE),
        ],
        out_shape=[
            shape((shards, rows, 2 * chans), bf16),
            shape((shards, 16, 2 * chans), f32),
            shape((shards, 8, 2 * chans), f32),
            shape((shards, 8, chans), f32),
            shape((steps, rows, 2 * heads), f32),
            shape((rows, 2 * STATE), f32),
        ],
        scratch_shapes=[
            pltpu.VMEM((rows + 8, width), f32),
            pltpu.VMEM((rows, width), f32),
            pltpu.VMEM((blocks, BLOCK, BLOCK), f32),
            pltpu.VMEM((blocks, BLOCK, BLOCK), f32),
            pltpu.VMEM((blocks + 1, STATE, width), f32),
            pltpu.VMEM((STATE, width), f32),
            pltpu.VMEM((rows + 8, width), f32),
            pltpu.VMEM((8, width), f32),
            pltpu.VMEM((rows, STATE), f32),
            pltpu.VMEM((rows, STATE), f32),
        ],
        compiler_params=params,
        cost_estimate=cost(43000, 20),
        name="backward_scan",
    )
    return local_state, forward, back_state, backward


def after(value, *others):
    def body(*refs):
        del refs

    anywhere = pl.BlockSpec(memory_space=pl.ANY)
    return pl.pallas_call(
        body,
        in_specs=[anywhere] * (1 + len(others)),
        out_specs=anywhere,
        out_shape=jax.ShapeDtypeStruct(value.shape, value.dtype),
        input_output_aliases={0: 0},
        name="after",
    )(value, *others)


def dp_sum(array):
    size = lax.axis_size("dp")
    total = array
    for k in range(1, size):
        total = total + lax.ppermute(array, "dp", [(i, (i + k) % size) for i in range(size)])
    return total


def dp_gather(array, *meanwhile):
    size = lax.axis_size("dp")
    me = lax.axis_index("dp")
    rows = array.shape[0]
    full = jnp.zeros((size * rows,) + array.shape[1:], array.dtype)
    full = lax.dynamic_update_slice(full, array, (me * rows, 0))
    for k in range(1, size):
        got = lax.ppermute(array, "dp", [(i, (i + k) % size) for i in range(size)])
        if meanwhile:
            got = after(got, *meanwhile)
        full = lax.dynamic_update_slice(full, got, (lax.rem(me - k + size, size) * rows, 0))
    return full


def dp_scatter(array, *meanwhile):
    size = lax.axis_size("dp")
    me = lax.axis_index("dp")
    part = array.shape[-1] // size
    total = lax.dynamic_slice_in_dim(array, me * part, part, array.ndim - 1).astype(f32)
    for k in range(1, size):
        there = lax.rem(me + k, size)
        piece = lax.dynamic_slice_in_dim(array, there * part, part, array.ndim - 1)
        got = lax.ppermute(piece, "dp", [(i, (i + k) % size) for i in range(size)])
        if meanwhile:
            got = after(got, *meanwhile)
        total = total + got.astype(f32)
    return total


def carried_states(own, totals, reverse):
    devices = lax.axis_size("mp")
    me = lax.axis_index("mp")
    shards, _, chans = own.shape

    def over_channels(logs):
        per_chan = jnp.repeat(logs.reshape(shards, 1, -1), HEAD_DIM, axis=-1)
        return jnp.exp(per_chan)

    result = jnp.zeros_like(own)
    result_log = jnp.zeros_like(totals[0])
    group_logs = totals
    span = 1
    while span < devices:
        got = lax.ppermute(own.astype(bf16), "mp", [(i, i ^ span) for i in range(devices)])
        got = got.astype(f32)
        high = lax.rem(me // span, 2) == 1
        nearer = jnp.logical_not(high) if reverse else high
        mine_log = lax.dynamic_index_in_dim(group_logs, me // span, 0, keepdims=False)
        theirs = lax.bitwise_xor(me // span, 1)
        their_log = lax.dynamic_index_in_dim(group_logs, theirs, 0, keepdims=False)
        result = result + jnp.where(nearer, over_channels(result_log), 0.0) * got
        result_log = result_log + jnp.where(nearer, their_log, 0.0)
        if 2 * span < devices:
            own = jnp.where(nearer, 1.0, over_channels(their_log)) * own
            own = own + jnp.where(nearer, over_channels(mine_log), 1.0) * got
        group_logs = group_logs.reshape(-1, 2, totals.shape[1]).sum(axis=1)
        span *= 2
    return result


def causal_filter(extended, taps, rows):
    result = taps[CONV]
    for offset in range(CONV):
        begin = 8 - (CONV - 1) + offset
        result = result + taps[offset] * extended[begin : begin + rows]
    return result


def adam_rows(weight_now, gradient, moments, decayed):
    first_moment = beta_one * moments[0] + (1.0 - beta_one) * gradient
    second_moment = beta_two * moments[1] + (1.0 - beta_two) * gradient * gradient
    direction = (
        first_moment
        / (1.0 - beta_one**STEP)
        / (jnp.sqrt(second_moment / (1.0 - beta_two**STEP)) + adam_eps)
    )
    if decayed:
        direction = direction + decay_rate * weight_now
    return jnp.stack([first_moment, second_moment, direction])


def local(
    tokens,
    cotangent,
    lengths,
    inner_weight,
    step_weight,
    state_weight,
    output_weight,
    inner_filter,
    state_filter,
    head_params,
    norm_gain,
    inner_moments,
    step_moments,
    state_moments,
    output_moments,
    inner_filter_moments,
    state_filter_moments,
    head_moments,
    gain_moments,
):
    shards = lax.axis_size("mp")
    mine = lax.axis_index("mp")
    rows, model = tokens.shape
    own_model, heads_here, _ = inner_weight.shape
    chans = heads_here * HEAD_DIM
    width = min(256, chans)
    step_heads = width // HEAD_DIM
    groups = chans // width
    heads = shards * heads_here
    blocks = rows // BLOCK
    onward = [(i, i + 1) for i in range(shards - 1)]
    homeward = [(i + 1, i) for i in range(shards - 1)]
    local_state, forward, back_state, backward = run_kernels(rows, shards, width)

    inner_groups = inner_weight.reshape(own_model, groups, step_heads, 2, HEAD_DIM)
    inner_groups = inner_groups.astype(bf16).transpose(1, 0, 3, 2, 4)
    inner_groups = inner_groups.reshape(groups, own_model, 2 * width)
    out_groups = output_weight.astype(bf16).reshape(own_model, groups, width)

    packed = jnp.concatenate(
        [
            inner_filter,
            norm_gain[None],
            jnp.repeat(head_params[2], HEAD_DIM)[None],
            jnp.pad(head_params[:2].reshape(1, -1), ((0, 0), (0, chans - 2 * heads_here))),
        ],
        axis=0,
    )
    own_lines = packed.shape[0]
    packed = jnp.concatenate([packed, step_weight.reshape(-1, chans)], axis=0)
    packed = lax.all_gather(packed, "mp", axis=0)
    head_rows = packed[:, 7, : 2 * heads_here].reshape(shards, 2, heads_here)
    step_bias = head_rows[:, 0].reshape(heads)
    decay_base = jnp.exp(head_rows[:, 1].reshape(heads))
    step_all = packed[:, own_lines:].reshape(shards, own_model, heads_here)
    step_all = step_all.astype(bf16).transpose(1, 0, 2).reshape(own_model, heads)
    packed = packed[:, :own_lines]
    params = []
    for group in range(groups):
        here = packed[:, :, group * width : (group + 1) * width]
        params.append(jnp.concatenate([jnp.zeros_like(here), here], axis=-1))

    small_own = jnp.concatenate([step_all, state_weight.astype(bf16)], axis=1)
    inner_low = [dp_gather(inner_groups[0])]
    small = dp_gather(after(small_own, inner_low[0]))

    raw_small = jnp.dot(tokens, small, preferred_element_type=f32)
    state_raw = raw_small[:, heads:]
    state_halo = lax.ppermute(state_raw[rows - 8 :], "mp", onward)
    state_ext = jnp.concatenate([state_halo, state_raw], axis=0)
    state_u = causal_filter(state_ext, state_filter, rows)
    state_sig = jax.nn.sigmoid(state_u)
    state_signal = state_u * state_sig
    writer = state_signal[:, :STATE]
    reader = state_signal[:, STATE:]
    writer_t = writer.T.astype(bf16)
    reader_t = reader.T.astype(bf16)
    writer_blocks = writer_t.reshape(STATE, blocks, BLOCK).transpose(1, 0, 2)
    reader_blocks = reader_t.reshape(STATE, blocks, BLOCK).transpose(1, 0, 2)
    step_arg = raw_small[:, :heads] + step_bias
    step_sizes = jax.nn.softplus(step_arg)
    log_decay = -step_sizes * decay_base
    lower = (jnp.arange(BLOCK)[:, None] >= jnp.arange(BLOCK)[None, :]).astype(f32)
    cumulative = jnp.einsum(
        "ts,bsh->bth", lower, log_decay.reshape(blocks, BLOCK, heads), precision=highest
    )
    block_total = cumulative[:, -1]
    running = jnp.cumsum(block_total, axis=0)
    before = running - block_total
    device_total = running[-1]
    dt_blocks = step_sizes.reshape(blocks, BLOCK, heads)
    from_start = cumulative + before[:, None]
    kinds = [
        cumulative,
        jnp.exp(cumulative),
        jnp.exp(block_total[:, None] - cumulative) * dt_blocks,
        jnp.exp(device_total - from_start) * dt_blocks,
        jnp.exp(from_start),
    ]
    by_group = (shards, groups, step_heads)
    columns = jnp.stack(kinds).reshape((KINDS, rows) + by_group)
    columns = [
        columns[:, :, :, group].transpose(2, 1, 0, 3).reshape(shards, rows, KINDS * step_heads)
        for group in range(groups)
    ]
    arows = (cumulative - jnp.log(dt_blocks)).reshape((blocks, BLOCK) + by_group)
    arows = arows.transpose(3, 2, 0, 4, 1)

    totals_all = lax.all_gather(device_total, "mp", axis=0)
    totals_groups = totals_all.reshape((shards,) + by_group).transpose(2, 0, 1, 3)
    totals_groups = totals_groups.reshape(groups, shards, shards * step_heads)

    for group in range(1, groups):
        inner_low.append(dp_gather(after(inner_groups[group], small), columns[0], totals_all))
    inner_full = [lax.all_gather(own, "mp", axis=0) for own in inner_low]
    parts, halos, states_in, gained = [], [], [], []
    squares = 0.0
    ready = [columns[0]]
    for group in range(groups):
        inner_full[group] = after(inner_full[group], *ready)
        part = jnp.einsum(
            "td,mdc->mtc", tokens, inner_full[group], preferred_element_type=f32
        )
        halo = lax.ppermute(part[:, rows - 8 :], "mp", onward)
        if group == 0:
            out_low = [
                dp_gather(after(out_groups[:, g], inner_low[-1]), halo) for g in range(groups)
            ]
            out_full = [lax.all_gather(own, "mp", axis=0) for own in out_low]
            halo = after(halo, *out_low)
        ends = local_state(part, halo, params[group], columns[group], writer_t)
        state_in = carried_states(ends, totals_groups[group], False)
        out, sq = forward(
            part, halo, params[group], columns[group], arows[group], writer, reader,
            writer_blocks, state_in,
        )
        squares = squares + sq
        ready = [out]
        parts.append(part)
        halos.append(halo)
        states_in.append(state_in)
        gained.append(out)
    norm_scale = lax.rsqrt(squares / INNER + eps_norm)
    branch = norm_scale * sum(
        jnp.einsum("mtc,mdc->td", gained[group], out_full[group], preferred_element_type=f32)
        for group in range(groups)
    )
    positions = mine * rows + jnp.arange(rows)
    live = (positions < lengths[0]).astype(f32)[:, None]
    mixed = (tokens.astype(f32) + live * branch).astype(bf16)

    masked = (cotangent.astype(f32) * live).astype(bf16)
    scaled_sum = jnp.sum(masked.astype(f32) * branch, axis=1, keepdims=True)
    row_columns = jnp.concatenate(
        [norm_scale, norm_scale * norm_scale * scaled_sum / INNER], axis=1
    )
    scaled_cot = after((masked.astype(f32) * norm_scale).astype(bf16), row_columns)
    out_parts = [
        jnp.einsum(
            "td,mtc->mcd", scaled_cot, gained[group], preferred_element_type=f32
        ).astype(bf16)
        for group in range(groups)
    ]
    out_sums = [lax.psum_scatter(part, "mp", scatter_dimension=0) for part in out_parts]
    ngrads, starts, gain_sums = [], [], []
    for group in range(groups):
        normed_grad = jnp.einsum(
            "td,mdc->mtc", masked, out_full[group], preferred_element_type=f32
        )
        start, gain_sum = back_state(
            parts[group], normed_grad, gained[group], params[group], columns[group],
            row_columns, reader_t,
        )
        ngrads.append(normed_grad)
        starts.append(start)
        gain_sums.append(gain_sum)
    dstates = [carried_states(starts[g], totals_groups[g], True) for g in range(groups)]
    waiting = out_parts + starts[1:]
    dparts, inner_sums, dbc, all_sums, all_dcols = [], [], 0.0, [], []
    for group in range(groups):
        last = group == groups - 1
        dpart, tail, du_head, sums, dcols, dbc_here = backward(
            parts[group], halos[group], ngrads[group], gained[group], params[group],
            columns[group], arows[group], row_columns, writer, reader, writer_blocks,
            reader_blocks, states_in[group], after(dstates[group], *waiting),
        )
        du_next = lax.ppermute(du_head, "mp", homeward)
        extra = [
            sum(params[group][:, k] * du_next[:, i - k] for k in range(i + 1))
            for i in range(CONV - 1)
        ]
        extra = jnp.concatenate(
            [jnp.zeros((shards, 13, 2 * width), f32), jnp.stack(extra, axis=1)], axis=1
        )
        dpart = lax.dynamic_update_slice(
            dpart, (tail + extra).astype(bf16), (0, rows - 16, 0)
        )
        if last:
            dpart = after(dpart, *inner_sums)
        inner_part = jnp.einsum("td,mtc->mcd", tokens, dpart, preferred_element_type=f32)
        inner_part = inner_part.astype(bf16)
        inner_sums.append(lax.psum_scatter(inner_part, "mp", scatter_dimension=0))
        waiting = [inner_part] + (out_sums if group == groups - 2 else [])
        dparts.append(dpart)
        dbc = dbc + dbc_here
        all_sums.append(sums)
        all_dcols.append(dcols)
    dbc = after(dbc, inner_part)
    all_dcols[-1] = after(all_dcols[-1], inner_part)

    dcols = jnp.stack(all_dcols).reshape(groups, shards, rows, 2, step_heads)
    dcols = dcols.transpose(3, 2, 1, 0, 4).reshape(2, rows, heads)
    dlog = jnp.einsum(
        "st,bsh->bth", lower, dcols[0].reshape(blocks, BLOCK, heads), precision=highest
    ).reshape(rows, heads)
    slope = jax.nn.sigmoid(step_arg)
    ratio = jnp.where(step_sizes > 1e-20, slope / jnp.maximum(step_sizes, 1e-20), 1.0)
    dstep = dcols[1] * ratio - dlog * decay_base * slope
    sums = jnp.concatenate(all_sums, axis=-1)
    gains = jnp.concatenate(gain_sums, axis=-1)
    head_line = jnp.concatenate(
        [
            jnp.sum(dstep, axis=0).reshape(shards, heads_here),
            jnp.sum(dlog * log_decay, axis=0).reshape(shards, heads_here),
            jnp.sum(sums[:, 6].reshape(shards, heads_here, HEAD_DIM), axis=-1),
        ],
        axis=1,
    )
    head_line = jnp.pad(head_line, ((0, 0), (0, chans - 3 * heads_here)))[:, None]
    du_state = dbc * (state_sig * (1.0 + state_u * (1.0 - state_sig)))
    du_state_next = lax.ppermute(du_state[:8], "mp", homeward)
    du_state_ext = jnp.concatenate([du_state, du_state_next], axis=0)
    dstate_raw = sum(
        state_filter[k] * du_state_ext[CONV - 1 - k : CONV - 1 - k + rows] for k in range(CONV)
    )
    state_filter_part = jnp.stack(
        [jnp.sum(du_state * state_ext[5 + k : 5 + k + rows], axis=0) for k in range(CONV)]
        + [jnp.sum(du_state, axis=0)]
    )
    dsmall = jnp.concatenate([dstep, dstate_raw], axis=1).astype(bf16)

    small_grad = lax.dot_general(
        dsmall, tokens, (((0,), (0,)), ((), ())), preferred_element_type=f32
    )
    state_share = 2 * STATE // shards
    lines = -(-(CONV + 1) * 2 * STATE // chans)
    filter_lines = jnp.pad(
        state_filter_part.reshape(-1), (0, lines * chans - (CONV + 1) * 2 * STATE)
    )
    filter_lines = jnp.broadcast_to(filter_lines.reshape(1, lines, chans), (shards, lines, chans))
    sums_here = jnp.concatenate(
        [sums[:, : CONV + 1], jnp.sum(gains, axis=1, keepdims=True), head_line, filter_lines],
        axis=1,
    ).reshape(shards, -1)
    sum_rows = -(-sums_here.shape[1] // model)
    sum_size = sums_here.shape[1]
    sums_here = jnp.pad(sums_here, ((0, 0), (0, sum_rows * model - sum_size)))
    small_grad = jnp.concatenate(
        [
            small_grad[:heads].reshape(shards, heads_here, model),
            small_grad[heads:].reshape(shards, state_share, model),
            sums_here.reshape(shards, sum_rows, model),
        ],
        axis=1,
    )
    small_rows = heads_here + state_share
    small_total = lax.psum_scatter(after(small_grad, inner_sums[-1]), "mp", scatter_dimension=0)

    input_part = 0.0
    for group in range(groups):
        input_part = input_part + jnp.einsum(
            "mtc,mdc->td", after(dparts[group], small_grad), inner_full[group], preferred_element_type=f32,
        )
    small_part = lax.dot_general(dsmall, small, (NT, ((), ())), preferred_element_type=f32)
    tokens_gradient = (cotangent.astype(f32) + input_part + small_part).astype(bf16)

    early = [after(total, inner_part) for total in out_sums + inner_sums[:-1]]
    early = [dp_scatter(total, tokens_gradient) for total in early]
    out_grads, inner_grads = early[:groups], early[groups:]
    inner_grads.append(dp_scatter(inner_sums[-1]))
    small_sum = dp_scatter(small_total[:small_rows])
    own = dp_sum(small_total[small_rows:]).reshape(-1)[:sum_size].reshape(-1, chans)
    step_gradient = small_sum[:heads_here].T
    state_gradient = lax.all_gather(small_sum[heads_here:], "mp", axis=0, tiled=True).T
    output_gradient = jnp.concatenate(out_grads, axis=0).T
    inner_gradient = jnp.stack(inner_grads)
    inner_gradient = inner_gradient.reshape(groups, 2, step_heads, HEAD_DIM, own_model)
    inner_gradient = inner_gradient.transpose(4, 0, 2, 1, 3)
    inner_gradient = inner_gradient.reshape(own_model, heads_here, 2 * HEAD_DIM)
    state_filter_gradient = own[CONV + 3 :].reshape(-1)[: (CONV + 1) * 2 * STATE]
    state_filter_gradient = state_filter_gradient.reshape(CONV + 1, 2 * STATE)
    inner_filter_gradient = own[: CONV + 1]
    gain_gradient = own[CONV + 1]
    head_gradient = own[CONV + 2, : 3 * heads_here].reshape(3, heads_here)

    inner_update = adam_rows(inner_weight, inner_gradient, inner_moments, True)
    step_update = adam_rows(step_weight, step_gradient, step_moments, True)
    state_update = adam_rows(state_weight, state_gradient, state_moments, True)
    output_update = adam_rows(output_weight, output_gradient, output_moments, True)
    inner_filter_update = adam_rows(inner_filter, inner_filter_gradient, inner_filter_moments, True)
    state_filter_update = adam_rows(state_filter, state_filter_gradient, state_filter_moments, True)
    head_update = adam_rows(head_params, head_gradient, head_moments, False)
    gain_update = adam_rows(norm_gain, gain_gradient, gain_moments, False)
    return (
        mixed,
        tokens_gradient,
        inner_gradient,
        step_gradient,
        state_gradient,
        output_gradient,
        inner_filter_gradient,
        state_filter_gradient,
        head_gradient,
        gain_gradient,
        inner_update,
        step_update,
        state_update,
        output_update,
        inner_filter_update,
        state_filter_update,
        head_update,
        gain_update,
    )


def solution(mesh):
    return jax.shard_map(
        local,
        mesh=mesh,
        in_specs=(
            P(("dp", "mp"), None),
            P(("dp", "mp"), None),
            P("dp"),
            P("dp", "mp", None),
            P("dp", "mp"),
            P("dp", None),
            P("dp", "mp"),
            P(None, "mp"),
            P(),
            P(None, "mp"),
            P("mp"),
            P(None, "dp", "mp", None),
            P(None, "dp", "mp"),
            P(None, "dp", None),
            P(None, "dp", "mp"),
            P(None, None, "mp"),
            P(),
            P(None, None, "mp"),
            P(None, "mp"),
        ),
        out_specs=(
            P(("dp", "mp"), None),
            P(("dp", "mp"), None),
            P("dp", "mp", None),
            P("dp", "mp"),
            P("dp", None),
            P("dp", "mp"),
            P(None, "mp"),
            P(),
            P(None, "mp"),
            P("mp"),
            P(None, "dp", "mp", None),
            P(None, "dp", "mp"),
            P(None, "dp", None),
            P(None, "dp", "mp"),
            P(None, None, "mp"),
            P(),
            P(None, None, "mp"),
            P(None, "mp"),
        ),
        check_vma=False,
    )
```

time: 4240 us -> 1210 us (0.29)
  local copies, waits for them, and re-layouts: 1360 us -> 152 us
  waiting for transfers between devices: 1100 us -> 246 us
  matrix products: 892 us -> 250 us
  other arithmetic: 582 us -> 69.4 us
  Pallas kernels: 0 us -> 340 us
  blocking collectives: 251 us -> 28.4 us
  starting transfers between devices: 0.45 us -> 96.1 us
    reduce_scatter x6 -> x5, waiting for transfers between devices: 865 us -> 0.03 us  [the longest x1 0.02 us: local(): lax.psum_scatter(after(small_grad, inner_sums[-1]), 'mp', scatter_dimensi...]
    dynamic_update_slice x128 -> x20, local copies, waits for them, and re-layouts: 855 us -> 17.9 us  [the longest x15 15 us: dp_gather(): lax.dynamic_update_slice(full, got, (lax.rem(me - k + size, size) * rows,...]
    dot_general x392 -> x17, matrix products: 826 us -> 250 us  [the longest x2 49 us: local(): jnp.einsum('td,mtc->mcd', tokens, dpart, preferred_element_type=f32)]
    pallas_call x0 -> x45, Pallas kernels: none -> 340 us  [the longest x2 198 us: local(): backward(parts[group], halos[group], ngrads[group], gained[group], params...]
    ppermute x0 -> x51, waiting for transfers between devices: none -> 246 us  [the longest x12 102 us: carried_states(): lax.ppermute(own.astype(bf16), 'mp', [(i, i ^ span) for i in range(device...]
    psum x4 -> x0, blocking collectives: 236 us -> none  [the longest x1 169 us: local(): lax.psum((state_partial, state_filter_partial), 'mp')]
    all_gather x5 -> x4, waiting for transfers between devices: 233 us -> 0.04 us  [the longest x2 0.02 us: local(): inner_full = [lax.all_gather(own, 'mp', axis=0) for own in inner_low]]
    reduce_sum x69 -> x6, other arithmetic: 158 us -> 5.9 us  [the longest x1 3.4 us: local(): jnp.sum(du_state, axis=0)]
  transfers between devices with their start and end apart: 11 -> 60, of which waited for: 6 -> 24; matrix products, arithmetic and copies ran while one was open for 29% -> 32% of each run, Pallas kernels for 0% -> 28%
where the time goes in v1:
time: 1210 us; the launch traced here: 1200 us
  Pallas kernels  340 us (28%)
  matrix products  250 us (21%)
  waiting for transfers between devices  246 us (20%)
  local copies, waits for them, and re-layouts  152 us (13%)
  starting transfers between devices  96.1 us (8%)
  other arithmetic  69.4 us (6%)
  blocking collectives  28.4 us (2%)
  between operations  17 us (1%)
    pallas_call x2, Pallas kernels, local(): backward(parts[group], halos[group], ngrads[group], gained[group], params...  198 us
    ppermute x12, waiting for transfers between devices, carried_states(): lax.ppermute(own.astype(bf16), 'mp', [(i, i ^ span) for i in range(device...  102 us
    pallas_call x2, Pallas kernels, local(): forward(part, halo, params[group], columns[group], arows[group], writer,...  75.5 us
    ppermute x15, waiting for transfers between devices, dp_gather(): got = lax.ppermute(array, 'dp', [(i, (i + k) % size) for i in range(size)])  72.6 us
    ppermute x15, waiting for transfers between devices, dp_scatter(): got = lax.ppermute(piece, 'dp', [(i, (i + k) % size) for i in range(size)])  67 us
    unnamed x259, local copies, waits for them, and re-layouts  61.9 us
    ppermute x15, starting transfers between devices, dp_gather(): got = lax.ppermute(array, 'dp', [(i, (i + k) % size) for i in range(size)])  50.7 us
    dot_general x2, matrix products, local(): jnp.einsum('td,mtc->mcd', tokens, dpart, preferred_element_type=f32)  49 us
  transfers between devices with their start and end apart: 60, of which 24 were waited for; matrix products, arithmetic and copies ran while one was open for 32% of the time, Pallas kernels for 28%

profile of v1, /device:TPU:0, one launch (start us, length us, event | category | flops | bytes accessed | tf_op | source)
XLA Modules:
  0.0 1199.3 jit_solution(1421703699898362757)
XLA Ops:
  19.9 8.8 collective-permute-done
  30.6 19.8 %collective-permute-done.1 = bf16[512,512]{1,0:T(8,128)(2,1)} collective-permute-done((bf16[512,512]{1,0:T(8,128)(2,1)S(1)}, bf16[512,512]{1,0:T(8,128)(2,1)}, u32[]{:S(2)}, u32[]{:S(2)}) %collective-permute-start.1) | collective-permute-done | bytes 524320 | tf_op jit(solution)/shard_map/ppermute | solution.py:520
  54.8 9.3 all-gather.1
  66.8 9.8 collective-permute-start.3
  82.6 7.2 collective-permute-done.3
  89.9 16.4 %collective-permute-done.4 = bf16[512,320]{1,0:T(8,128)(2,1)S(1)} collective-permute-done((bf16[512,320]{1,0:T(8,128)(2,1)}, bf16[512,320]{1,0:T(8,128)(2,1)S(1)}, u32[]{:S(2)}, u32[]{:S(2)}) %collective-permute-start.4) | collective-permute-done | bytes 327712 | tf_op jit(solution)/shard_map/ppermute | solution.py:520
  107.6 8.8 collective-permute-start.7
  118.8 5.2 convolution_bitcast_fusion.2
  135.8 9.7 all-gather.5
  145.7 4.4 collective-permute-done.8.refs_0_
  158.1 11.4 collective-permute-start.10
  172.9 23.4 %convolution_bitcast_fusion.1.part_ref = f32[8,1024,512]{2,1,0:T(8,128)S(1)} fusion(bf16[8,2048,512]{2,1,0:T(8,128)(2,1)} %after.38, bf16[1024,2048]{1,0:T(8,128)(2,1)} %param.19), kind=kOutput, calls=%fused_computation.7 | convolution fusion | flops 17179869184 | bytes 37748736 | tf_op jit(solution)/shard_map/td,mdc->mtc/dot_general | solution.py:715
  197.9 4.2 copy-done.107
  228.0 12.3 %collective-permute-done.14.refs_0_ = bf16[512,256]{1,0:T(8,128)(2,1)} collective-permute-done((bf16[512,256]{1,0:T(8,128)(2,1)}, bf16[512,256]{1,0:T(8,128)(2,1)}, u32[]{:S(2)}, u32[]{:S(2)}) %collective-permute-start.14) | collective-permute-done | bytes 262176 | tf_op jit(solution)/shard_map/ppermute | solution.py:520
  244.2 15.1 %local_state.2 = f32[8,128,256]{2,1,0:T(8,128)} custom-call(f32[8,1024,512]{2,1,0:T(8,128)} %copy-done.107, f32[8,8,512]{2,1,0:T(8,128)} %after.51.halo_ref, f32[8,8,512]{2,1,0:T(8,128)} %concatenate.54.par_ref, f32[8,1024,20]{2,1,0:T(8,128)} %copy.346.refs_1_.cols_ref, bf16[128,1024]{1,0:T(8,128)(2,1)} %copy.362.bt_ref), custom_call_target="tpu_custom_call" | custom-call | flops 14680064000 | bytes 16777216 | tf_op jit(solution)/shard_map/local_state/pallas_call | solution.py:725
  274.9 18.8 %collective-permute-done.18 = bf16[8,128,256]{2,1,0:T(8,128)(2,1)S(1)} collective-permute-done((bf16[8,128,256]{2,1,0:T(8,128)(2,1)}, bf16[8,128,256]{2,1,0:T(8,128)(2,1)S(1)}, u32[]{:S(2)}, u32[]{:S(2)}) %collective-permute-start.18) | collective-permute-done | bytes 524320 | tf_op jit(solution)/shard_map/ppermute | solution.py:556
  300.6 20.1 %collective-permute-done.19 = bf16[8,128,256]{2,1,0:T(8,128)(2,1)S(1)} collective-permute-done((bf16[8,128,256]{2,1,0:T(8,128)(2,1)}, bf16[8,128,256]{2,1,0:T(8,128)(2,1)S(1)}, u32[]{:S(2)}, u32[]{:S(2)}) %collective-permute-start.19) | collective-permute-done | bytes 524320 | tf_op jit(solution)/shard_map/ppermute | solution.py:556
  321.9 37.8 %forward_scan.2 = (bf16[8,1024,256]{2,1,0:T(8,128)(2,1)}, f32[1024,1]{1,0:T(8,128)}) custom-call(f32[8,1024,512]{2,1,0:T(8,128)} %copy-done.107, f32[8,8,512]{2,1,0:T(8,128)} %after.51.halo_ref, f32[8,8,512]{2,1,0:T(8,128)} %concatenate.54.par_ref, f32[8,1024,20]{2,1,0:T(8,128)} %copy.346.refs_1_.cols_ref, f32[8,4,4,256]{3,2,1,0:T(4,128)} %get-tuple-element.240.arow_ref, ...), custom_call_target="tpu_custom_call" | custom-call | flops 35651584000 | bytes 20971520 | tf_op jit(solution)/shard_map/forward_scan/pallas_call | solution.py:727
  359.7 23.0 %convolution_bitcast_fusion.part_ref = f32[8,1024,512]{2,1,0:T(8,128)S(1)} fusion(bf16[8,2048,512]{2,1,0:T(8,128)(2,1)} %after.52, bf16[1024,2048]{1,0:T(8,128)(2,1)} %param.19), kind=kOutput, calls=%fused_computation.6 | convolution fusion | flops 17179869184 | bytes 37748736 | tf_op jit(solution)/shard_map/td,mdc->mtc/dot_general | solution.py:715
  392.0 14.9 %local_state.3 = f32[8,128,256]{2,1,0:T(8,128)} custom-call(f32[8,1024,512]{2,1,0:T(8,128)} %copy-done.108, f32[8,8,512]{2,1,0:T(8,128)} %copy-done.112, f32[8,8,512]{2,1,0:T(8,128)} %concatenate.56.par_ref, f32[8,1024,20]{2,1,0:T(8,128)} %copy.376.cols_ref, bf16[128,1024]{1,0:T(8,128)(2,1)} %copy.362.bt_ref), custom_call_target="tpu_custom_call" | custom-call | flops 14680064000 | bytes 16777216 | tf_op jit(solution)/shard_map/local_state/pallas_call | solution.py:725
  412.6 13.0 %collective-permute-done.22 = bf16[8,128,256]{2,1,0:T(8,128)(2,1)S(1)} collective-permute-done((bf16[8,128,256]{2,1,0:T(8,128)(2,1)S(1)}, bf16[8,128,256]{2,1,0:T(8,128)(2,1)S(1)}, u32[]{:S(2)}, u32[]{:S(2)}) %collective-permute-start.22) | collective-permute-done | bytes 524320 | tf_op jit(solution)/shard_map/ppermute | solution.py:556
  428.9 10.2 collective-permute-done.23
  440.4 37.7 %forward_scan.3 = (bf16[8,1024,256]{2,1,0:T(8,128)(2,1)}, f32[1024,1]{1,0:T(8,128)}) custom-call(f32[8,1024,512]{2,1,0:T(8,128)} %copy-done.108, f32[8,8,512]{2,1,0:T(8,128)} %copy-done.112, f32[8,8,512]{2,1,0:T(8,128)} %concatenate.56.par_ref, f32[8,1024,20]{2,1,0:T(8,128)} %copy.376.cols_ref, f32[8,4,4,256]{3,2,1,0:T(4,128)} %get-tuple-element.239.arow_ref, ...), custom_call_target="tpu_custom_call" | custom-call | flops 35651584000 | bytes 20971520 | tf_op jit(solution)/shard_map/forward_scan/pallas_call | solution.py:727
  479.4 14.5 %fusion.174 = f32[1024,2048,1]{1,0,2:T(8,128)} fusion(bf16[8,1024,256]{2,1,0:T(8,128)(2,1)} %get-tuple-element.39.refs_1_.gated_ref, bf16[8,2048,256]{2,1,0:T(8,128)(2,1)} %bitcast.428), kind=kOutput, calls=%fused_computation.394 | convolution fusion | flops 8589934592 | bytes 20971520 | tf_op jit(solution)/shard_map/mtc,mdc->td/dot_general | solution.py:739
  494.0 18.4 %fusion.3 = (f32[1024]{0:T(1024)S(1)}, bf16[1024,2048]{1,0:T(8,128)(2,1)}, bf16[1024,2048]{1,0:T(8,128)(2,1)}) fusion(f32[1024]{0:T(1024)S(1)} %fusion.108, bf16[1024,2048]{1,0:T(8,128)(2,1)} %param.20, bf16[1024,2048]{1,0:T(8,128)(2,1)} %param.19, f32[1024]{0:T(1024)S(1)} %get-tuple-element.184, bf16[8,1024,256]{2,1,0:T(8,128)(2,1)} %get-tuple-element.41.gated_ref, ...), kind=kOutput, calls=%fused_computation.11 | convolution fusion | flops 8619293696 | bytes 37761024 | tf_op jit(solution)/shard_map/mtc,mdc->td/dot_general | solution.py:739
  513.6 14.0 %convolution_convert_fusion.3.refs_1_ = bf16[8,256,2048]{2,1,0:T(8,128)(2,1)} fusion(bf16[8,1024,256]{2,1,0:T(8,128)(2,1)} %get-tuple-element.39.refs_1_.gated_ref, bf16[1024,2048]{1,0:T(8,128)(2,1)} %after.53), kind=kOutput, calls=%fused_computation.19 | convolution fusion | flops 8594128896 | bytes 16777216 | tf_op jit(solution)/shard_map/td,mtc->mcd/dot_general | solution.py:753
  531.5 15.8 %fusion.19.ngrad_ref = f32[8,1024,256]{2,1,0:T(8,128)} fusion(bf16[8,2048,256]{2,1,0:T(8,128)(2,1)} %bitcast.429, bf16[1024,2048]{1,0:T(8,128)(2,1)} %param.20, f32[1024]{0:T(1024)S(1)} %fusion.108), kind=kOutput, calls=%fused_computation.31 | convolution fusion | flops 8596226048 | bytes 20975616 | tf_op jit(solution)/shard_map/td,mdc->mtc/dot_general | solution.py:761
  547.3 18.4 %back_state.2 = (f32[8,128,256]{2,1,0:T(8,128)}, f32[8,8,256]{2,1,0:T(8,128)}) custom-call(f32[8,1024,512]{2,1,0:T(8,128)} %copy-done.107, f32[8,1024,256]{2,1,0:T(8,128)} %fusion.19.ngrad_ref, bf16[8,1024,256]{2,1,0:T(8,128)(2,1)} %get-tuple-element.39.refs_1_.gated_ref, f32[8,8,512]{2,1,0:T(8,128)} %concatenate.54.par_ref, ...), custom_call_target="tpu_custom_call" | custom-call | flops 16777216000 | bytes 29360128 | tf_op jit(solution)/shard_map/back_state/pallas_call | solution.py:764
  567.1 13.7 %fusion.16.ngrad_ref = f32[8,1024,256]{2,1,0:T(8,128)} fusion(bf16[8,2048,256]{2,1,0:T(8,128)(2,1)} %bitcast.431, bf16[1024,2048]{1,0:T(8,128)(2,1)S(1)} %copy-done.29, f32[1024]{0:T(1024)S(1)} %fusion.108), kind=kOutput, calls=%fused_computation.30 | convolution fusion | flops 8596226048 | bytes 20975616 | tf_op jit(solution)/shard_map/td,mdc->mtc/dot_general | solution.py:761
  581.1 11.6 convolution_convert_fusion.2.refs_2_
  592.7 11.4 collective-permute-done.25
  606.3 17.5 %back_state.3 = (f32[8,128,256]{2,1,0:T(8,128)}, f32[8,8,256]{2,1,0:T(8,128)}) custom-call(f32[8,1024,512]{2,1,0:T(8,128)} %copy-done.108, f32[8,1024,256]{2,1,0:T(8,128)} %fusion.16.ngrad_ref, bf16[8,1024,256]{2,1,0:T(8,128)(2,1)} %get-tuple-element.41.gated_ref, f32[8,8,512]{2,1,0:T(8,128)} %concatenate.56.par_ref, f32[8,1024,20]{2,1,0:T(8,128)} %copy.376.cols_ref, ...), custom_call_target="tpu_custom_call" | custom-call | flops 16777216000 | bytes 29360128 | tf_op jit(solution)/shard_map/back_state/pallas_call | solution.py:764
  625.2 99.1 %backward_scan.2 = (bf16[8,1024,512]{2,1,0:T(8,128)(2,1)}, f32[8,16,512]{2,1,0:T(8,128)}, f32[8,8,512]{2,1,0:T(8,128)}, f32[8,8,256]{2,1,0:T(8,128)}, f32[8,1024,8]{2,1,0:T(8,128)}, /*index=5*/f32[1024,256]{1,0:T(8,128)}) custom-call(f32[8,1024,512]{2,1,0:T(8,128)} %copy-done.107, f32[8,8,512]{2,1,0:T(8,128)} %after.51.halo_ref, ...), custom_call_target="tpu_custom_call" | custom-call | flops 90177536000 | bytes 41943040 | tf_op jit(solution)/shard_map/backward_scan/pallas_call | solution.py:776
  729.5 23.9 %convolution_convert_fusion.1.refs_1_ = bf16[8,512,2048]{2,1,0:T(8,128)(2,1)} fusion(bf16[8,1024,512]{2,1,0:T(8,128)(2,1)} %fusion.86.refs_0_, bf16[1024,2048]{1,0:T(8,128)(2,1)S(1)} %copy-done.110), kind=kOutput, calls=%fused_computation.1 | convolution fusion | flops 17188257792 | bytes 29360128 | tf_op jit(solution)/shard_map/td,mtc->mcd/dot_general | solution.py:794
  760.1 13.0 %collective-permute-done.29 = bf16[8,128,256]{2,1,0:T(8,128)(2,1)S(1)} collective-permute-done((bf16[8,128,256]{2,1,0:T(8,128)(2,1)S(1)}, bf16[8,128,256]{2,1,0:T(8,128)(2,1)S(1)}, u32[]{:S(2)}, u32[]{:S(2)}) %collective-permute-start.29) | collective-permute-done | bytes 524320 | tf_op jit(solution)/shard_map/ppermute | solution.py:556
  773.9 12.9 %collective-permute-done.30 = bf16[8,128,256]{2,1,0:T(8,128)(2,1)S(1)} collective-permute-done((bf16[8,128,256]{2,1,0:T(8,128)(2,1)S(1)}, bf16[8,128,256]{2,1,0:T(8,128)(2,1)S(1)}, u32[]{:S(2)}, u32[]{:S(2)}) %collective-permute-start.30) | collective-permute-done | bytes 524320 | tf_op jit(solution)/shard_map/ppermute | solution.py:556
  788.1 99.4 %backward_scan.3 = (bf16[8,1024,512]{2,1,0:T(8,128)(2,1)}, f32[8,16,512]{2,1,0:T(8,128)}, f32[8,8,512]{2,1,0:T(8,128)}, f32[8,8,256]{2,1,0:T(8,128)}, f32[8,1024,8]{2,1,0:T(8,128)}, /*index=5*/f32[1024,256]{1,0:T(8,128)}) custom-call(f32[8,1024,512]{2,1,0:T(8,128)} %copy-done.108, f32[8,8,512]{2,1,0:T(8,128)} %copy-done.112, ...), custom_call_target="tpu_custom_call" | custom-call | flops 90177536000 | bytes 41943040 | tf_op jit(solution)/shard_map/backward_scan/pallas_call | solution.py:776
  892.7 25.0 %convolution_convert_fusion.refs_1_ = bf16[8,512,2048]{2,1,0:T(8,128)(2,1)} fusion(bf16[8,1024,512]{2,1,0:T(8,128)(2,1)} %after.56.refs_0_, bf16[1024,2048]{1,0:T(8,128)(2,1)} %param.19), kind=kOutput, calls=%fused_computation | convolution fusion | flops 17188257792 | bytes 29360128 | tf_op jit(solution)/shard_map/td,mtc->mcd/dot_general | solution.py:794
  919.8 3.8 fusion.160
  988.9 25.0 %fusion.176 = f32[1024,2048,1]{1,0,2:T(8,128)} fusion(bf16[8,1024,512]{2,1,0:T(8,128)(2,1)} %after.60, bf16[8,2048,512]{2,1,0:T(8,128)(2,1)} %after.52), kind=kOutput, calls=%fused_computation.396 | convolution fusion | flops 17179869184 | bytes 33554432 | tf_op jit(solution)/shard_map/mtc,mdc->td/dot_general | solution.py:865
  1013.9 21.7 %fusion.175 = f32[1024,2048,1]{1,0,2:T(8,128)} fusion(bf16[8,1024,512]{2,1,0:T(8,128)(2,1)S(1)} %copy-done.17, bf16[8,2048,512]{2,1,0:T(8,128)(2,1)} %after.38), kind=kOutput, calls=%fused_computation.395 | convolution fusion | flops 17179869184 | bytes 33554432 | tf_op jit(solution)/shard_map/mtc,mdc->td/dot_general | solution.py:865
  1037.2 12.3 %fusion.2.refs_1_ = bf16[1024,2048]{1,0:T(8,128)(2,1)} fusion(bf16[1024,2048]{1,0:T(8,128)(2,1)} %param.20, f32[1024,2048,1]{1,0,2:T(8,128)} %fusion.176, f32[1024,2048,1]{1,0,2:T(8,128)} %fusion.175, bf16[2048,320]{1,0:T(8,128)(2,1)} %copy-done.7, bf16[1024,256]{1,0:T(8,128)(2,1)} %copy-done.40, bf16[1024,64]{1,0:T(8,128)(2,1)S(1)} %get-tuple-element.181), kind=kOutput, calls=%fused_computation.10 | convolution fusion | flops 1353973760 | bytes 27131904 | tf_op jit(solution)/shard_map/dot_general | solution.py:868
  1056.5 3.9 fusion.75
  1072.6 3.8 copy.422
  1076.4 22.3 %collective-permute-done.34.refs_0_ = bf16[512,512]{1,0:T(8,128)(2,1)} collective-permute-done((bf16[512,512]{1,0:T(8,128)(2,1)}, bf16[512,512]{1,0:T(8,128)(2,1)}, u32[]{:S(2)}, u32[]{:S(2)}) %collective-permute-start.34) | collective-permute-done | bytes 524320 | tf_op jit(solution)/shard_map/ppermute | solution.py:535
  1100.4 43.3 %collective-permute-done.37 = bf16[512,512]{1,0:T(8,128)(2,1)} collective-permute-done((bf16[512,512]{1,0:T(8,128)(2,1)}, bf16[512,512]{1,0:T(8,128)(2,1)}, u32[]{:S(2)}, u32[]{:S(2)}) %collective-permute-start.37) | collective-permute-done | bytes 524320 | tf_op jit(solution)/shard_map/ppermute | solution.py:535
  1156.6 6.6 copy.420
  1179.1 9.4 all_gather.47
  (699 shorter events, 280.4 us)
Async XLA Ops:
  7.2 165.7 %all-gather.11.cloned.1.call-start = ((), (), s32[]{:S(2)}) async-start(), calls=%async_computation.10 | async-start | bytes 18874368 | tf_op jit(solution)/shard_map/all_gather | solution.py:709
  10.6 18.1 %collective-permute-start = (bf16[512,512]{1,0:T(8,128)(2,1)S(1)}, bf16[512,512]{1,0:T(8,128)(2,1)}, u32[]{:S(2)}, u32[]{:S(2)}) collective-permute-start(bf16[512,512]{1,0:T(8,128)(2,1)S(1)} %copy.328), channel_id=1, source_target_pairs={{0,8},{8,16},{16,24},{24,0},{1,9},{9,17},{17,25},{25,1},{2,10},{10... | collective-permute-start | bytes 1572872 | tf_op jit(solution)/shard_map/ppermute | solution.py:520
  13.7 36.7 %collective-permute-start.1 = (bf16[512,512]{1,0:T(8,128)(2,1)S(1)}, bf16[512,512]{1,0:T(8,128)(2,1)}, u32[]{:S(2)}, u32[]{:S(2)}) collective-permute-start(bf16[512,512]{1,0:T(8,128)(2,1)S(1)} %copy.328), channel_id=1, source_target_pairs={{0,16},{8,24},{16,0},{24,8},{1,17},{9,25},{17,1},{25,9},{2,18},{10... | collective-permute-start | bytes 1572872 | tf_op jit(solution)/shard_map/ppermute | solution.py:520
  16.3 35.9 %collective-permute-start.2 = (bf16[512,512]{1,0:T(8,128)(2,1)S(1)}, bf16[512,512]{1,0:T(8,128)(2,1)}, u32[]{:S(2)}, u32[]{:S(2)}) collective-permute-start(bf16[512,512]{1,0:T(8,128)(2,1)S(1)} %copy.328), channel_id=1, source_target_pairs={{0,24},{8,0},{16,8},{24,16},{1,25},{9,1},{17,9},{25,17},{2,26},{10... | collective-permute-start | bytes 1572872 | tf_op jit(solution)/shard_map/ppermute | solution.py:520
  54.1 305.6 %all-gather.13.cloned.1.call-start = ((), (), s32[]{:S(2)}) async-start(), calls=%async_computation.11 | async-start | bytes 18874368 | tf_op jit(solution)/shard_map/all_gather | solution.py:709
  66.8 23.0 %collective-permute-start.3 = (bf16[512,320]{1,0:T(8,128)(2,1)}, bf16[512,320]{1,0:T(8,128)(2,1)S(1)}, u32[]{:S(2)}, u32[]{:S(2)}) collective-permute-start(bf16[512,320]{1,0:T(8,128)(2,1)} %after.37), channel_id=1, source_target_pairs={{0,8},{8,16},{16,24},{24,0},{1,9},{9,17},{17,25},{25,1},{2,10},{10... | collective-permute-start | bytes 983048 | tf_op jit(solution)/shard_map/ppermute | solution.py:520
  76.7 29.6 %collective-permute-start.4 = (bf16[512,320]{1,0:T(8,128)(2,1)}, bf16[512,320]{1,0:T(8,128)(2,1)S(1)}, u32[]{:S(2)}, u32[]{:S(2)}) collective-permute-start(bf16[512,320]{1,0:T(8,128)(2,1)} %after.37), channel_id=1, source_target_pairs={{0,16},{8,24},{16,0},{24,8},{1,17},{9,25},{17,1},{25,9},{2,18},{10... | collective-permute-start | bytes 983048 | tf_op jit(solution)/shard_map/ppermute | solution.py:520
  81.4 24.9 %collective-permute-start.5 = (bf16[512,320]{1,0:T(8,128)(2,1)}, bf16[512,320]{1,0:T(8,128)(2,1)S(1)}, u32[]{:S(2)}, u32[]{:S(2)}) collective-permute-start(bf16[512,320]{1,0:T(8,128)(2,1)} %after.37), channel_id=1, source_target_pairs={{0,24},{8,0},{16,8},{24,16},{1,25},{9,1},{17,9},{25,17},{2,26},{10... | collective-permute-start | bytes 983048 | tf_op jit(solution)/shard_map/ppermute | solution.py:520
  107.6 38.1 %collective-permute-start.7 = (bf16[512,512]{1,0:T(8,128)(2,1)}, bf16[512,512]{1,0:T(8,128)(2,1)}, u32[]{:S(2)}, u32[]{:S(2)}) collective-permute-start(bf16[512,512]{1,0:T(8,128)(2,1)} %after.39), channel_id=1, source_target_pairs={{0,8},{8,16},{16,24},{24,0},{1,9},{9,17},{17,25},{25,1},{2,10},{10... | collective-permute-start | bytes 1572872 | tf_op jit(solution)/shard_map/ppermute | solution.py:520
  116.4 33.7 %collective-permute-start.8 = (bf16[512,512]{1,0:T(8,128)(2,1)}, bf16[512,512]{1,0:T(8,128)(2,1)}, u32[]{:S(2)}, u32[]{:S(2)}) collective-permute-start(bf16[512,512]{1,0:T(8,128)(2,1)} %after.39), channel_id=1, source_target_pairs={{0,16},{8,24},{16,0},{24,8},{1,17},{9,25},{17,1},{25,9},{2,18},{10... | collective-permute-start | bytes 1572872 | tf_op jit(solution)/shard_map/ppermute | solution.py:520
  116.4 34.3 %collective-permute-start.9 = (bf16[512,512]{1,0:T(8,128)(2,1)}, bf16[512,512]{1,0:T(8,128)(2,1)S(1)}, u32[]{:S(2)}, u32[]{:S(2)}) collective-permute-start(bf16[512,512]{1,0:T(8,128)(2,1)} %after.39), channel_id=1, source_target_pairs={{0,24},{8,0},{16,8},{24,16},{1,25},{9,1},{17,9},{25,17},{2,26},{10... | collective-permute-start | bytes 1572872 | tf_op jit(solution)/shard_map/ppermute | solution.py:520
  156.3 323.1 %all-gather.15.cloned.1.call-start = ((), (), s32[]{:S(2)}) async-start(), calls=%async_computation.12 | async-start | bytes 9437184 | tf_op jit(solution)/shard_map/all_gather | solution.py:723
  158.1 39.9 %collective-permute-start.10 = (bf16[512,256]{1,0:T(8,128)(2,1)}, bf16[512,256]{1,0:T(8,128)(2,1)S(1)}, u32[]{:S(2)}, u32[]{:S(2)}) collective-permute-start(bf16[512,256]{1,0:T(8,128)(2,1)} %after.43), channel_id=1, source_target_pairs={{0,8},{8,16},{16,24},{24,0},{1,9},{9,17},{17,25},{25,1},{2,10},{10... | collective-permute-start | bytes 786440 | tf_op jit(solution)/shard_map/ppermute | solution.py:520
  169.5 34.0 %collective-permute-start.11 = (bf16[512,256]{1,0:T(8,128)(2,1)}, bf16[512,256]{1,0:T(8,128)(2,1)S(1)}, u32[]{:S(2)}, u32[]{:S(2)}) collective-permute-start(bf16[512,256]{1,0:T(8,128)(2,1)} %after.43), channel_id=1, source_target_pairs={{0,16},{8,24},{16,0},{24,8},{1,17},{9,25},{17,1},{25,9},{2,18},{10... | collective-permute-start | bytes 786440 | tf_op jit(solution)/shard_map/ppermute | solution.py:520
  172.9 31.3 %collective-permute-start.12 = (bf16[512,256]{1,0:T(8,128)(2,1)}, bf16[512,256]{1,0:T(8,128)(2,1)S(1)}, u32[]{:S(2)}, u32[]{:S(2)}) collective-permute-start(bf16[512,256]{1,0:T(8,128)(2,1)} %after.43), channel_id=1, source_target_pairs={{0,24},{8,0},{16,8},{24,16},{1,25},{9,1},{17,9},{25,17},{2,26},{10... | collective-permute-start | bytes 786440 | tf_op jit(solution)/shard_map/ppermute | solution.py:520
  208.8 285.1 %all-gather.17.cloned.1.call-start = ((), (), s32[]{:S(2)}) async-start(), calls=%async_computation.13 | async-start | bytes 9437184 | tf_op jit(solution)/shard_map/all_gather | solution.py:723
  217.8 10.2 collective-permute-start.13
  219.8 20.5 %collective-permute-start.14 = (bf16[512,256]{1,0:T(8,128)(2,1)}, bf16[512,256]{1,0:T(8,128)(2,1)}, u32[]{:S(2)}, u32[]{:S(2)}) collective-permute-start(bf16[512,256]{1,0:T(8,128)(2,1)} %after.47), channel_id=1, source_target_pairs={{0,16},{8,24},{16,0},{24,8},{1,17},{9,25},{17,1},{25,9},{2,18},{10... | collective-permute-start | bytes 786440 | tf_op jit(solution)/shard_map/ppermute | solution.py:520
  220.7 19.6 %collective-permute-start.15 = (bf16[512,256]{1,0:T(8,128)(2,1)}, bf16[512,256]{1,0:T(8,128)(2,1)}, u32[]{:S(2)}, u32[]{:S(2)}) collective-permute-start(bf16[512,256]{1,0:T(8,128)(2,1)} %after.47), channel_id=1, source_target_pairs={{0,24},{8,0},{16,8},{24,16},{1,25},{9,1},{17,9},{25,17},{2,26},{10... | collective-permute-start | bytes 786440 | tf_op jit(solution)/shard_map/ppermute | solution.py:520
  260.6 9.7 collective-permute-start.17
  272.5 21.2 %collective-permute-start.18 = (bf16[8,128,256]{2,1,0:T(8,128)(2,1)}, bf16[8,128,256]{2,1,0:T(8,128)(2,1)S(1)}, u32[]{:S(2)}, u32[]{:S(2)}) collective-permute-start(bf16[8,128,256]{2,1,0:T(8,128)(2,1)} %fusion.69), channel_id=1, source_target_pairs={{0,2},{1,3},{2,0},{3,1},{4,6},{5,7},{6,4},{7,5},{8,10},{9,11},{10,... | collective-permute-start | bytes 1572872 | tf_op jit(solution)/shard_map/ppermute | solution.py:556
  294.8 25.9 %collective-permute-start.19 = (bf16[8,128,256]{2,1,0:T(8,128)(2,1)}, bf16[8,128,256]{2,1,0:T(8,128)(2,1)S(1)}, u32[]{:S(2)}, u32[]{:S(2)}) collective-permute-start(bf16[8,128,256]{2,1,0:T(8,128)(2,1)} %fusion.35), channel_id=1, source_target_pairs={{0,4},{1,5},{2,6},{3,7},{4,0},{5,1},{6,2},{7,3},{8,12},{9,13},{10,... | collective-permute-start | bytes 1572872 | tf_op jit(solution)/shard_map/ppermute | solution.py:556
  300.6 487.4 %reduce-scatter.6.cloned.1.call-start = ((), (), s32[]{:S(2)}) async-start(), calls=%async_computation.5 | async-start | bytes 9437184 | tf_op jit(solution)/shard_map/reduce_scatter | solution.py:758
  382.8 8.6 collective-permute-start.20
  411.6 14.0 %collective-permute-start.22 = (bf16[8,128,256]{2,1,0:T(8,128)(2,1)S(1)}, bf16[8,128,256]{2,1,0:T(8,128)(2,1)S(1)}, u32[]{:S(2)}, u32[]{:S(2)}) collective-permute-start(bf16[8,128,256]{2,1,0:T(8,128)(2,1)S(1)} %fusion.68), channel_id=1, source_target_pairs={{0,2},{1,3},{2,0},{3,1},{4,6},{5,7},{6,4},{7,5},{8,10},{9,11},{10,... | collective-permute-start | bytes 1572872 | tf_op jit(solution)/shard_map/ppermute | solution.py:556
  425.9 13.2 %collective-permute-start.23 = (bf16[8,128,256]{2,1,0:T(8,128)(2,1)S(1)}, bf16[8,128,256]{2,1,0:T(8,128)(2,1)S(1)}, u32[]{:S(2)}, u32[]{:S(2)}) collective-permute-start(bf16[8,128,256]{2,1,0:T(8,128)(2,1)S(1)} %fusion.40), channel_id=1, source_target_pairs={{0,4},{1,5},{2,6},{3,7},{4,0},{5,1},{6,2},{7,3},{8,12},{9,13},{10,... | collective-permute-start | bytes 1572872 | tf_op jit(solution)/shard_map/ppermute | solution.py:556
  527.7 260.3 %reduce-scatter.8.cloned.1.call-start = ((), (), s32[]{:S(2)}) async-start(), calls=%async_computation.6 | async-start | bytes 9437184 | tf_op jit(solution)/shard_map/reduce_scatter | solution.py:758
  567.0 13.8 %collective-permute-start.24 = (bf16[8,128,256]{2,1,0:T(8,128)(2,1)S(1)}, bf16[8,128,256]{2,1,0:T(8,128)(2,1)S(1)}, u32[]{:S(2)}, u32[]{:S(2)}) collective-permute-start(bf16[8,128,256]{2,1,0:T(8,128)(2,1)S(1)} %convert_element_type.234), channel_id=1, source_target_pairs={{0,1},{1,0},{2,3},{3,2},{4,5},{5,4},{6,7},{7,6},{8,9},{9,8},{10,11... | collective-permute-start | bytes 1572872 | tf_op jit(solution)/shard_map/ppermute | solution.py:556
  581.0 23.1 %collective-permute-start.25 = (bf16[8,128,256]{2,1,0:T(8,128)(2,1)S(1)}, bf16[8,128,256]{2,1,0:T(8,128)(2,1)S(1)}, u32[]{:S(2)}, u32[]{:S(2)}) collective-permute-start(bf16[8,128,256]{2,1,0:T(8,128)(2,1)S(1)} %fusion.67), channel_id=1, source_target_pairs={{0,2},{1,3},{2,0},{3,1},{4,6},{5,7},{6,4},{7,5},{8,10},{9,11},{10,... | collective-permute-start | bytes 1572872 | tf_op jit(solution)/shard_map/ppermute | solution.py:556
  604.4 19.5 %collective-permute-start.26 = (bf16[8,128,256]{2,1,0:T(8,128)(2,1)S(1)}, bf16[8,128,256]{2,1,0:T(8,128)(2,1)S(1)}, u32[]{:S(2)}, u32[]{:S(2)}) collective-permute-start(bf16[8,128,256]{2,1,0:T(8,128)(2,1)S(1)} %fusion.45), channel_id=1, source_target_pairs={{0,4},{1,5},{2,6},{3,7},{4,0},{5,1},{6,2},{7,3},{8,12},{9,13},{10,... | collective-permute-start | bytes 1572872 | tf_op jit(solution)/shard_map/ppermute | solution.py:556
  623.9 268.8 %reduce-scatter.10.cloned.1.call-start = ((), (), s32[]{:S(2)}) async-start(), calls=%async_computation.7 | async-start | bytes 18874368 | tf_op jit(solution)/shard_map/reduce_scatter | solution.py:796
  753.5 282.2 %reduce-scatter.12.cloned.1.call-start = ((), (), s32[]{:S(2)}) async-start(), calls=%async_computation.8 | async-start | bytes 18874368 | tf_op jit(solution)/shard_map/reduce_scatter | solution.py:796
  758.8 14.3 %collective-permute-start.29 = (bf16[8,128,256]{2,1,0:T(8,128)(2,1)S(1)}, bf16[8,128,256]{2,1,0:T(8,128)(2,1)S(1)}, u32[]{:S(2)}, u32[]{:S(2)}) collective-permute-start(bf16[8,128,256]{2,1,0:T(8,128)(2,1)S(1)} %fusion.66), channel_id=1, source_target_pairs={{0,2},{1,3},{2,0},{3,1},{4,6},{5,7},{6,4},{7,5},{8,10},{9,11},{10,... | collective-permute-start | bytes 1572872 | tf_op jit(solution)/shard_map/ppermute | solution.py:556
  773.3 13.4 %collective-permute-start.30 = (bf16[8,128,256]{2,1,0:T(8,128)(2,1)S(1)}, bf16[8,128,256]{2,1,0:T(8,128)(2,1)S(1)}, u32[]{:S(2)}, u32[]{:S(2)}) collective-permute-start(bf16[8,128,256]{2,1,0:T(8,128)(2,1)S(1)} %fusion.50), channel_id=1, source_target_pairs={{0,4},{1,5},{2,6},{3,7},{4,0},{5,1},{6,2},{7,3},{8,12},{9,13},{10,... | collective-permute-start | bytes 1572872 | tf_op jit(solution)/shard_map/ppermute | solution.py:556
  917.7 245.5 %reduce-scatter.14.cloned.1.call-start = ((), (), s32[]{:S(2)}) async-start(), calls=%async_computation.9 | async-start | bytes 3538944 | tf_op jit(solution)/shard_map/reduce_scatter | solution.py:861
  970.3 12.4 %collective-permute-start.32 = (f32[8,256]{1,0:T(8,128)S(1)}, f32[8,256]{1,0:T(8,128)S(1)}, u32[]{:S(2)}, u32[]{:S(2)}) collective-permute-start(f32[8,256]{1,0:T(8,128)S(1)} %slice.419), channel_id=1, source_target_pairs={{1,0},{2,1},{3,2},{4,3},{5,4},{6,5},{7,6},{9,8},{10,9},{11,10},{12... | collective-permute-start | bytes 24584 | tf_op jit(solution)/shard_map/ppermute | solution.py:825
  973.9 61.8 %collective-permute-start.47 = (bf16[256,512]{1,0:T(8,128)(2,1)}, bf16[256,512]{1,0:T(8,128)(2,1)}, u32[]{:S(2)}, u32[]{:S(2)}) collective-permute-start(bf16[256,512]{1,0:T(8,128)(2,1)} %get-tuple-element.219), channel_id=1, source_target_pairs={{0,24},{8,0},{16,8},{24,16},{1,25},{9,1},{17,9},{25,17},{2,26},{10... | collective-permute-start | bytes 786440 | tf_op jit(solution)/shard_map/ppermute | solution.py:535
  976.7 72.8 %collective-permute-start.46 = (bf16[256,512]{1,0:T(8,128)(2,1)}, bf16[256,512]{1,0:T(8,128)(2,1)}, u32[]{:S(2)}, u32[]{:S(2)}) collective-permute-start(bf16[256,512]{1,0:T(8,128)(2,1)} %get-tuple-element.220), channel_id=1, source_target_pairs={{0,16},{8,24},{16,0},{24,8},{1,17},{9,25},{17,1},{25,9},{2,18},{10... | collective-permute-start | bytes 786440 | tf_op jit(solution)/shard_map/ppermute | solution.py:535
  976.7 74.9 %collective-permute-start.45 = (bf16[256,512]{1,0:T(8,128)(2,1)}, bf16[256,512]{1,0:T(8,128)(2,1)}, u32[]{:S(2)}, u32[]{:S(2)}) collective-permute-start(bf16[256,512]{1,0:T(8,128)(2,1)} %get-tuple-element.218), channel_id=1, source_target_pairs={{0,8},{8,16},{16,24},{24,0},{1,9},{9,17},{17,25},{25,1},{2,10},{10... | collective-permute-start | bytes 786440 | tf_op jit(solution)/shard_map/ppermute | solution.py:535
  979.9 72.3 %collective-permute-start.44 = (bf16[256,512]{1,0:T(8,128)(2,1)}, bf16[256,512]{1,0:T(8,128)(2,1)}, u32[]{:S(2)}, u32[]{:S(2)}) collective-permute-start(bf16[256,512]{1,0:T(8,128)(2,1)} %get-tuple-element.216), channel_id=1, source_target_pairs={{0,24},{8,0},{16,8},{24,16},{1,25},{9,1},{17,9},{25,17},{2,26},{10... | collective-permute-start | bytes 786440 | tf_op jit(solution)/shard_map/ppermute | solution.py:535
  982.7 71.1 %collective-permute-start.43 = (bf16[256,512]{1,0:T(8,128)(2,1)}, bf16[256,512]{1,0:T(8,128)(2,1)}, u32[]{:S(2)}, u32[]{:S(2)}) collective-permute-start(bf16[256,512]{1,0:T(8,128)(2,1)} %get-tuple-element.217), channel_id=1, source_target_pairs={{0,16},{8,24},{16,0},{24,8},{1,17},{9,25},{17,1},{25,9},{2,18},{10... | collective-permute-start | bytes 786440 | tf_op jit(solution)/shard_map/ppermute | solution.py:535
  1035.7 18.0 %collective-permute-start.42 = (bf16[256,512]{1,0:T(8,128)(2,1)}, bf16[256,512]{1,0:T(8,128)(2,1)}, u32[]{:S(2)}, u32[]{:S(2)}) collective-permute-start(bf16[256,512]{1,0:T(8,128)(2,1)} %get-tuple-element.215), channel_id=1, source_target_pairs={{0,8},{8,16},{16,24},{24,0},{1,9},{9,17},{17,25},{25,1},{2,10},{10... | collective-permute-start | bytes 786440 | tf_op jit(solution)/shard_map/ppermute | solution.py:535
  1049.5 15.1 %collective-permute-start.35 = (bf16[512,512]{1,0:T(8,128)(2,1)}, bf16[512,512]{1,0:T(8,128)(2,1)}, u32[]{:S(2)}, u32[]{:S(2)}) collective-permute-start(bf16[512,512]{1,0:T(8,128)(2,1)} %get-tuple-element.203), channel_id=1, source_target_pairs={{0,24},{8,0},{16,8},{24,16},{1,25},{9,1},{17,9},{25,17},{2,26},{10... | collective-permute-start | bytes 1572872 | tf_op jit(solution)/shard_map/ppermute | solution.py:535
  1051.7 47.0 %collective-permute-start.34 = (bf16[512,512]{1,0:T(8,128)(2,1)}, bf16[512,512]{1,0:T(8,128)(2,1)}, u32[]{:S(2)}, u32[]{:S(2)}) collective-permute-start(bf16[512,512]{1,0:T(8,128)(2,1)} %get-tuple-element.204), channel_id=1, source_target_pairs={{0,16},{8,24},{16,0},{24,8},{1,17},{9,25},{17,1},{25,9},{2,18},{10... | collective-permute-start | bytes 1572872 | tf_op jit(solution)/shard_map/ppermute | solution.py:535
  1052.2 46.4 %collective-permute-start.33 = (bf16[512,512]{1,0:T(8,128)(2,1)}, bf16[512,512]{1,0:T(8,128)(2,1)}, u32[]{:S(2)}, u32[]{:S(2)}) collective-permute-start(bf16[512,512]{1,0:T(8,128)(2,1)} %get-tuple-element.202), channel_id=1, source_target_pairs={{0,8},{8,16},{16,24},{24,0},{1,9},{9,17},{17,25},{25,1},{2,10},{10... | collective-permute-start | bytes 1572872 | tf_op jit(solution)/shard_map/ppermute | solution.py:535
  1061.6 38.8 %collective-permute-start.38 = (bf16[512,512]{1,0:T(8,128)(2,1)}, bf16[512,512]{1,0:T(8,128)(2,1)}, u32[]{:S(2)}, u32[]{:S(2)}) collective-permute-start(bf16[512,512]{1,0:T(8,128)(2,1)} %get-tuple-element.206), channel_id=1, source_target_pairs={{0,24},{8,0},{16,8},{24,16},{1,25},{9,1},{17,9},{25,17},{2,26},{10... | collective-permute-start | bytes 1572872 | tf_op jit(solution)/shard_map/ppermute | solution.py:535
  1063.9 79.7 %collective-permute-start.37 = (bf16[512,512]{1,0:T(8,128)(2,1)}, bf16[512,512]{1,0:T(8,128)(2,1)}, u32[]{:S(2)}, u32[]{:S(2)}) collective-permute-start(bf16[512,512]{1,0:T(8,128)(2,1)} %get-tuple-element.207), channel_id=1, source_target_pairs={{0,16},{8,24},{16,0},{24,8},{1,17},{9,25},{17,1},{25,9},{2,18},{10... | collective-permute-start | bytes 1572872 | tf_op jit(solution)/shard_map/ppermute | solution.py:535
  1064.6 79.0 %collective-permute-start.36 = (bf16[512,512]{1,0:T(8,128)(2,1)}, bf16[512,512]{1,0:T(8,128)(2,1)}, u32[]{:S(2)}, u32[]{:S(2)}) collective-permute-start(bf16[512,512]{1,0:T(8,128)(2,1)} %get-tuple-element.205), channel_id=1, source_target_pairs={{0,8},{8,16},{16,24},{24,0},{1,9},{9,17},{17,25},{25,1},{2,10},{10... | collective-permute-start | bytes 1572872 | tf_op jit(solution)/shard_map/ppermute | solution.py:535
  (127 other events, 1985.1 us)
Sparse Core Ops, SparseCore 0:
  54.2 100.2 all-gather.10
  157.0 101.1 all-gather.12
  260.7 69.2 all-gather.14
  332.2 54.4 all-gather.16
  527.8 79.9 reduce-scatter.5
  624.0 70.6 reduce-scatter.7
  753.6 117.6 reduce-scatter.9
  917.9 117.6 reduce-scatter.11
  1039.0 46.2 reduce-scatter.13

commit v2 on v1

--- a/solution.py
+++ b/solution.py
@@ -55,14 +55,19 @@
     return tiles[0] if len(tiles) == 1 else jnp.concatenate(tiles, axis=1)
 
 
-def head_sums(value, heads):
-    first = lax.broadcasted_iota(jnp.int32, (value.shape[0], 128), 1) < HEAD_DIM
-    sums = []
-    for pair in range(heads // 2):
-        tile = value[:, 128 * pair : 128 * (pair + 1)]
-        sums.append(jnp.sum(jnp.where(first, tile, 0.0), axis=1, keepdims=True))
-        sums.append(jnp.sum(jnp.where(first, 0.0, tile), axis=1, keepdims=True))
-    return sums
+def head_sums(one, two, heads):
+    width = one.shape[1]
+    lanes = lax.broadcasted_iota(jnp.int32, (width, 2 * heads), 0) // HEAD_DIM
+    places = lax.broadcasted_iota(jnp.int32, (width, 2 * heads), 1)
+    pick_one = jnp.where(lanes == places, 1.0, 0.0).astype(bf16)
+    pick_two = jnp.where(lanes + heads == places, 1.0, 0.0).astype(bf16)
+    one_high = one.astype(bf16)
+    two_high = two.astype(bf16)
+    one_low = (one - one_high.astype(f32)).astype(bf16)
+    two_low = (two - two_high.astype(f32)).astype(bf16)
+    return (dot(one_high, pick_one) + dot(one_low, pick_one)) + (
+        dot(two_high, pick_two) + dot(two_low, pick_two)
+    )
 
 
 def head_mask(width, head):
@@ -71,7 +76,7 @@
 
 
 def block_rows(index):
-    return pl.ds(pl.multiple_of(index * BLOCK, BLOCK), BLOCK)
+    return pl.ds(index * BLOCK, BLOCK)
 
 
 def filtered(extended, taps, base):
@@ -93,76 +98,66 @@
     return rows >= lax.broadcasted_iota(jnp.int32, (BLOCK, BLOCK), 1)
 
 
-def load_signal(part_ref, halo_ref, xext, width):
-    rows = part_ref.shape[1]
-    xext[0:8] = halo_ref[0, :, width:].astype(f32)
-    xext[8 : 8 + rows] = part_ref[0, :, width:].astype(f32)
-
-
-def state_kernel(width, part_ref, halo_ref, par_ref, cols_ref, bt_ref, state_ref, xext, weighted):
+def state_kernel(
+    width, x_ref, halo_ref, par_ref, cols_ref, bt_ref, state_ref, u_ref, xext, weighted
+):
     heads = width // HEAD_DIM
-    rows = part_ref.shape[1]
-    load_signal(part_ref, halo_ref, xext, width)
+    rows = x_ref.shape[1]
+    xext[0:8] = halo_ref[0, :, width:]
+    xext[8 : 8 + rows] = x_ref[0]
     taps = par_ref[0, :, width:]
     for block in range(rows // BLOCK):
         at = pl.ds(block * BLOCK, BLOCK)
         u = filtered(xext, taps, block * BLOCK)
+        u_ref[0, at, :] = u
         weight = expand(cols_ref[0, at, :], WDEV_COL, heads)
         weighted[at] = (u * sigmoid(u) * weight).astype(bf16)
     state_ref[0] = dot(bt_ref[...], weighted[...])
 
 
 def forward_kernel(
-    width, part_ref, halo_ref, par_ref, cols_ref, arow_ref, b_ref, c_ref, bt_ref, sin_ref,
-    gated_ref, sq_ref, xext, signal, scores, state, squares,
+    width, z_ref, u_ref, par_ref, cols_ref, arow_ref, b_ref, c_ref, bt_ref, sin_ref, *rest
 ):
+    gained_ref, sq_ref, states_ref, scores, squares = rest[-5:]
     heads = width // HEAD_DIM
-    rows = part_ref.shape[1]
+    rows = z_ref.shape[1]
     blocks = rows // BLOCK
 
     @pl.when(pl.program_id(0) == 0)
     def _():
         squares[...] = jnp.zeros_like(squares)
         for block in range(blocks):
-            at = pl.ds(block * BLOCK, BLOCK)
+            at = block_rows(block)
             scores[block] = exact_dot(c_ref[at], b_ref[at], NT)
 
-    load_signal(part_ref, halo_ref, xext, width)
-    taps = par_ref[0, :, width:]
     gain = par_ref[0, 5:6, width:]
     skip = par_ref[0, 6:7, width:]
+    causal = causal_mask()
+    state = sin_ref[0]
+    states_ref[0, 0] = state
     for block in range(blocks):
-        u = filtered(xext, taps, block * BLOCK)
-        signal[pl.ds(block * BLOCK, BLOCK)] = u * sigmoid(u)
-    state[...] = sin_ref[0]
-
-    def body(block, carry):
         at = block_rows(block)
-        causal = causal_mask()
         cols = cols_ref[0, at, :]
-        x = signal[at]
+        u = u_ref[0, at, :]
+        x = u * sigmoid(u)
         xl = x.astype(bf16)
-        s = state[...].astype(bf16)
         ea = expand(cols, EA_COL, heads)
-        y = ea * dot(c_ref[at].astype(bf16), s)
+        y = ea * dot(c_ref[at].astype(bf16), state.astype(bf16))
         g = scores[block]
         for head in range(heads):
             m = (g * decay_of(cols, arow_ref, block, head, heads, causal)).astype(bf16)
             y = y + dot(m, xl * head_mask(width, head))
-        z = part_ref[0, at, :width].astype(f32)
+        z = z_ref[0, at, :]
         gated = (y + skip * x) * (z * sigmoid(z))
-        gated_ref[0, at, :] = (gated * gain).astype(bf16)
+        gained_ref[0, at, :] = (gated * gain).astype(bf16)
         sq = gated * gated
         total = sq[:, :128]
         for tile in range(1, width // 128):
             total = total + sq[:, 128 * tile : 128 * (tile + 1)]
         squares[at] += total
         weight = expand(cols, W_COL, heads)
-        bt = bt_ref[block]
-        state[...] = ea[BLOCK - 1 :] * state[...] + dot(bt, (weight * x).astype(bf16))
-        return carry
-
-    lax.fori_loop(0, blocks, body, 0)
+        state = ea[BLOCK - 1 :] * state + dot(bt_ref[block], (weight * x).astype(bf16))
+        states_ref[0, block + 1] = state
 
     @pl.when(pl.program_id(0) == pl.num_programs(0) - 1)
     def _():
@@ -179,18 +174,18 @@
 
 
 def back_state_kernel(
-    width, part_ref, ngrad_ref, gated_ref, par_ref, cols_ref, row_ref, ct_ref,
+    width, z_ref, ngrad_ref, gated_ref, par_ref, cols_ref, row_ref, ct_ref,
     dstate_ref, gain_ref, weighted,
 ):
     heads = width // HEAD_DIM
-    rows = part_ref.shape[1]
+    rows = z_ref.shape[1]
     gain_sum = jnp.zeros((8, width), f32)
     for block in range(rows // BLOCK):
         at = pl.ds(block * BLOCK, BLOCK)
         ngrad = ngrad_ref[0, at, :]
         gated = gated_ref[0, at, :]
         grad, silu_z, _ = gate_grads(
-            part_ref[0, at, :], ngrad, gated, par_ref[0], row_ref[at], width
+            z_ref[0, at, :], ngrad, gated, par_ref[0], row_ref[at], width
         )
         weight = expand(cols_ref[0, at, :], EADEV_COL, heads)
         weighted[at] = (grad * silu_z * weight).astype(bf16)
@@ -238,10 +233,10 @@
 
 
 def backward_kernel(
-    width, part_ref, halo_ref, ngrad_ref, gated_ref, par_ref, cols_ref, arow_ref, row_ref,
-    b_ref, c_ref, bt_ref, ct_ref, sin_ref, din_ref,
+    width, part_ref, u_ref, halo_ref, ngrad_ref, gained_ref, par_ref, cols_ref, arow_ref, row_ref,
+    b_ref, c_ref, ct_ref, states_ref, din_ref,
     dpart_ref, tail_ref, head_ref, sums_ref, dcols_ref, dbc_ref,
-    xext, uval, scores, dscores, states, dstate, duext, skip_sum, dbacc, dcacc,
+    scores, dscores, duext, dbacc, dcacc,
 ):
     heads = width // HEAD_DIM
     rows = part_ref.shape[1]
@@ -254,127 +249,102 @@
         dbacc[...] = jnp.zeros_like(dbacc)
         dcacc[...] = jnp.zeros_like(dcacc)
         for block in range(blocks):
-            at = pl.ds(block * BLOCK, BLOCK)
+            at = block_rows(block)
             scores[block] = exact_dot(c_ref[at], b_ref[at], NT)
 
-    load_signal(part_ref, halo_ref, xext, width)
     taps = par_ref[0, :, width:]
     skip = par_ref[0, 6:7, width:]
-    for block in range(blocks):
-        uval[pl.ds(block * BLOCK, BLOCK)] = filtered(xext, taps, block * BLOCK)
-    states[0] = sin_ref[0]
-    dstate[...] = din_ref[0]
-    skip_sum[...] = jnp.zeros_like(skip_sum)
-
-    def state_body(block, carry):
+    skip_sum = jnp.zeros((8, width), f32)
+    tap_sums = [jnp.zeros((8, width), f32) for _ in range(CONV + 1)]
+    causal = causal_mask()
+    is_last = lax.broadcasted_iota(jnp.int32, (BLOCK, 1), 0) == BLOCK - 1
+    d = din_ref[0]
+    duext[rows : rows + 8] = jnp.zeros((8, width), f32)
+    for block in range(blocks - 1, -1, -1):
         at = block_rows(block)
-        cols = cols_ref[0, at, :]
-        u = uval[at]
-        weight = expand(cols, W_COL, heads)
-        last = expand(cols[BLOCK - 8 :], EA_COL, heads)[7:8]
-        states[block + 1] = last * states[block] + dot(
-            bt_ref[block], (weight * (u * sigmoid(u))).astype(bf16)
-        )
-        return carry
-
-    lax.fori_loop(0, blocks, state_body, 0)
-
-    def body(count, carry):
-        block = blocks - 1 - count
-        at = block_rows(block)
-        causal = causal_mask()
         cols = cols_ref[0, at, :]
         part = part_ref[0, at, :]
         grad, silu_z, slope_z = gate_grads(
-            part, ngrad_ref[0, at, :], gated_ref[0, at, :], par_ref[0], row_ref[at], width
-        )
-        u = uval[at]
+            part, ngrad_ref[0, at, :], gained_ref[0, at, :], par_ref[0], row_ref[at], width
+        )
+        u = u_ref[0, at, :]
         su = sigmoid(u)
         x = u * su
         xl = x.astype(bf16)
         dy = grad * silu_z
         dyl = dy.astype(bf16)
         dyt = dy.T.astype(bf16)
-        s = states[block].astype(bf16)
-        d = dstate[...]
+        s = states_ref[0, block].astype(bf16)
         dl = d.astype(bf16)
         ea = expand(cols, EA_COL, heads)
         weight = expand(cols, W_COL, heads)
-        b = b_ref[at].astype(bf16)
-        c = c_ref[at].astype(bf16)
         g = scores[block]
-        y = ea * dot(c, s)
+        y = ea * dot(c_ref[at].astype(bf16), s)
         dg = dscores[block]
         terms = product_terms(dy, x)
         dxt = []
         for head in range(heads):
             decay = decay_of(cols, arow_ref, block, head, heads, causal)
             m = (g * decay).astype(bf16)
-            keep = head_mask(width, head)
-            y = y + dot(m, xl * keep)
-            dm = dot(terms[head][0], terms[head][1], NT)
-            dg = dg + dm * decay
+            y = y + dot(m, xl * head_mask(width, head))
+            dg = dg + dot(terms[head][0], terms[head][1], NT) * decay
             dxt.append(dot(dyt[HEAD_DIM * head : HEAD_DIM * (head + 1)], m))
         dscores[block] = dg
-        dx = jnp.concatenate(dxt, axis=0).T + weight * dot(b, dl)
-        xf = xl.astype(f32)
-        zz = xf * dx
+        dx = jnp.concatenate(dxt, axis=0).T + weight * dot(b_ref[at].astype(bf16), dl)
+        zz = xl.astype(f32) * dx
         da = dyl.astype(f32) * y - zz
-        ends = jnp.sum(states[block + 1] * d, axis=0, keepdims=True)
-        is_last = lax.broadcasted_iota(jnp.int32, (BLOCK, 1), 0) == BLOCK - 1
+        ends = jnp.sum(states_ref[0, block + 1] * d, axis=0, keepdims=True)
         da = da + jnp.where(is_last, ends, 0.0)
-        columns = head_sums(da, heads) + head_sums(zz, heads)
-        lanes = lax.broadcasted_iota(jnp.int32, (BLOCK, 2 * heads), 1)
-        packed = jnp.broadcast_to(columns[0], (BLOCK, 2 * heads))
-        for at_lane in range(1, 2 * heads):
-            packed = jnp.where(lanes == at_lane, columns[at_lane], packed)
-        dcols_ref[0, at, :] = packed
+        dcols_ref[0, at, :] = head_sums(da, zz, heads)
         edy = (ea * dy).astype(bf16)
         dcacc[at] += dot(edy, s, NT)
         dbacc[at] += dot((weight * x).astype(bf16), dl, NT)
-        dstate[...] = ea[BLOCK - 1 :] * d + dot(ct_ref[block], edy)
+        d = ea[BLOCK - 1 :] * d + dot(ct_ref[block], edy)
         du = (dx + skip * dy) * (su * (1.0 + u * (1.0 - su)))
         duext[at] = du
-        skip_sum[...] += fold_rows(dy * x)
+        skip_sum = skip_sum + fold_rows(dy * x)
         dz = grad * (y + skip * x) * slope_z
         dpart_ref[0, at, :width] = dz.astype(bf16)
-        return carry
-
-    lax.fori_loop(0, blocks, body, 0)
-    duext[rows : rows + 8] = jnp.zeros((8, width), f32)
-
-    tap_sums = [jnp.zeros((8, width), f32) for _ in range(CONV + 1)]
-    for block in range(blocks):
-        base = block * BLOCK
-        du = duext[base : base + BLOCK]
-        dx = taps[CONV - 1 : CONV] * du
+
+        raw = part[:, width:]
+        draw = taps[CONV - 1 : CONV] * du
         tap_sums[CONV] = tap_sums[CONV] + fold_rows(du)
-        for offset in range(CONV):
-            begin = base + 8 - (CONV - 1) + offset
-            tap_sums[offset] = tap_sums[offset] + fold_rows(du * xext[begin : begin + BLOCK])
-            if offset < CONV - 1:
-                ahead = base + CONV - 1 - offset
-                dx = dx + taps[offset : offset + 1] * duext[ahead : ahead + BLOCK]
-        dpart_ref[0, base : base + BLOCK, width:] = dx.astype(bf16)
+        tap_sums[CONV - 1] = tap_sums[CONV - 1] + fold_rows(du * raw)
+        for offset in range(CONV - 1):
+            ahead = block * BLOCK + CONV - 1 - offset
+            shifted = duext[ahead : ahead + BLOCK]
+            draw = draw + taps[offset : offset + 1] * shifted
+            tap_sums[offset] = tap_sums[offset] + fold_rows(shifted * raw)
+        dpart_ref[0, at, width:] = draw.astype(bf16)
         if block == blocks - 1:
-            tail_ref[0, :, width:] = dx[BLOCK - 16 :]
+            tail_ref[0, :, width:] = draw[BLOCK - 16 :]
+
     tail_ref[0, :, :width] = dpart_ref[0, rows - 16 : rows, :width].astype(f32)
+    first_du = duext[0:8]
     head_ref[0, :, :width] = jnp.zeros((8, width), f32)
-    head_ref[0, :, width:] = duext[0:8]
-    lines = tap_sums + [jnp.zeros((8, width), f32), skip_sum[...]]
+    head_ref[0, :, width:] = first_du
+    for offset in range(CONV - 1):
+        for row in range(CONV - 1 - offset):
+            at_halo = 8 - (CONV - 1) + offset + row
+            tap_sums[offset] = tap_sums[offset] + jnp.where(
+                lax.broadcasted_iota(jnp.int32, (8, 1), 0) == row,
+                first_du * halo_ref[0, at_halo : at_halo + 1, width:],
+                0.0,
+            )
+    lines = tap_sums + [jnp.zeros((8, width), f32), skip_sum]
     out_rows = [jnp.sum(line, axis=0, keepdims=True) for line in lines]
     sums_ref[0] = jnp.concatenate(out_rows + [jnp.zeros((1, width), f32)], axis=0)
 
     @pl.when(step == pl.num_programs(0) - 1)
     def _():
         for block in range(blocks):
-            at = pl.ds(block * BLOCK, BLOCK)
+            at = block_rows(block)
             dg = dscores[block]
             dbc_ref[at, :STATE] = dbacc[at] + exact_dot(dg.T, c_ref[at])
             dbc_ref[at, STATE:] = dcacc[at] + exact_dot(dg, b_ref[at])
 
 
-def run_kernels(rows, shards, width):
+def run_kernels(rows, shards, width, group=0, groups=1):
     heads = width // HEAD_DIM
     steps = shards
     blocks = rows // BLOCK
@@ -393,6 +363,8 @@
     halo = over(8, 2 * width)
     par = over(8, 2 * width)
     chan = over(rows, width)
+    group_chan = pl.BlockSpec((1, rows, width), lambda i: (i, 0, group))
+    anywhere = pl.BlockSpec(memory_space=pl.ANY)
     cols = each(rows, KINDS * heads)
     arow = each(blocks, heads, BLOCK)
     state = over(STATE, width)
@@ -411,12 +383,14 @@
             flops=elements * per_element, bytes_accessed=elements * reads, transcendentals=0
         )
 
+    x_only = pl.BlockSpec((1, rows, width), lambda i: (i, 0, 1))
+    all_states = each(blocks + 1, STATE, width)
     local_state = pl.pallas_call(
         functools.partial(state_kernel, width),
         grid=(steps,),
-        in_specs=[part, halo, par, cols, bct_flat],
-        out_specs=state,
-        out_shape=shape((shards, STATE, chans), f32),
+        in_specs=[x_only, halo, par, cols, bct_flat],
+        out_specs=[state, chan],
+        out_shape=[shape((shards, STATE, chans), f32), shape((shards, rows, chans), f32)],
         scratch_shapes=[pltpu.VMEM((rows + 8, width), f32), pltpu.VMEM((rows, width), bf16)],
         compiler_params=params,
         cost_estimate=cost(7000, 8),
@@ -425,14 +399,16 @@
     forward = pl.pallas_call(
         functools.partial(forward_kernel, width),
         grid=(steps,),
-        in_specs=[part, halo, par, cols, arow, bc, bc, bct, state],
-        out_specs=[chan, whole(rows, 1)],
-        out_shape=[shape((shards, rows, chans), bf16), shape((rows, 1), f32)],
+        in_specs=[chan, chan, par, cols, arow, bc, bc, bct, state] + [anywhere] * (group > 0),
+        out_specs=[group_chan, whole(rows, 1), all_states],
+        input_output_aliases={9: 0} if group else {},
+        out_shape=[
+            shape((shards, rows, groups * chans), bf16),
+            shape((rows, 1), f32),
+            shape((shards, blocks + 1, STATE, chans), f32),
+        ],
         scratch_shapes=[
-            pltpu.VMEM((rows + 8, width), f32),
-            pltpu.VMEM((rows, width), f32),
             pltpu.VMEM((blocks, BLOCK, BLOCK), f32),
-            pltpu.VMEM((STATE, width), f32),
             pltpu.VMEM((rows, 128), f32),
         ],
         compiler_params=params,
@@ -442,7 +418,7 @@
     back_state = pl.pallas_call(
         functools.partial(back_state_kernel, width),
         grid=(steps,),
-        in_specs=[part, chan, chan, par, cols, rowcols, bct_flat],
+        in_specs=[chan, group_chan, group_chan, par, cols, rowcols, bct_flat],
         out_specs=[state, over(8, width)],
         out_shape=[shape((shards, STATE, chans), f32), shape((shards, 8, chans), f32)],
         scratch_shapes=[pltpu.VMEM((rows, width), bf16)],
@@ -454,7 +430,8 @@
         functools.partial(backward_kernel, width),
         grid=(steps,),
         in_specs=[
-            part, halo, chan, chan, par, cols, arow, rowcols, bc, bc, bct, bct, state, state
+            part, chan, halo, group_chan, group_chan, par, cols, arow, rowcols, bc, bc, bct, all_states,
+            state,
         ],
         out_specs=[
             part, over(16, 2 * width), over(8, 2 * width), over(8, width),
@@ -469,14 +446,9 @@
             shape((rows, 2 * STATE), f32),
         ],
         scratch_shapes=[
-            pltpu.VMEM((rows + 8, width), f32),
-            pltpu.VMEM((rows, width), f32),
             pltpu.VMEM((blocks, BLOCK, BLOCK), f32),
             pltpu.VMEM((blocks, BLOCK, BLOCK), f32),
-            pltpu.VMEM((blocks + 1, STATE, width), f32),
-            pltpu.VMEM((STATE, width), f32),
             pltpu.VMEM((rows + 8, width), f32),
-            pltpu.VMEM((8, width), f32),
             pltpu.VMEM((rows, STATE), f32),
             pltpu.VMEM((rows, STATE), f32),
         ],
@@ -502,12 +474,23 @@
     )(value, *others)
 
 
-def dp_sum(array):
-    size = lax.axis_size("dp")
-    total = array
-    for k in range(1, size):
-        total = total + lax.ppermute(array, "dp", [(i, (i + k) % size) for i in range(size)])
-    return total
+def mp_scatter(array, hold):
+    devices = lax.axis_size("mp")
+    me = lax.axis_index("mp")
+    dims = devices.bit_length() - 1
+    array = array.reshape((2,) * dims + array.shape[1:])
+    hold = list(hold)
+    for bit in range(dims):
+        axis = dims - 1 - bit
+        upper = lax.rem(lax.div(me, 1 << bit), 2)
+        keep = lax.dynamic_index_in_dim(array, upper, axis, keepdims=False)
+        give = lax.dynamic_index_in_dim(array, 1 - upper, axis, keepdims=False)
+        got = lax.ppermute(give, "mp", [(i, i ^ (1 << bit)) for i in range(devices)])
+        ahead = hold.pop(0) if hold else None
+        if ahead is not None:
+            got = after(got, ahead)
+        array = keep + got
+    return array
 
 
 def dp_gather(array, *meanwhile):
@@ -539,35 +522,41 @@
     return total
 
 
-def carried_states(own, totals, reverse):
+def exchange_states(carry, totals, reverse, *hold):
+    span, own, result, result_log = carry
     devices = lax.axis_size("mp")
-    me = lax.axis_index("mp")
+    place = lax.div(lax.axis_index("mp"), span)
     shards, _, chans = own.shape
 
     def over_channels(logs):
         per_chan = jnp.repeat(logs.reshape(shards, 1, -1), HEAD_DIM, axis=-1)
         return jnp.exp(per_chan)
 
-    result = jnp.zeros_like(own)
-    result_log = jnp.zeros_like(totals[0])
-    group_logs = totals
-    span = 1
-    while span < devices:
-        got = lax.ppermute(own.astype(bf16), "mp", [(i, i ^ span) for i in range(devices)])
-        got = got.astype(f32)
-        high = lax.rem(me // span, 2) == 1
-        nearer = jnp.logical_not(high) if reverse else high
-        mine_log = lax.dynamic_index_in_dim(group_logs, me // span, 0, keepdims=False)
-        theirs = lax.bitwise_xor(me // span, 1)
-        their_log = lax.dynamic_index_in_dim(group_logs, theirs, 0, keepdims=False)
-        result = result + jnp.where(nearer, over_channels(result_log), 0.0) * got
-        result_log = result_log + jnp.where(nearer, their_log, 0.0)
-        if 2 * span < devices:
-            own = jnp.where(nearer, 1.0, over_channels(their_log)) * own
-            own = own + jnp.where(nearer, over_channels(mine_log), 1.0) * got
-        group_logs = group_logs.reshape(-1, 2, totals.shape[1]).sum(axis=1)
-        span *= 2
-    return result
+    got = lax.ppermute(own.astype(bf16), "mp", [(i, i ^ span) for i in range(devices)])
+    if hold:
+        got = after(got, *hold)
+    got = got.astype(f32)
+    group_logs = totals.reshape(devices // span, span, -1).sum(axis=1)
+    high = lax.rem(place, 2) == 1
+    nearer = jnp.logical_not(high) if reverse else high
+    mine_log = lax.dynamic_index_in_dim(group_logs, place, 0, keepdims=False)
+    their_log = lax.dynamic_index_in_dim(
+        group_logs, lax.bitwise_xor(place, 1), 0, keepdims=False
+    )
+    result = result + jnp.where(nearer, over_channels(result_log), 0.0) * got
+    result_log = result_log + jnp.where(nearer, their_log, 0.0)
+    if 2 * span < devices:
+        own = jnp.where(nearer, 1.0, over_channels(their_log)) * own
+        own = own + jnp.where(nearer, over_channels(mine_log), 1.0) * got
+    return 2 * span, own, result, result_log
+
+
+def carried_states(own, totals, reverse, hold=(), until=None):
+    carry = (1, own, jnp.zeros_like(own), jnp.zeros_like(totals[0]))
+    hold = list(hold)
+    while carry[0] < (until or lax.axis_size("mp")):
+        carry = exchange_states(carry, totals, reverse, *(hold.pop(0) if hold else ()))
+    return carry
 
 
 def causal_filter(extended, taps, rows):
@@ -624,12 +613,11 @@
     blocks = rows // BLOCK
     onward = [(i, i + 1) for i in range(shards - 1)]
     homeward = [(i + 1, i) for i in range(shards - 1)]
-    local_state, forward, back_state, backward = run_kernels(rows, shards, width)
+    kernels = [run_kernels(rows, shards, width, group, groups) for group in range(groups)]
 
     inner_groups = inner_weight.reshape(own_model, groups, step_heads, 2, HEAD_DIM)
     inner_groups = inner_groups.astype(bf16).transpose(1, 0, 3, 2, 4)
     inner_groups = inner_groups.reshape(groups, own_model, 2 * width)
-    out_groups = output_weight.astype(bf16).reshape(own_model, groups, width)
 
     packed = jnp.concatenate(
         [
@@ -707,7 +695,7 @@
     for group in range(1, groups):
         inner_low.append(dp_gather(after(inner_groups[group], small), columns[0], totals_all))
     inner_full = [lax.all_gather(own, "mp", axis=0) for own in inner_low]
-    parts, halos, states_in, gained = [], [], [], []
+    parts, halos, all_states, all_u, gained_before = [], [], [], [], []
     squares = 0.0
     ready = [columns[0]]
     for group in range(groups):
@@ -717,27 +705,25 @@
         )
         halo = lax.ppermute(part[:, rows - 8 :], "mp", onward)
         if group == 0:
-            out_low = [
-                dp_gather(after(out_groups[:, g], inner_low[-1]), halo) for g in range(groups)
-            ]
-            out_full = [lax.all_gather(own, "mp", axis=0) for own in out_low]
-            halo = after(halo, *out_low)
-        ends = local_state(part, halo, params[group], columns[group], writer_t)
-        state_in = carried_states(ends, totals_groups[group], False)
-        out, sq = forward(
-            part, halo, params[group], columns[group], arows[group], writer, reader,
-            writer_blocks, state_in,
-        )
+            out_low = dp_gather(after(output_weight.astype(bf16), inner_low[-1]), halo)
+            out_full = lax.all_gather(out_low, "mp", axis=0)
+            halo = after(halo, out_low)
+        ends, u = kernels[group][0](part, halo, params[group], columns[group], writer_t)
+        state_in = carried_states(ends, totals_groups[group], False)[2]
+        gained, sq, states = kernels[group][1](
+            part, u, params[group], columns[group], arows[group], writer, reader,
+            writer_blocks, state_in, *gained_before,
+        )
+        gained_before = [gained]
         squares = squares + sq
-        ready = [out]
+        ready = [states]
         parts.append(part)
         halos.append(halo)
-        states_in.append(state_in)
-        gained.append(out)
+        all_states.append(states)
+        all_u.append(u)
     norm_scale = lax.rsqrt(squares / INNER + eps_norm)
-    branch = norm_scale * sum(
-        jnp.einsum("mtc,mdc->td", gained[group], out_full[group], preferred_element_type=f32)
-        for group in range(groups)
+    branch = norm_scale * jnp.einsum(
+        "mtc,mdc->td", gained, out_full, preferred_element_type=f32
     )
     positions = mine * rows + jnp.arange(rows)
     live = (positions < lengths[0]).astype(f32)[:, None]
@@ -748,35 +734,35 @@
     row_columns = jnp.concatenate(
         [norm_scale, norm_scale * norm_scale * scaled_sum / INNER], axis=1
     )
-    scaled_cot = after((masked.astype(f32) * norm_scale).astype(bf16), row_columns)
-    out_parts = [
-        jnp.einsum(
-            "td,mtc->mcd", scaled_cot, gained[group], preferred_element_type=f32
-        ).astype(bf16)
-        for group in range(groups)
-    ]
-    out_sums = [lax.psum_scatter(part, "mp", scatter_dimension=0) for part in out_parts]
-    ngrads, starts, gain_sums = [], [], []
+    normed_grad = jnp.einsum("td,mdc->mtc", masked, out_full, preferred_element_type=f32)
+    starts, gain_sums = [], []
     for group in range(groups):
-        normed_grad = jnp.einsum(
-            "td,mdc->mtc", masked, out_full[group], preferred_element_type=f32
-        )
-        start, gain_sum = back_state(
-            parts[group], normed_grad, gained[group], params[group], columns[group],
-            row_columns, reader_t,
-        )
-        ngrads.append(normed_grad)
+        start, gain_sum = kernels[group][2](
+            parts[group], normed_grad, gained, params[group], columns[group],
+            after(row_columns, *starts), reader_t,
+        )
         starts.append(start)
         gain_sums.append(gain_sum)
-    dstates = [carried_states(starts[g], totals_groups[g], True) for g in range(groups)]
-    waiting = out_parts + starts[1:]
+    scaled_cot = after((masked.astype(f32) * norm_scale).astype(bf16), starts[-1])
+    out_part = jnp.einsum(
+        "td,mtc->mcd", scaled_cot, gained, preferred_element_type=f32
+    ).astype(bf16)
+    out_sum = lax.psum_scatter(out_part, "mp", scatter_dimension=0)
+    carries = []
+    for group in range(groups):
+        hold = [starts[1:], [out_part]] if group == 0 else [[out_part]]
+        until = shards if group == 0 else shards // 2
+        carries.append(carried_states(starts[group], totals_groups[group], True, hold, until))
+    waiting = [carry[1] for carry in carries[1:]] + [out_part]
     dparts, inner_sums, dbc, all_sums, all_dcols = [], [], 0.0, [], []
     for group in range(groups):
-        last = group == groups - 1
-        dpart, tail, du_head, sums, dcols, dbc_here = backward(
-            parts[group], halos[group], ngrads[group], gained[group], params[group],
-            columns[group], arows[group], row_columns, writer, reader, writer_blocks,
-            reader_blocks, states_in[group], after(dstates[group], *waiting),
+        carry = carries[group]
+        if group:
+            carry = exchange_states(carry, totals_groups[group], True, dw_part)
+        dpart, tail, du_head, sums, dcols, dbc_here = kernels[group][3](
+            parts[group], all_u[group], halos[group], normed_grad, gained,
+            params[group], columns[group], arows[group], row_columns, writer, reader,
+            reader_blocks, all_states[group], after(carry[2], *waiting),
         )
         du_next = lax.ppermute(du_head, "mp", homeward)
         extra = [
@@ -789,12 +775,15 @@
         dpart = lax.dynamic_update_slice(
             dpart, (tail + extra).astype(bf16), (0, rows - 16, 0)
         )
-        if last:
-            dpart = after(dpart, *inner_sums)
         inner_part = jnp.einsum("td,mtc->mcd", tokens, dpart, preferred_element_type=f32)
-        inner_part = inner_part.astype(bf16)
+        inner_part = dw_part = inner_part.astype(bf16)
+        if group == 0:
+            out_sum = after(out_sum, dcols).reshape(chans, -1, own_model).transpose(1, 0, 2)
+            out_sum = lax.psum_scatter(out_sum, "dp", scatter_dimension=0)
+            inner_part = after(inner_part, out_sum)
+        inner_part = after(inner_part, *inner_sums)
         inner_sums.append(lax.psum_scatter(inner_part, "mp", scatter_dimension=0))
-        waiting = [inner_part] + (out_sums if group == groups - 2 else [])
+        waiting = [inner_part] + ([out_sum] if group == groups - 2 else [])
         dparts.append(dpart)
         dbc = dbc + dbc_here
         all_sums.append(sums)
@@ -858,25 +847,45 @@
         axis=1,
     )
     small_rows = heads_here + state_share
-    small_total = lax.psum_scatter(after(small_grad, inner_sums[-1]), "mp", scatter_dimension=0)
-
-    input_part = 0.0
-    for group in range(groups):
-        input_part = input_part + jnp.einsum(
-            "mtc,mdc->td", after(dparts[group], small_grad), inner_full[group], preferred_element_type=f32,
-        )
+    def input_gradient(group, *others):
+        return jnp.einsum(
+            "mtc,mdc->td", after(dparts[group], *others), inner_full[group],
+            preferred_element_type=f32,
+        )
+
+    input_parts = [input_gradient(group, small_grad) for group in range(groups - 1)]
+    output_gradient = after(out_sum, *input_parts).astype(f32).T
+    output_update = adam_rows(output_weight, output_gradient, output_moments, True)
+    inner_grads = [
+        dp_scatter(after(total, *input_parts), output_update) for total in inner_sums[:-1]
+    ]
+    small_total = mp_scatter(small_grad, input_parts + [output_update])
     small_part = lax.dot_general(dsmall, small, (NT, ((), ())), preferred_element_type=f32)
-    tokens_gradient = (cotangent.astype(f32) + input_part + small_part).astype(bf16)
-
-    early = [after(total, inner_part) for total in out_sums + inner_sums[:-1]]
-    early = [dp_scatter(total, tokens_gradient) for total in early]
-    out_grads, inner_grads = early[:groups], early[groups:]
-    inner_grads.append(dp_scatter(inner_sums[-1]))
-    small_sum = dp_scatter(small_total[:small_rows])
-    own = dp_sum(small_total[small_rows:]).reshape(-1)[:sum_size].reshape(-1, chans)
+    last_sum = inner_sums[-1].reshape(2 * width, -1, own_model).transpose(1, 0, 2)
+    input_parts.append(input_gradient(groups - 1, small_total, last_sum))
+    tokens_gradient = sum(input_parts) + (cotangent.astype(f32) + small_part)
+    tokens_gradient = tokens_gradient.astype(bf16)
+    last_sum = lax.psum_scatter(last_sum, "dp", scatter_dimension=0)
+    inner_grads.append(last_sum.astype(f32))
+
+    dp_size = lax.axis_size("dp")
+    dp_mine = lax.axis_index("dp")
+    sum_lines = small_total[small_rows:].reshape(-1, own_model)
+
+    def share(owner):
+        piece = lax.dynamic_slice_in_dim(small_total[:small_rows], owner * own_model, own_model, 1)
+        return jnp.concatenate([piece, sum_lines], axis=0)
+
+    small_sum = share(dp_mine)
+    for k in range(1, dp_size):
+        got = lax.ppermute(
+            share(lax.rem(dp_mine + k, dp_size)), "dp",
+            [(i, (i + k) % dp_size) for i in range(dp_size)],
+        )
+        small_sum = small_sum + after(got, tokens_gradient)
+    own = small_sum[small_rows:].reshape(-1)[:sum_size].reshape(-1, chans)
     step_gradient = small_sum[:heads_here].T
-    state_gradient = lax.all_gather(small_sum[heads_here:], "mp", axis=0, tiled=True).T
-    output_gradient = jnp.concatenate(out_grads, axis=0).T
+    state_gradient = lax.all_gather(small_sum[heads_here:small_rows], "mp", axis=0, tiled=True).T
     inner_gradient = jnp.stack(inner_grads)
     inner_gradient = inner_gradient.reshape(groups, 2, step_heads, HEAD_DIM, own_model)
     inner_gradient = inner_gradient.transpose(4, 0, 2, 1, 3)
@@ -890,7 +899,6 @@
     inner_update = adam_rows(inner_weight, inner_gradient, inner_moments, True)
     step_update = adam_rows(step_weight, step_gradient, step_moments, True)
     state_update = adam_rows(state_weight, state_gradient, state_moments, True)
-    output_update = adam_rows(output_weight, output_gradient, output_moments, True)
     inner_filter_update = adam_rows(inner_filter, inner_filter_gradient, inner_filter_moments, True)
     state_filter_update = adam_rows(state_filter, state_filter_gradient, state_filter_moments, True)
     head_update = adam_rows(head_params, head_gradient, head_moments, False)

time: 1210 us -> 1050 us (0.87)
  Pallas kernels: 340 us -> 248 us
  waiting for transfers between devices: 246 us -> 208 us
  matrix products: 250 us -> 234 us
  local copies, waits for them, and re-layouts: 152 us -> 138 us
    pallas_call x8, Pallas kernels: 340 us -> 247 us  [the longest x2 139 us: local(): kernels[group][3]]
    ppermute x15 -> x3, waiting for transfers between devices: 67 us -> 0.51 us  [dp_scatter(): got = lax.ppermute(piece, 'dp', [(i, (i + k) % size) for i in range(size)])]
    ppermute x15 -> x18, waiting for transfers between devices: 102 us -> 79.8 us  [the longest x12 58.5 us: exchange_states(): lax.ppermute(own.astype(bf16), 'mp', [(i, i ^ span) for i in range(device...]
    reduce_scatter x3, waiting for transfers between devices: 0.02 us -> 19.4 us  [the longest x1 12.4 us: local(): out_sum = lax.psum_scatter(out_sum, 'dp', scatter_dimension=0)]
    reduce_scatter x2, waiting for transfers between devices: 0.01 us -> 18 us  [local(): inner_sums.append(lax.psum_scatter(inner_part, 'mp', scatter_dimension=0))]
    ppermute x15 -> x12, starting transfers between devices: 50.7 us -> 34.3 us  [dp_gather(): got = lax.ppermute(array, 'dp', [(i, (i + k) % size) for i in range(size)])]
    ppermute x15 -> x12, waiting for transfers between devices: 72.6 us -> 88.2 us  [dp_gather(): got = lax.ppermute(array, 'dp', [(i, (i + k) % size) for i in range(size)])]
    ppermute x15 -> x3, starting transfers between devices: 19.8 us -> 4.43 us  [dp_scatter(): got = lax.ppermute(piece, 'dp', [(i, (i + k) % size) for i in range(size)])]
  transfers between devices with their start and end apart: 60 -> 47, of which waited for: 24 -> 22; matrix products, arithmetic and copies ran while one was open for 32% -> 31% of each run, Pallas kernels for 28% -> 21%
where the time goes in v2:
time: 1050 us; the launch traced here: 1040 us
  Pallas kernels  248 us (24%)
  matrix products  234 us (22%)
  waiting for transfers between devices  208 us (20%)
  local copies, waits for them, and re-layouts  138 us (13%)
  starting transfers between devices  84.7 us (8%)
  other arithmetic  76.7 us (7%)
  blocking collectives  28.9 us (3%)
  between operations  17.6 us (2%)
    pallas_call x2, Pallas kernels, local(): kernels[group][3]  139 us
    ppermute x12, waiting for transfers between devices, dp_gather(): got = lax.ppermute(array, 'dp', [(i, (i + k) % size) for i in range(size)])  88.2 us
    ppermute x12, waiting for transfers between devices, exchange_states(): lax.ppermute(own.astype(bf16), 'mp', [(i, i ^ span) for i in range(device...  58.5 us
    unnamed x295, local copies, waits for them, and re-layouts  51.6 us
    dot_general x2, matrix products, local(): jnp.einsum('td,mtc->mcd', tokens, dpart, preferred_element_type=f32)  48.9 us
    pallas_call x2, Pallas kernels, local(): kernels[group][1]  46.9 us
    dot_general x2, matrix products, input_gradient(): jnp.einsum('mtc,mdc->td', after(dparts[group], *others), inner_full[group...  46.1 us
    dot_general x2, matrix products, local(): jnp.einsum('td,mdc->mtc', tokens, inner_full[group], preferred_element_ty...  46 us
  transfers between devices with their start and end apart: 47, of which 22 were waited for; matrix products, arithmetic and copies ran while one was open for 31% of the time, Pallas kernels for 21%

profile of v2, /device:TPU:0, one launch (start us, length us, event | category | flops | bytes accessed | tf_op | source)
XLA Modules:
  0.0 1035.5 jit_solution(7495746287920194415)
XLA Ops:
  18.1 10.9 %collective-permute-done = bf16[512,512]{1,0:T(8,128)(2,1)} collective-permute-done((bf16[512,512]{1,0:T(8,128)(2,1)S(1)}, bf16[512,512]{1,0:T(8,128)(2,1)}, u32[]{:S(2)}, u32[]{:S(2)}) %collective-permute-start) | collective-permute-done | bytes 524320 | tf_op jit(solution)/shard_map/ppermute | solution.py:503
  30.1 20.4 %collective-permute-done.1 = bf16[512,512]{1,0:T(8,128)(2,1)S(1)} collective-permute-done((bf16[512,512]{1,0:T(8,128)(2,1)S(1)}, bf16[512,512]{1,0:T(8,128)(2,1)S(1)}, u32[]{:S(2)}, u32[]{:S(2)}) %collective-permute-start.1) | collective-permute-done | bytes 524320 | tf_op jit(solution)/shard_map/ppermute | solution.py:503
  53.8 9.3 all-gather.1
  65.8 11.7 %collective-permute-start.3 = (bf16[512,320]{1,0:T(8,128)(2,1)}, bf16[512,320]{1,0:T(8,128)(2,1)S(1)}, u32[]{:S(2)}, u32[]{:S(2)}) collective-permute-start(bf16[512,320]{1,0:T(8,128)(2,1)} %after.39), channel_id=1, source_target_pairs={{0,8},{8,16},{16,24},{24,0},{1,9},{9,17},{17,25},{25,1},{2,10},{10... | collective-permute-start | bytes 983048 | tf_op jit(solution)/shard_map/ppermute | solution.py:503
  81.4 7.5 collective-permute-done.3
  88.9 16.4 %collective-permute-done.4 = bf16[512,320]{1,0:T(8,128)(2,1)S(1)} collective-permute-done((bf16[512,320]{1,0:T(8,128)(2,1)}, bf16[512,320]{1,0:T(8,128)(2,1)S(1)}, u32[]{:S(2)}, u32[]{:S(2)}) %collective-permute-start.4) | collective-permute-done | bytes 327712 | tf_op jit(solution)/shard_map/ppermute | solution.py:503
  106.7 9.6 collective-permute-start.9
  117.0 5.2 convolution_bitcast_fusion.4
  133.8 9.5 all-gather.4
  143.5 19.4 %collective-permute-done.8.refs_0_ = bf16[512,512]{1,0:T(8,128)(2,1)} collective-permute-done((bf16[512,512]{1,0:T(8,128)(2,1)}, bf16[512,512]{1,0:T(8,128)(2,1)}, u32[]{:S(2)}, u32[]{:S(2)}) %collective-permute-start.8) | collective-permute-done | bytes 524320 | tf_op jit(solution)/shard_map/ppermute | solution.py:503
  172.5 23.1 %convolution_bitcast_fusion.2.x_ref.z_ref.part_ref = f32[8,1024,512]{2,1,0:T(8,128)S(1)} fusion(bf16[8,2048,512]{2,1,0:T(8,128)(2,1)} %after.40, bf16[1024,2048]{1,0:T(8,128)(2,1)} %param.19), kind=kOutput, calls=%fused_computation.9 | convolution fusion | flops 17179869184 | bytes 37748736 | tf_op jit(solution)/shard_map/td,mdc->mtc/dot_general | solution.py:703
  197.4 4.2 copy-done.128
  202.2 13.5 %collective-permute-done.11.refs_0_ = bf16[512,512]{1,0:T(8,128)(2,1)} collective-permute-done((bf16[512,512]{1,0:T(8,128)(2,1)}, bf16[512,512]{1,0:T(8,128)(2,1)}, u32[]{:S(2)}, u32[]{:S(2)}) %collective-permute-start.11) | collective-permute-done | bytes 524320 | tf_op jit(solution)/shard_map/ppermute | solution.py:503
  229.3 14.7 %local_state.2 = (f32[8,128,256]{2,1,0:T(8,128)}, f32[8,1024,256]{2,1,0:T(8,128)}) custom-call(f32[8,1024,512]{2,1,0:T(8,128)} %copy-done.128, f32[8,8,512]{2,1,0:T(8,128)} %after.49.halo_ref, f32[8,8,512]{2,1,0:T(8,128)} %concatenate.72.par_ref, f32[8,1024,20]{2,1,0:T(8,128)} %copy.442.refs_1_.cols_ref, bf16[128,1024]{1,0:T(8,128)(2,1)} %copy.451.bt_ref), custom_call_target="tpu_custom_call" | custom-call | flops 14680064000 | bytes 16777216 | tf_op jit(solution)/shard_map/local_state/pallas_call | solution.py:711
  257.1 9.0 collective-permute-done.15
  272.4 9.3 collective-permute-done.16
  284.0 23.4 %forward_scan.2 = (bf16[8,1024,512]{2,1,0:T(8,128)(2,1)}, f32[1024,1]{1,0:T(8,128)}, f32[8,5,128,256]{3,2,1,0:T(8,128)}) custom-call(f32[8,1024,512]{2,1,0:T(8,128)} %copy-done.128, f32[8,1024,256]{2,1,0:T(8,128)} %get-tuple-element.44.u_ref, f32[8,8,512]{2,1,0:T(8,128)} %concatenate.72.par_ref, f32[8,1024,20]{2,1,0:T(8,128)} %copy.442.refs_1_.cols_ref, ...), custom_call_target="tpu_custom_call" | custom-call | flops 35651584000 | bytes 20971520 | tf_op jit(solution)/shard_map/forward_scan/pallas_call | solution.py:713
  307.4 22.8 %convolution_bitcast_fusion.1.x_ref.z_ref.part_ref = f32[8,1024,512]{2,1,0:T(8,128)S(1)} fusion(bf16[8,2048,512]{2,1,0:T(8,128)(2,1)} %after.50, bf16[1024,2048]{1,0:T(8,128)(2,1)} %param.19), kind=kOutput, calls=%fused_computation.8 | convolution fusion | flops 17179869184 | bytes 37748736 | tf_op jit(solution)/shard_map/td,mdc->mtc/dot_general | solution.py:703
  330.3 13.0 %collective-permute-start.17 = (f32[8,8,512]{2,1,0:T(8,128)S(1)}, f32[8,8,512]{2,1,0:T(8,128)S(1)}, u32[]{:S(2)}, u32[]{:S(2)}) collective-permute-start(f32[8,8,512]{2,1,0:T(8,128)S(1)} %slice.391), channel_id=1, source_target_pairs={{0,1},{1,2},{2,3},{3,4},{4,5},{5,6},{6,7},{8,9},{9,10},{10,11},{11... | collective-permute-start | bytes 393224 | tf_op jit(solution)/shard_map/ppermute | solution.py:706
  347.8 14.8 %local_state.3 = (f32[8,128,256]{2,1,0:T(8,128)}, f32[8,1024,256]{2,1,0:T(8,128)}) custom-call(f32[8,1024,512]{2,1,0:T(8,128)} %copy-done.129, f32[8,8,512]{2,1,0:T(8,128)} %copy-done.133, f32[8,8,512]{2,1,0:T(8,128)} %concatenate.74.par_ref, f32[8,1024,20]{2,1,0:T(8,128)} %copy.463.cols_ref, bf16[128,1024]{1,0:T(8,128)(2,1)} %copy.451.bt_ref), custom_call_target="tpu_custom_call" | custom-call | flops 14680064000 | bytes 16777216 | tf_op jit(solution)/shard_map/local_state/pallas_call | solution.py:711
  367.2 3.7 collective-permute-start.19
  372.0 11.4 %collective-permute-done.19 = bf16[8,128,256]{2,1,0:T(8,128)(2,1)S(1)} collective-permute-done((bf16[8,128,256]{2,1,0:T(8,128)(2,1)S(1)}, bf16[8,128,256]{2,1,0:T(8,128)(2,1)S(1)}, u32[]{:S(2)}, u32[]{:S(2)}) %collective-permute-start.19) | collective-permute-done | bytes 524320 | tf_op jit(solution)/shard_map/ppermute | solution.py:535
  386.1 11.2 %collective-permute-done.20 = bf16[8,128,256]{2,1,0:T(8,128)(2,1)S(1)} collective-permute-done((bf16[8,128,256]{2,1,0:T(8,128)(2,1)S(1)}, bf16[8,128,256]{2,1,0:T(8,128)(2,1)S(1)}, u32[]{:S(2)}, u32[]{:S(2)}) %collective-permute-start.20) | collective-permute-done | bytes 524320 | tf_op jit(solution)/shard_map/ppermute | solution.py:535
  398.6 23.5 %forward_scan.3 = (bf16[8,1024,512]{2,1,0:T(8,128)(2,1)}, f32[1024,1]{1,0:T(8,128)}, f32[8,5,128,256]{3,2,1,0:T(8,128)}) custom-call(f32[8,1024,512]{2,1,0:T(8,128)} %copy-done.129, f32[8,1024,256]{2,1,0:T(8,128)} %get-tuple-element.48.u_ref, f32[8,8,512]{2,1,0:T(8,128)} %concatenate.74.par_ref, ...), custom_call_target="tpu_custom_call", output_to_operand_aliasing={{0}: (9, {})} | custom-call | flops 35651584000 | bytes 20971520 | tf_op jit(solution)/shard_map/forward_scan/pallas_call | solution.py:713
  423.4 24.9 %convolution_bitcast_fusion.ngrad_ref = f32[8,1024,512]{2,1,0:T(8,128)} fusion(bf16[8,2048,512]{2,1,0:T(8,128)(2,1)} %bitcast.403, bf16[1024,2048]{1,0:T(8,128)(2,1)} %param.20, f32[1024]{0:T(1024)S(1)} %fusion.95), kind=kOutput, calls=%fused_computation.7 | convolution fusion | flops 17186160640 | bytes 37752832 | tf_op jit(solution)/shard_map/td,mdc->mtc/dot_general | solution.py:737
  448.3 25.8 %fusion.3 = (f32[1024]{0:T(1024)S(1)}, bf16[1024,2048]{1,0:T(8,128)(2,1)}, bf16[1024,2048]{1,0:T(8,128)(2,1)}) fusion(f32[1024]{0:T(1024)S(1)} %get-tuple-element.213, f32[1024]{0:T(1024)S(1)} %fusion.95, bf16[1024,2048]{1,0:T(8,128)(2,1)S(1)} %copy-done.36, bf16[1024,2048]{1,0:T(8,128)(2,1)S(1)} %copy-done.131, ...), kind=kOutput, calls=%fused_computation.13 | convolution fusion | flops 17207132160 | bytes 41955328 | tf_op jit(solution)/shard_map/mtc,mdc->td/dot_general | solution.py:725
  476.5 16.0 %back_state.2 = (f32[8,128,256]{2,1,0:T(8,128)}, f32[8,8,256]{2,1,0:T(8,128)}) custom-call(f32[8,1024,512]{2,1,0:T(8,128)} %copy-done.128, f32[8,1024,512]{2,1,0:T(8,128)} %convolution_bitcast_fusion.ngrad_ref, bf16[8,1024,512]{2,1,0:T(8,128)(2,1)} %get-tuple-element.52.gated_ref.gained_ref, f32[8,8,512]{2,1,0:T(8,128)} %concatenate.72.par_ref, ...), custom_call_target="tpu_custom_call" | custom-call | flops 16777216000 | bytes 29360128 | tf_op jit(solution)/shard_map/back_state/pallas_call | solution.py:740
  492.5 16.0 %back_state.3 = (f32[8,128,256]{2,1,0:T(8,128)}, f32[8,8,256]{2,1,0:T(8,128)}) custom-call(f32[8,1024,512]{2,1,0:T(8,128)} %copy-done.129, f32[8,1024,512]{2,1,0:T(8,128)} %convolution_bitcast_fusion.ngrad_ref, bf16[8,1024,512]{2,1,0:T(8,128)(2,1)} %get-tuple-element.52.gated_ref.gained_ref, f32[8,8,512]{2,1,0:T(8,128)} %concatenate.74.par_ref, ...), custom_call_target="tpu_custom_call" | custom-call | flops 16777216000 | bytes 29360128 | tf_op jit(solution)/shard_map/back_state/pallas_call | solution.py:740
  508.5 25.0 %convolution_convert_fusion.2.refs_1_.refs_2_ = bf16[8,512,2048]{2,1,0:T(8,128)(2,1)} fusion(bf16[8,1024,512]{2,1,0:T(8,128)(2,1)} %get-tuple-element.52.gated_ref.gained_ref, bf16[1024,2048]{1,0:T(8,128)(2,1)} %after.54), kind=kOutput, calls=%fused_computation.2 | convolution fusion | flops 17188257792 | bytes 29360128 | tf_op jit(solution)/shard_map/td,mtc->mcd/dot_general | solution.py:747
  548.2 7.4 collective-permute-done.22.refs_0_
  559.4 6.8 collective-permute-done.25
  573.0 69.4 %backward_scan.2 = (bf16[8,1024,512]{2,1,0:T(8,128)(2,1)}, f32[8,16,512]{2,1,0:T(8,128)}, f32[8,8,512]{2,1,0:T(8,128)}, f32[8,8,256]{2,1,0:T(8,128)}, f32[8,1024,8]{2,1,0:T(8,128)}, /*index=5*/f32[1024,256]{1,0:T(8,128)}) custom-call(f32[8,1024,512]{2,1,0:T(8,128)} %copy-done.128, f32[8,1024,256]{2,1,0:T(8,128)} %get-tuple-element.44.u_ref, ...), custom_call_target="tpu_custom_call" | custom-call | flops 90177536000 | bytes 41943040 | tf_op jit(solution)/shard_map/backward_scan/pallas_call | solution.py:762
  642.5 7.0 reduce-scatter.6.cloned.1.call-done
  660.7 24.8 %convolution_convert_fusion.1.refs_1_.refs_0_ = bf16[8,512,2048]{2,1,0:T(8,128)(2,1)} fusion(bf16[8,1024,512]{2,1,0:T(8,128)(2,1)} %fusion.72.refs_0_, bf16[1024,2048]{1,0:T(8,128)(2,1)} %param.19), kind=kOutput, calls=%fused_computation.1 | convolution fusion | flops 17188257792 | bytes 29360128 | tf_op jit(solution)/shard_map/td,mtc->mcd/dot_general | solution.py:778
  686.3 12.4 %reduce-scatter.8.cloned.1.call-done = bf16[1,512,512]{2,1,0:T(8,128)(2,1)} async-done(((bf16[4,512,512]{2,1,0:T(8,128)(2,1)}), bf16[1,512,512]{2,1,0:T(8,128)(2,1)}) %reduce-scatter.8.cloned.1.call-update) | async-done | bytes 524304 | tf_op jit(solution)/shard_map/reduce_scatter | solution.py:782
  702.3 69.6 %backward_scan.3 = (bf16[8,1024,512]{2,1,0:T(8,128)(2,1)}, f32[8,16,512]{2,1,0:T(8,128)}, f32[8,8,512]{2,1,0:T(8,128)}, f32[8,8,256]{2,1,0:T(8,128)}, f32[8,1024,8]{2,1,0:T(8,128)}, /*index=5*/f32[1024,256]{1,0:T(8,128)}) custom-call(f32[8,1024,512]{2,1,0:T(8,128)} %copy-done.129, f32[8,1024,256]{2,1,0:T(8,128)} %get-tuple-element.48.u_ref, ...), custom_call_target="tpu_custom_call" | custom-call | flops 90177536000 | bytes 41943040 | tf_op jit(solution)/shard_map/backward_scan/pallas_call | solution.py:762
  777.2 24.0 %convolution_convert_fusion.refs_0_ = bf16[8,512,2048]{2,1,0:T(8,128)(2,1)} fusion(bf16[8,1024,512]{2,1,0:T(8,128)(2,1)} %fusion.71.refs_0_, bf16[1024,2048]{1,0:T(8,128)(2,1)S(1)} %copy-done.132), kind=kOutput, calls=%fused_computation | convolution fusion | flops 17188257792 | bytes 29360128 | tf_op jit(solution)/shard_map/td,mtc->mcd/dot_general | solution.py:778
  801.3 18.0 %reduce-scatter.10.cloned.1.call-done = bf16[1,512,2048]{2,1,0:T(8,128)(2,1)} async-done(((bf16[8,512,2048]{2,1,0:T(8,128)(2,1)}), bf16[1,512,2048]{2,1,0:T(8,128)(2,1)}) %reduce-scatter.10.cloned.1.call-update) | async-done | bytes 2097168 | tf_op jit(solution)/shard_map/reduce_scatter | solution.py:785
  822.2 4.5 fusion.132
  838.2 3.7 fusion.123
  855.9 4.0 fusion.60
  865.6 24.5 %convolution_bitcast_fusion.3.refs_1_ = f32[1024,2048]{1,0:T(8,128)} fusion(bf16[8,1024,512]{2,1,0:T(8,128)(2,1)} %after.66, bf16[8,2048,512]{2,1,0:T(8,128)(2,1)} %after.40), kind=kOutput, calls=%fused_computation.19 | convolution fusion | flops 17179869184 | bytes 33554432 | tf_op jit(solution)/shard_map/mtc,mdc->td/dot_general | solution.py:851
  908.9 18.5 %collective-permute-done.31 = f32[2,43,2048]{2,0,1:T(2,128)S(1)} collective-permute-done((f32[2,43,2048]{2,0,1:T(2,128)S(1)}, f32[2,43,2048]{2,0,1:T(2,128)S(1)}, u32[]{:S(2)}, u32[]{:S(2)}) %collective-permute-start.31) | collective-permute-done | bytes 704544 | tf_op jit(solution)/shard_map/ppermute | solution.py:488
  961.0 21.6 %fusion.145 = f32[1024,2048,1]{1,0,2:T(8,128)S(1)} fusion(bf16[8,1024,512]{2,1,0:T(8,128)(2,1)} %after.70, bf16[8,2048,512]{2,1,0:T(8,128)(2,1)} %after.50), kind=kOutput, calls=%fused_computation.361 | convolution fusion | flops 17179869184 | bytes 33554432 | tf_op jit(solution)/shard_map/mtc,mdc->td/dot_general | solution.py:851
  982.6 7.0 fusion.2.refs_1_
  993.8 10.1 all_gather.39
  1013.0 4.4 fusion.19
  1021.6 6.6 copy.516
  (715 shorter events, 248.0 us)
Async XLA Ops:
  7.2 165.3 %all-gather.9.cloned.1.call-start = ((), (), s32[]{:S(2)}) async-start(), calls=%async_computation.10 | async-start | bytes 18874368 | tf_op jit(solution)/shard_map/all_gather | solution.py:697
  10.9 18.1 %collective-permute-start = (bf16[512,512]{1,0:T(8,128)(2,1)S(1)}, bf16[512,512]{1,0:T(8,128)(2,1)}, u32[]{:S(2)}, u32[]{:S(2)}) collective-permute-start(bf16[512,512]{1,0:T(8,128)(2,1)S(1)} %copy.424), channel_id=1, source_target_pairs={{0,8},{8,16},{16,24},{24,0},{1,9},{9,17},{17,25},{25,1},{2,10},{10... | collective-permute-start | bytes 1572872 | tf_op jit(solution)/shard_map/ppermute | solution.py:503
  14.0 36.6 %collective-permute-start.1 = (bf16[512,512]{1,0:T(8,128)(2,1)S(1)}, bf16[512,512]{1,0:T(8,128)(2,1)S(1)}, u32[]{:S(2)}, u32[]{:S(2)}) collective-permute-start(bf16[512,512]{1,0:T(8,128)(2,1)S(1)} %copy.424), channel_id=1, source_target_pairs={{0,16},{8,24},{16,0},{24,8},{1,17},{9,25},{17,1},{25,9},{2,18},{10... | collective-permute-start | bytes 1572872 | tf_op jit(solution)/shard_map/ppermute | solution.py:503
  16.6 34.0 %collective-permute-start.2 = (bf16[512,512]{1,0:T(8,128)(2,1)S(1)}, bf16[512,512]{1,0:T(8,128)(2,1)}, u32[]{:S(2)}, u32[]{:S(2)}) collective-permute-start(bf16[512,512]{1,0:T(8,128)(2,1)S(1)} %copy.424), channel_id=1, source_target_pairs={{0,24},{8,0},{16,8},{24,16},{1,25},{9,1},{17,9},{25,17},{2,26},{10... | collective-permute-start | bytes 1572872 | tf_op jit(solution)/shard_map/ppermute | solution.py:503
  53.1 254.3 %all-gather.11.cloned.1.call-start = ((), (), s32[]{:S(2)}) async-start(), calls=%async_computation.11 | async-start | bytes 18874368 | tf_op jit(solution)/shard_map/all_gather | solution.py:697
  65.8 23.1 %collective-permute-start.3 = (bf16[512,320]{1,0:T(8,128)(2,1)}, bf16[512,320]{1,0:T(8,128)(2,1)S(1)}, u32[]{:S(2)}, u32[]{:S(2)}) collective-permute-start(bf16[512,320]{1,0:T(8,128)(2,1)} %after.39), channel_id=1, source_target_pairs={{0,8},{8,16},{16,24},{24,0},{1,9},{9,17},{17,25},{25,1},{2,10},{10... | collective-permute-start | bytes 983048 | tf_op jit(solution)/shard_map/ppermute | solution.py:503
  77.5 27.8 %collective-permute-start.4 = (bf16[512,320]{1,0:T(8,128)(2,1)}, bf16[512,320]{1,0:T(8,128)(2,1)S(1)}, u32[]{:S(2)}, u32[]{:S(2)}) collective-permute-start(bf16[512,320]{1,0:T(8,128)(2,1)} %after.39), channel_id=1, source_target_pairs={{0,16},{8,24},{16,0},{24,8},{1,17},{9,25},{17,1},{25,9},{2,18},{10... | collective-permute-start | bytes 983048 | tf_op jit(solution)/shard_map/ppermute | solution.py:503
  80.4 25.0 %collective-permute-start.5 = (bf16[512,320]{1,0:T(8,128)(2,1)S(1)}, bf16[512,320]{1,0:T(8,128)(2,1)S(1)}, u32[]{:S(2)}, u32[]{:S(2)}) collective-permute-start(bf16[512,320]{1,0:T(8,128)(2,1)S(1)} %copy-done.38), channel_id=1, source_target_pairs={{0,24},{8,0},{16,8},{24,16},{1,25},{9,1},{17,9},{25,17},{2,26},{10... | collective-permute-start | bytes 983048 | tf_op jit(solution)/shard_map/ppermute | solution.py:503
  106.7 36.8 %collective-permute-start.9 = (bf16[512,512]{1,0:T(8,128)(2,1)}, bf16[512,512]{1,0:T(8,128)(2,1)}, u32[]{:S(2)}, u32[]{:S(2)}) collective-permute-start(bf16[512,512]{1,0:T(8,128)(2,1)} %after.41), channel_id=1, source_target_pairs={{0,24},{8,0},{16,8},{24,16},{1,25},{9,1},{17,9},{25,17},{2,26},{10... | collective-permute-start | bytes 1572872 | tf_op jit(solution)/shard_map/ppermute | solution.py:503
  116.3 46.6 %collective-permute-start.8 = (bf16[512,512]{1,0:T(8,128)(2,1)}, bf16[512,512]{1,0:T(8,128)(2,1)}, u32[]{:S(2)}, u32[]{:S(2)}) collective-permute-start(bf16[512,512]{1,0:T(8,128)(2,1)} %after.41), channel_id=1, source_target_pairs={{0,16},{8,24},{16,0},{24,8},{1,17},{9,25},{17,1},{25,9},{2,18},{10... | collective-permute-start | bytes 1572872 | tf_op jit(solution)/shard_map/ppermute | solution.py:503
  117.0 46.0 %collective-permute-start.7 = (bf16[512,512]{1,0:T(8,128)(2,1)}, bf16[512,512]{1,0:T(8,128)(2,1)S(1)}, u32[]{:S(2)}, u32[]{:S(2)}) collective-permute-start(bf16[512,512]{1,0:T(8,128)(2,1)} %after.41), channel_id=1, source_target_pairs={{0,8},{8,16},{16,24},{24,0},{1,9},{9,17},{17,25},{25,1},{2,10},{10... | collective-permute-start | bytes 1572872 | tf_op jit(solution)/shard_map/ppermute | solution.py:503
  168.4 255.0 %all-gather.13.cloned.1.call-start = ((), (), s32[]{:S(2)}) async-start(), calls=%async_computation.12 | async-start | bytes 18874368 | tf_op jit(solution)/shard_map/all_gather | solution.py:709
  169.6 31.9 %collective-permute-start.12 = (bf16[512,512]{1,0:T(8,128)(2,1)}, bf16[512,512]{1,0:T(8,128)(2,1)}, u32[]{:S(2)}, u32[]{:S(2)}) collective-permute-start(bf16[512,512]{1,0:T(8,128)(2,1)} %after.45), channel_id=1, source_target_pairs={{0,24},{8,0},{16,8},{24,16},{1,25},{9,1},{17,9},{25,17},{2,26},{10... | collective-permute-start | bytes 1572872 | tf_op jit(solution)/shard_map/ppermute | solution.py:503
  169.6 46.1 %collective-permute-start.11 = (bf16[512,512]{1,0:T(8,128)(2,1)}, bf16[512,512]{1,0:T(8,128)(2,1)}, u32[]{:S(2)}, u32[]{:S(2)}) collective-permute-start(bf16[512,512]{1,0:T(8,128)(2,1)} %after.45), channel_id=1, source_target_pairs={{0,16},{8,24},{16,0},{24,8},{1,17},{9,25},{17,1},{25,9},{2,18},{10... | collective-permute-start | bytes 1572872 | tf_op jit(solution)/shard_map/ppermute | solution.py:503
  170.5 45.2 %collective-permute-start.10 = (bf16[512,512]{1,0:T(8,128)(2,1)}, bf16[512,512]{1,0:T(8,128)(2,1)S(1)}, u32[]{:S(2)}, u32[]{:S(2)}) collective-permute-start(bf16[512,512]{1,0:T(8,128)(2,1)} %after.45), channel_id=1, source_target_pairs={{0,8},{8,16},{16,24},{24,0},{1,9},{9,17},{17,25},{25,1},{2,10},{10... | collective-permute-start | bytes 1572872 | tf_op jit(solution)/shard_map/ppermute | solution.py:503
  195.7 5.8 collective-permute-start.6
  221.2 428.3 %reduce-scatter.6.cloned.1.call-start = ((), (), s32[]{:S(2)}) async-start(), calls=%async_computation.5 | async-start | bytes 18874368 | tf_op jit(solution)/shard_map/reduce_scatter | solution.py:750
  222.1 4.6 collective-permute-start.13
  228.5 156.8 %copy-start.43 = (bf16[1024,128]{1,0:T(8,128)(2,1)}, bf16[1024,128]{1,0:T(8,128)(2,1)S(1)}, u32[]{:S(2)}) copy-start(bf16[1024,128]{1,0:T(8,128)(2,1)S(1)} %get-tuple-element.240) | copy-start | bytes 786436
  246.2 4.8 collective-permute-start.14
  252.0 14.1 %collective-permute-start.15 = (bf16[8,128,256]{2,1,0:T(8,128)(2,1)}, bf16[8,128,256]{2,1,0:T(8,128)(2,1)}, u32[]{:S(2)}, u32[]{:S(2)}) collective-permute-start(bf16[8,128,256]{2,1,0:T(8,128)(2,1)} %fusion.55), channel_id=1, source_target_pairs={{0,2},{1,3},{2,0},{3,1},{4,6},{5,7},{6,4},{7,5},{8,10},{9,11},{10,... | collective-permute-start | bytes 1572872 | tf_op jit(solution)/shard_map/ppermute | solution.py:535
  268.3 13.4 %collective-permute-start.16 = (bf16[8,128,256]{2,1,0:T(8,128)(2,1)}, bf16[8,128,256]{2,1,0:T(8,128)(2,1)S(1)}, u32[]{:S(2)}, u32[]{:S(2)}) collective-permute-start(bf16[8,128,256]{2,1,0:T(8,128)(2,1)} %fusion.24), channel_id=1, source_target_pairs={{0,4},{1,5},{2,6},{3,7},{4,0},{5,1},{6,2},{7,3},{8,12},{9,13},{10,... | collective-permute-start | bytes 1572872 | tf_op jit(solution)/shard_map/ppermute | solution.py:535
  330.3 16.9 %collective-permute-start.17 = (f32[8,8,512]{2,1,0:T(8,128)S(1)}, f32[8,8,512]{2,1,0:T(8,128)S(1)}, u32[]{:S(2)}, u32[]{:S(2)}) collective-permute-start(f32[8,8,512]{2,1,0:T(8,128)S(1)} %slice.391), channel_id=1, source_target_pairs={{0,1},{1,2},{2,3},{3,4},{4,5},{5,6},{6,7},{8,9},{9,10},{10,11},{11... | collective-permute-start | bytes 393224 | tf_op jit(solution)/shard_map/ppermute | solution.py:706
  364.0 3.0 collective-permute-start.18
  367.2 16.1 %collective-permute-start.19 = (bf16[8,128,256]{2,1,0:T(8,128)(2,1)S(1)}, bf16[8,128,256]{2,1,0:T(8,128)(2,1)S(1)}, u32[]{:S(2)}, u32[]{:S(2)}) collective-permute-start(bf16[8,128,256]{2,1,0:T(8,128)(2,1)S(1)} %fusion.54), channel_id=1, source_target_pairs={{0,2},{1,3},{2,0},{3,1},{4,6},{5,7},{6,4},{7,5},{8,10},{9,11},{10,... | collective-permute-start | bytes 1572872 | tf_op jit(solution)/shard_map/ppermute | solution.py:535
  383.6 13.7 %collective-permute-start.20 = (bf16[8,128,256]{2,1,0:T(8,128)(2,1)S(1)}, bf16[8,128,256]{2,1,0:T(8,128)(2,1)S(1)}, u32[]{:S(2)}, u32[]{:S(2)}) collective-permute-start(bf16[8,128,256]{2,1,0:T(8,128)(2,1)S(1)} %fusion.29), channel_id=1, source_target_pairs={{0,4},{1,5},{2,6},{3,7},{4,0},{5,1},{6,2},{7,3},{8,12},{9,13},{10,... | collective-permute-start | bytes 1572872 | tf_op jit(solution)/shard_map/ppermute | solution.py:535
  533.6 165.1 %reduce-scatter.8.cloned.1.call-start = ((), (), s32[]{:S(2)}) async-start(), calls=%async_computation.6 | async-start | bytes 2621440 | tf_op jit(solution)/shard_map/reduce_scatter | solution.py:782
  535.7 2.1 collective-permute-start.21
  536.5 6.2 collective-permute-start.24
  540.6 15.1 %collective-permute-start.22 = (bf16[8,128,256]{2,1,0:T(8,128)(2,1)}, bf16[8,128,256]{2,1,0:T(8,128)(2,1)}, u32[]{:S(2)}, u32[]{:S(2)}) collective-permute-start(bf16[8,128,256]{2,1,0:T(8,128)(2,1)} %fusion.53), channel_id=1, source_target_pairs={{0,2},{1,3},{2,0},{3,1},{4,6},{5,7},{6,4},{7,5},{8,10},{9,11},{10,... | collective-permute-start | bytes 1572872 | tf_op jit(solution)/shard_map/ppermute | solution.py:535
  546.6 19.6 %collective-permute-start.25 = (bf16[8,128,256]{2,1,0:T(8,128)(2,1)}, bf16[8,128,256]{2,1,0:T(8,128)(2,1)}, u32[]{:S(2)}, u32[]{:S(2)}) collective-permute-start(bf16[8,128,256]{2,1,0:T(8,128)(2,1)} %fusion.52), channel_id=1, source_target_pairs={{0,2},{1,3},{2,0},{3,1},{4,6},{5,7},{6,4},{7,5},{8,10},{9,11},{10,... | collective-permute-start | bytes 1572872 | tf_op jit(solution)/shard_map/ppermute | solution.py:535
  558.0 12.8 %collective-permute-start.23 = (bf16[8,128,256]{2,1,0:T(8,128)(2,1)}, bf16[8,128,256]{2,1,0:T(8,128)(2,1)S(1)}, u32[]{:S(2)}, u32[]{:S(2)}) collective-permute-start(bf16[8,128,256]{2,1,0:T(8,128)(2,1)} %fusion.34), channel_id=1, source_target_pairs={{0,4},{1,5},{2,6},{3,7},{4,0},{5,1},{6,2},{7,3},{8,12},{9,13},{10,... | collective-permute-start | bytes 1572872 | tf_op jit(solution)/shard_map/ppermute | solution.py:535
  654.7 164.5 %reduce-scatter.10.cloned.1.call-start = ((), (), s32[]{:S(2)}) async-start(), calls=%async_computation.7 | async-start | bytes 18874368 | tf_op jit(solution)/shard_map/reduce_scatter | solution.py:785
  655.6 4.3 collective-permute-start.26
  656.9 28.6 %collective-permute-start.27 = (bf16[8,128,256]{2,1,0:T(8,128)(2,1)S(1)}, bf16[8,128,256]{2,1,0:T(8,128)(2,1)S(1)}, u32[]{:S(2)}, u32[]{:S(2)}) collective-permute-start(bf16[8,128,256]{2,1,0:T(8,128)(2,1)S(1)} %copy-done.72), channel_id=1, source_target_pairs={{0,4},{1,5},{2,6},{3,7},{4,0},{5,1},{6,2},{7,3},{8,12},{9,13},{10,... | collective-permute-start | bytes 1572872 | tf_op jit(solution)/shard_map/ppermute | solution.py:535
  698.8 256.9 %reduce-scatter.12.cloned.1.call-start = ((), (), s32[]{:S(2)}) async-start(), calls=%async_computation.8 | async-start | bytes 18874368 | tf_op jit(solution)/shard_map/reduce_scatter | solution.py:785
  771.9 3.5 collective-permute-start.28
  819.2 190.3 %reduce-scatter.14.cloned.1.call-start = ((), (), s32[]{:S(2)}) async-start(), calls=%async_computation.9 | async-start | bytes 2621440 | tf_op jit(solution)/shard_map/reduce_scatter | solution.py:868
  844.1 10.5 %collective-permute-start.29 = (f32[8,256]{1,0:T(8,128)}, f32[8,256]{1,0:T(8,128)}, u32[]{:S(2)}, u32[]{:S(2)}) collective-permute-start(f32[8,256]{1,0:T(8,128)} %slice.404), channel_id=1, source_target_pairs={{1,0},{2,1},{3,2},{4,3},{5,4},{6,5},{7,6},{9,8},{10,9},{11,10},{12... | collective-permute-start | bytes 24584 | tf_op jit(solution)/shard_map/ppermute | solution.py:814
  862.4 35.6 %collective-permute-start.30 = (f32[2,2,43,2048]{3,1,2,0:T(2,128)S(1)}, f32[2,2,43,2048]{3,1,2,0:T(2,128)}, u32[]{:S(2)}, u32[]{:S(2)}) collective-permute-start(f32[2,2,43,2048]{3,1,2,0:T(2,128)S(1)} %bitcast.360), channel_id=1, source_target_pairs={{0,1},{1,0},{2,3},{3,2},{4,5},{5,4},{6,7},{7,6},{8,9},{9,8},{10,11... | collective-permute-start | bytes 4227080 | tf_op jit(solution)/shard_map/ppermute | solution.py:488
  893.5 49.6 %collective-permute-start.33 = (bf16[512,512]{1,0:T(8,128)(2,1)}, bf16[512,512]{1,0:T(8,128)(2,1)}, u32[]{:S(2)}, u32[]{:S(2)}) collective-permute-start(bf16[512,512]{1,0:T(8,128)(2,1)} %get-tuple-element.230), channel_id=1, source_target_pairs={{0,8},{8,16},{16,24},{24,0},{1,9},{9,17},{17,25},{25,1},{2,10},{10... | collective-permute-start | bytes 1572872 | tf_op jit(solution)/shard_map/ppermute | solution.py:518
  894.8 47.9 %collective-permute-start.35 = (bf16[512,512]{1,0:T(8,128)(2,1)}, bf16[512,512]{1,0:T(8,128)(2,1)}, u32[]{:S(2)}, u32[]{:S(2)}) collective-permute-start(bf16[512,512]{1,0:T(8,128)(2,1)} %get-tuple-element.231), channel_id=1, source_target_pairs={{0,24},{8,0},{16,8},{24,16},{1,25},{9,1},{17,9},{25,17},{2,26},{10... | collective-permute-start | bytes 1572872 | tf_op jit(solution)/shard_map/ppermute | solution.py:518
  897.6 45.6 %collective-permute-start.34 = (bf16[512,512]{1,0:T(8,128)(2,1)}, bf16[512,512]{1,0:T(8,128)(2,1)}, u32[]{:S(2)}, u32[]{:S(2)}) collective-permute-start(bf16[512,512]{1,0:T(8,128)(2,1)} %get-tuple-element.232), channel_id=1, source_target_pairs={{0,16},{8,24},{16,0},{24,8},{1,17},{9,25},{17,1},{25,9},{2,18},{10... | collective-permute-start | bytes 1572872 | tf_op jit(solution)/shard_map/ppermute | solution.py:518
  904.1 23.3 %collective-permute-start.31 = (f32[2,43,2048]{2,0,1:T(2,128)S(1)}, f32[2,43,2048]{2,0,1:T(2,128)S(1)}, u32[]{:S(2)}, u32[]{:S(2)}) collective-permute-start(f32[2,43,2048]{2,0,1:T(2,128)S(1)} %bitcast.368), channel_id=1, source_target_pairs={{0,2},{1,3},{2,0},{3,1},{4,6},{5,7},{6,4},{7,5},{8,10},{9,11},{10,... | collective-permute-start | bytes 2113544 | tf_op jit(solution)/shard_map/ppermute | solution.py:488
  931.1 16.6 %collective-permute-start.32 = (f32[43,2048]{1,0:T(8,128)S(1)}, f32[43,2048]{1,0:T(8,128)}, u32[]{:S(2)}, u32[]{:S(2)}) collective-permute-start(f32[43,2048]{1,0:T(8,128)S(1)} %dynamic-slice_bitcast_fusion.1), channel_id=1, source_target_pairs={{0,4},{1,5},{2,6},{3,7},{4,0},{5,1},{6,2},{7,3},{8,12},{9,13},{10,... | collective-permute-start | bytes 1056776 | tf_op jit(solution)/shard_map/ppermute | solution.py:488
  950.3 39.3 %collective-permute-start.36 = (f32[52,512]{1,0:T(8,128)}, f32[52,512]{1,0:T(8,128)}, u32[]{:S(2)}, u32[]{:S(2)}) collective-permute-start(f32[52,512]{1,0:T(8,128)} %get-tuple-element.273), channel_id=1, source_target_pairs={{0,8},{8,16},{16,24},{24,0},{1,9},{9,17},{17,25},{25,1},{2,10},{10... | collective-permute-start | bytes 319496 | tf_op jit(solution)/shard_map/ppermute | solution.py:881
  951.8 37.8 %collective-permute-start.37 = (f32[52,512]{1,0:T(8,128)}, f32[52,512]{1,0:T(8,128)}, u32[]{:S(2)}, u32[]{:S(2)}) collective-permute-start(f32[52,512]{1,0:T(8,128)} %get-tuple-element.274), channel_id=1, source_target_pairs={{0,16},{8,24},{16,0},{24,8},{1,17},{9,25},{17,1},{25,9},{2,18},{10... | collective-permute-start | bytes 319496 | tf_op jit(solution)/shard_map/ppermute | solution.py:881
  954.2 35.5 %collective-permute-start.38 = (f32[52,512]{1,0:T(8,128)}, f32[52,512]{1,0:T(8,128)}, u32[]{:S(2)}, u32[]{:S(2)}) collective-permute-start(f32[52,512]{1,0:T(8,128)} %get-tuple-element.275), channel_id=1, source_target_pairs={{0,24},{8,0},{16,8},{24,16},{1,25},{9,1},{17,9},{25,17},{2,26},{10... | collective-permute-start | bytes 319496 | tf_op jit(solution)/shard_map/ppermute | solution.py:881
  (135 other events, 1243.7 us)
Sparse Core Ops, SparseCore 0:
  53.2 100.2 all-gather.8
  168.5 88.1 all-gather.10
  259.2 101.0 all-gather.12
  533.7 115.6 reduce-scatter.5
  654.8 43.8 reduce-scatter.7
  702.6 116.5 reduce-scatter.9
  823.2 124.8 reduce-scatter.11
  961.0 41.1 reduce-scatter.13

commit v3 on v2

--- a/solution.py
+++ b/solution.py
@@ -580,6 +580,79 @@
     return jnp.stack([first_moment, second_moment, direction])
 
 
+def adam_step(weight_now, gradient, first_moment, second_moment):
+    first_moment = beta_one * first_moment + (1.0 - beta_one) * gradient
+    second_moment = beta_two * second_moment + (1.0 - beta_two) * gradient * gradient
+    direction = (
+        first_moment
+        / (1.0 - beta_one**STEP)
+        / (jnp.sqrt(second_moment / (1.0 - beta_two**STEP)) + adam_eps)
+    )
+    return first_moment, second_moment, direction + decay_rate * weight_now
+
+
+def inner_update_kernel(step_heads, *refs):
+    sums = refs[:-4]
+    weight_ref, moments_ref, grad_ref, update_ref = refs[-4:]
+    width = step_heads * HEAD_DIM
+    for head in range(weight_ref.shape[1]):
+        total = sums[head // step_heads]
+        begin = head % step_heads * HEAD_DIM
+        gate = total[begin : begin + HEAD_DIM].astype(f32)
+        signal = total[width + begin : width + begin + HEAD_DIM].astype(f32)
+        grad_ref[:, head, :] = jnp.concatenate([gate, signal], axis=0).T
+    results = adam_step(weight_ref[...], grad_ref[...], moments_ref[0], moments_ref[1])
+    for place, result in enumerate(results):
+        update_ref[place] = result
+
+
+def update_inner(totals, weight, moments, step_heads):
+    rows, heads, lanes = weight.shape
+    tile = 128
+    flat = pl.BlockSpec((tile, heads, lanes), lambda i: (i, 0, 0))
+    stacked = [pl.BlockSpec((n, tile, heads, lanes), lambda i: (0, i, 0, 0)) for n in (2, 3)]
+    return pl.pallas_call(
+        functools.partial(inner_update_kernel, step_heads),
+        grid=(rows // tile,),
+        in_specs=[pl.BlockSpec((total.shape[0], tile), lambda i: (0, i)) for total in totals]
+        + [flat, stacked[0]],
+        out_specs=[flat, stacked[1]],
+        out_shape=[
+            jax.ShapeDtypeStruct(weight.shape, f32),
+            jax.ShapeDtypeStruct((3,) + weight.shape, f32),
+        ],
+        compiler_params=pltpu.CompilerParams(vmem_limit_bytes=40 * 1024 * 1024),
+        name="inner_update",
+    )(*totals, weight, moments)
+
+
+def output_update_kernel(total_ref, weight_ref, moments_ref, grad_ref, update_ref):
+    gradient = total_ref[...].astype(f32).T
+    grad_ref[...] = gradient
+    results = adam_step(weight_ref[...], gradient, moments_ref[0], moments_ref[1])
+    for place, result in enumerate(results):
+        update_ref[place] = result
+
+
+def update_output(total, weight, moments):
+    rows, columns = weight.shape
+    tile = 128
+    flat = pl.BlockSpec((tile, columns), lambda i: (i, 0))
+    stacked = [pl.BlockSpec((n, tile, columns), lambda i: (0, i, 0)) for n in (2, 3)]
+    return pl.pallas_call(
+        output_update_kernel,
+        grid=(rows // tile,),
+        in_specs=[pl.BlockSpec((columns, tile), lambda i: (0, i)), flat, stacked[0]],
+        out_specs=[flat, stacked[1]],
+        out_shape=[
+            jax.ShapeDtypeStruct(weight.shape, f32),
+            jax.ShapeDtypeStruct((3,) + weight.shape, f32),
+        ],
+        compiler_params=pltpu.CompilerParams(vmem_limit_bytes=40 * 1024 * 1024),
+        name="output_update",
+    )(total, weight, moments)
+
+
 def local(
     tokens,
     cotangent,
@@ -722,19 +795,20 @@
         all_states.append(states)
         all_u.append(u)
     norm_scale = lax.rsqrt(squares / INNER + eps_norm)
-    branch = norm_scale * jnp.einsum(
-        "mtc,mdc->td", gained, out_full, preferred_element_type=f32
-    )
     positions = mine * rows + jnp.arange(rows)
     live = (positions < lengths[0]).astype(f32)[:, None]
-    mixed = (tokens.astype(f32) + live * branch).astype(bf16)
-
     masked = (cotangent.astype(f32) * live).astype(bf16)
-    scaled_sum = jnp.sum(masked.astype(f32) * branch, axis=1, keepdims=True)
-    row_columns = jnp.concatenate(
-        [norm_scale, norm_scale * norm_scale * scaled_sum / INNER], axis=1
-    )
-    normed_grad = jnp.einsum("td,mdc->mtc", masked, out_full, preferred_element_type=f32)
+    scaled_cot = (masked.astype(f32) * norm_scale).astype(bf16)
+    out_part = jnp.einsum(
+        "td,mtc->mcd", scaled_cot, gained, preferred_element_type=f32
+    ).astype(bf16)
+    out_sum = lax.psum_scatter(out_part, "mp", scatter_dimension=0)
+
+    normed_grad = jnp.einsum(
+        "td,mdc->mtc", after(masked, out_part), out_full, preferred_element_type=f32
+    )
+    inner_sum = jnp.sum(normed_grad * gained.astype(f32), axis=(0, 2))[:, None]
+    row_columns = jnp.concatenate([norm_scale, norm_scale**3 * inner_sum / INNER], axis=1)
     starts, gain_sums = [], []
     for group in range(groups):
         start, gain_sum = kernels[group][2](
@@ -743,22 +817,22 @@
         )
         starts.append(start)
         gain_sums.append(gain_sum)
-    scaled_cot = after((masked.astype(f32) * norm_scale).astype(bf16), starts[-1])
-    out_part = jnp.einsum(
-        "td,mtc->mcd", scaled_cot, gained, preferred_element_type=f32
-    ).astype(bf16)
-    out_sum = lax.psum_scatter(out_part, "mp", scatter_dimension=0)
+
+    branch = norm_scale * jnp.einsum(
+        "mtc,mdc->td", gained, after(out_full, *starts), preferred_element_type=f32
+    )
+    mixed = (tokens.astype(f32) + live * branch).astype(bf16)
     carries = []
     for group in range(groups):
-        hold = [starts[1:], [out_part]] if group == 0 else [[out_part]]
+        hold = [starts[1:], [mixed]] if group == 0 else [[mixed]]
         until = shards if group == 0 else shards // 2
         carries.append(carried_states(starts[group], totals_groups[group], True, hold, until))
-    waiting = [carry[1] for carry in carries[1:]] + [out_part]
+    waiting = [carry[1] for carry in carries[1:]] + [mixed]
     dparts, inner_sums, dbc, all_sums, all_dcols = [], [], 0.0, [], []
     for group in range(groups):
         carry = carries[group]
         if group:
-            carry = exchange_states(carry, totals_groups[group], True, dw_part)
+            carry = exchange_states(carry, totals_groups[group], True, inner_part)
         dpart, tail, du_head, sums, dcols, dbc_here = kernels[group][3](
             parts[group], all_u[group], halos[group], normed_grad, gained,
             params[group], columns[group], arows[group], row_columns, writer, reader,
@@ -776,14 +850,12 @@
             dpart, (tail + extra).astype(bf16), (0, rows - 16, 0)
         )
         inner_part = jnp.einsum("td,mtc->mcd", tokens, dpart, preferred_element_type=f32)
-        inner_part = dw_part = inner_part.astype(bf16)
         if group == 0:
             out_sum = after(out_sum, dcols).reshape(chans, -1, own_model).transpose(1, 0, 2)
             out_sum = lax.psum_scatter(out_sum, "dp", scatter_dimension=0)
-            inner_part = after(inner_part, out_sum)
-        inner_part = after(inner_part, *inner_sums)
+        inner_part = after(inner_part.astype(bf16), *(inner_sums or [out_sum]))
         inner_sums.append(lax.psum_scatter(inner_part, "mp", scatter_dimension=0))
-        waiting = [inner_part] + ([out_sum] if group == groups - 2 else [])
+        waiting = [inner_part]
         dparts.append(dpart)
         dbc = dbc + dbc_here
         all_sums.append(sums)
@@ -854,19 +926,18 @@
         )
 
     input_parts = [input_gradient(group, small_grad) for group in range(groups - 1)]
-    output_gradient = after(out_sum, *input_parts).astype(f32).T
-    output_update = adam_rows(output_weight, output_gradient, output_moments, True)
-    inner_grads = [
-        dp_scatter(after(total, *input_parts), output_update) for total in inner_sums[:-1]
-    ]
-    small_total = mp_scatter(small_grad, input_parts + [output_update])
+    inner_grads = [dp_scatter(total, *input_parts) for total in inner_sums[:-1]]
+    output_gradient, output_update = update_output(
+        after(out_sum, *input_parts, *inner_grads), output_weight, output_moments
+    )
+    last_sum = inner_sums[-1].reshape(2 * width, -1, own_model).transpose(1, 0, 2)
+    small_total = mp_scatter(small_grad, [None] + input_parts[:1] + [output_update])
     small_part = lax.dot_general(dsmall, small, (NT, ((), ())), preferred_element_type=f32)
-    last_sum = inner_sums[-1].reshape(2 * width, -1, own_model).transpose(1, 0, 2)
     input_parts.append(input_gradient(groups - 1, small_total, last_sum))
     tokens_gradient = sum(input_parts) + (cotangent.astype(f32) + small_part)
     tokens_gradient = tokens_gradient.astype(bf16)
     last_sum = lax.psum_scatter(last_sum, "dp", scatter_dimension=0)
-    inner_grads.append(last_sum.astype(f32))
+    inner_grads.append(last_sum)
 
     dp_size = lax.axis_size("dp")
     dp_mine = lax.axis_index("dp")
@@ -886,17 +957,15 @@
     own = small_sum[small_rows:].reshape(-1)[:sum_size].reshape(-1, chans)
     step_gradient = small_sum[:heads_here].T
     state_gradient = lax.all_gather(small_sum[heads_here:small_rows], "mp", axis=0, tiled=True).T
-    inner_gradient = jnp.stack(inner_grads)
-    inner_gradient = inner_gradient.reshape(groups, 2, step_heads, HEAD_DIM, own_model)
-    inner_gradient = inner_gradient.transpose(4, 0, 2, 1, 3)
-    inner_gradient = inner_gradient.reshape(own_model, heads_here, 2 * HEAD_DIM)
+    inner_gradient, inner_update = update_inner(
+        inner_grads, inner_weight, inner_moments, step_heads
+    )
     state_filter_gradient = own[CONV + 3 :].reshape(-1)[: (CONV + 1) * 2 * STATE]
     state_filter_gradient = state_filter_gradient.reshape(CONV + 1, 2 * STATE)
     inner_filter_gradient = own[: CONV + 1]
     gain_gradient = own[CONV + 1]
     head_gradient = own[CONV + 2, : 3 * heads_here].reshape(3, heads_here)
 
-    inner_update = adam_rows(inner_weight, inner_gradient, inner_moments, True)
     step_update = adam_rows(step_weight, step_gradient, step_moments, True)
     state_update = adam_rows(state_weight, state_gradient, state_moments, True)
     inner_filter_update = adam_rows(inner_filter, inner_filter_gradient, inner_filter_moments, True)

time: 1050 us -> 1050 us (level)
  Pallas kernels: 248 us -> 259 us
    ppermute x12, waiting for transfers between devices: 58.5 us -> 73 us  [exchange_states(): lax.ppermute(own.astype(bf16), 'mp', [(i, i ^ span) for i in range(device...]
    ppermute x2, starting transfers between devices: 14.4 us -> 2.77 us  [local(): halo = lax.ppermute(part[:, rows - 8:], 'mp', onward)]
    unnamed x295 -> x258, local copies, waits for them, and re-layouts: 51.6 us -> 48.2 us
  transfers between devices with their start and end apart: 47 -> 47, of which waited for: 22 -> 21; matrix products, arithmetic and copies ran while one was open for 31% -> 40% of each run, Pallas kernels for 21% -> 25%
where the time goes in v3:
time: 1050 us; the launch traced here: 1040 us
  Pallas kernels  259 us (25%)
  matrix products  232 us (22%)
  waiting for transfers between devices  201 us (19%)
  local copies, waits for them, and re-layouts  139 us (13%)
  other arithmetic  81.9 us (8%)
  starting transfers between devices  75.5 us (7%)
  blocking collectives  28.2 us (3%)
  between operations  17.2 us (2%)
    pallas_call x2, Pallas kernels, local(): kernels[group][3]  141 us
    ppermute x12, waiting for transfers between devices, dp_gather(): got = lax.ppermute(array, 'dp', [(i, (i + k) % size) for i in range(size)])  88.9 us
    ppermute x12, waiting for transfers between devices, exchange_states(): lax.ppermute(own.astype(bf16), 'mp', [(i, i ^ span) for i in range(device...  73 us
    dot_general x2, matrix products, local(): jnp.einsum('td,mtc->mcd', tokens, dpart, preferred_element_type=f32)  48.7 us
    unnamed x258, local copies, waits for them, and re-layouts  48.2 us
    pallas_call x2, Pallas kernels, local(): kernels[group][1]  47.4 us
    dot_general x2, matrix products, local(): jnp.einsum('td,mdc->mtc', tokens, inner_full[group], preferred_element_ty...  45.3 us
    dot_general x2, matrix products, input_gradient(): jnp.einsum('mtc,mdc->td', after(dparts[group], *others), inner_full[group...  43.6 us
  transfers between devices with their start and end apart: 47, of which 21 were waited for; matrix products, arithmetic and copies ran while one was open for 40% of the time, Pallas kernels for 25%

profile of v3, /device:TPU:0, one launch (start us, length us, event | category | flops | bytes accessed | tf_op | source)
XLA Modules:
  0.0 1035.0 jit_solution(14262859475786333829)
XLA Ops:
  17.4 10.9 %collective-permute-done = bf16[512,512]{1,0:T(8,128)(2,1)} collective-permute-done((bf16[512,512]{1,0:T(8,128)(2,1)S(1)}, bf16[512,512]{1,0:T(8,128)(2,1)}, u32[]{:S(2)}, u32[]{:S(2)}) %collective-permute-start) | collective-permute-done | bytes 524320 | tf_op jit(solution)/shard_map/ppermute | solution.py:503
  29.3 20.6 %collective-permute-done.1 = bf16[512,512]{1,0:T(8,128)(2,1)} collective-permute-done((bf16[512,512]{1,0:T(8,128)(2,1)S(1)}, bf16[512,512]{1,0:T(8,128)(2,1)}, u32[]{:S(2)}, u32[]{:S(2)}) %collective-permute-start.1) | collective-permute-done | bytes 524320 | tf_op jit(solution)/shard_map/ppermute | solution.py:503
  54.1 9.3 all-gather.1
  66.1 10.6 %collective-permute-start.3 = (bf16[512,320]{1,0:T(8,128)(2,1)}, bf16[512,320]{1,0:T(8,128)(2,1)S(1)}, u32[]{:S(2)}, u32[]{:S(2)}) collective-permute-start(bf16[512,320]{1,0:T(8,128)(2,1)} %after.38), channel_id=1, source_target_pairs={{0,8},{8,16},{16,24},{24,0},{1,9},{9,17},{17,25},{25,1},{2,10},{10... | collective-permute-start | bytes 983048 | tf_op jit(solution)/shard_map/ppermute | solution.py:503
  81.9 7.2 collective-permute-done.3
  89.2 16.4 %collective-permute-done.4 = bf16[512,320]{1,0:T(8,128)(2,1)S(1)} collective-permute-done((bf16[512,320]{1,0:T(8,128)(2,1)}, bf16[512,320]{1,0:T(8,128)(2,1)S(1)}, u32[]{:S(2)}, u32[]{:S(2)}) %collective-permute-start.4) | collective-permute-done | bytes 327712 | tf_op jit(solution)/shard_map/ppermute | solution.py:503
  106.9 8.6 collective-permute-start.9
  117.2 5.2 convolution_bitcast_fusion.4
  133.2 9.7 all-gather.4
  143.1 20.0 %collective-permute-done.8.refs_0_ = bf16[512,512]{1,0:T(8,128)(2,1)} collective-permute-done((bf16[512,512]{1,0:T(8,128)(2,1)}, bf16[512,512]{1,0:T(8,128)(2,1)}, u32[]{:S(2)}, u32[]{:S(2)}) %collective-permute-start.8) | collective-permute-done | bytes 524320 | tf_op jit(solution)/shard_map/ppermute | solution.py:503
  171.9 23.2 %convolution_bitcast_fusion.2.x_ref.z_ref.part_ref = f32[8,1024,512]{2,1,0:T(8,128)S(1)} fusion(bf16[8,2048,512]{2,1,0:T(8,128)(2,1)} %after.39, bf16[1024,2048]{1,0:T(8,128)(2,1)} %param.19), kind=kOutput, calls=%fused_computation.8 | convolution fusion | flops 17179869184 | bytes 37748736 | tf_op jit(solution)/shard_map/td,mdc->mtc/dot_general | solution.py:776
  196.7 4.3 copy-done.114
  201.7 13.8 %collective-permute-done.11.refs_0_ = bf16[512,512]{1,0:T(8,128)(2,1)} collective-permute-done((bf16[512,512]{1,0:T(8,128)(2,1)}, bf16[512,512]{1,0:T(8,128)(2,1)}, u32[]{:S(2)}, u32[]{:S(2)}) %collective-permute-start.11) | collective-permute-done | bytes 524320 | tf_op jit(solution)/shard_map/ppermute | solution.py:503
  229.2 14.7 %local_state.2 = (f32[8,128,256]{2,1,0:T(8,128)}, f32[8,1024,256]{2,1,0:T(8,128)}) custom-call(f32[8,1024,512]{2,1,0:T(8,128)} %copy-done.114, f32[8,8,512]{2,1,0:T(8,128)} %after.48.halo_ref, f32[8,8,512]{2,1,0:T(8,128)} %concatenate.71.par_ref, f32[8,1024,20]{2,1,0:T(8,128)} %copy.409.refs_1_.cols_ref, bf16[128,1024]{1,0:T(8,128)(2,1)} %copy.418.bt_ref), custom_call_target="tpu_custom_call" | custom-call | flops 14680064000 | bytes 16777216 | tf_op jit(solution)/shard_map/local_state/pallas_call | solution.py:784
  257.8 9.5 collective-permute-done.15
  276.2 13.1 %collective-permute-done.16 = bf16[8,128,256]{2,1,0:T(8,128)(2,1)S(1)} collective-permute-done((bf16[8,128,256]{2,1,0:T(8,128)(2,1)}, bf16[8,128,256]{2,1,0:T(8,128)(2,1)S(1)}, u32[]{:S(2)}, u32[]{:S(2)}) %collective-permute-start.16) | collective-permute-done | bytes 524320 | tf_op jit(solution)/shard_map/ppermute | solution.py:535
  291.7 23.9 %forward_scan.2 = (bf16[8,1024,512]{2,1,0:T(8,128)(2,1)}, f32[1024,1]{1,0:T(8,128)}, f32[8,5,128,256]{3,2,1,0:T(8,128)}) custom-call(f32[8,1024,512]{2,1,0:T(8,128)} %copy-done.114, f32[8,1024,256]{2,1,0:T(8,128)} %get-tuple-element.48.u_ref, f32[8,8,512]{2,1,0:T(8,128)} %concatenate.71.par_ref, f32[8,1024,20]{2,1,0:T(8,128)} %copy.409.refs_1_.cols_ref, ...), custom_call_target="tpu_custom_call" | custom-call | flops 35651584000 | bytes 20971520 | tf_op jit(solution)/shard_map/forward_scan/pallas_call | solution.py:786
  315.7 22.0 %convolution_bitcast_fusion.1.x_ref.z_ref.part_ref = f32[8,1024,512]{2,1,0:T(8,128)S(1)} fusion(bf16[8,2048,512]{2,1,0:T(8,128)(2,1)} %after.49, bf16[1024,2048]{1,0:T(8,128)(2,1)} %param.19), kind=kOutput, calls=%fused_computation.7 | convolution fusion | flops 17179869184 | bytes 37748736 | tf_op jit(solution)/shard_map/td,mdc->mtc/dot_general | solution.py:776
  347.0 14.8 %local_state.3 = (f32[8,128,256]{2,1,0:T(8,128)}, f32[8,1024,256]{2,1,0:T(8,128)}) custom-call(f32[8,1024,512]{2,1,0:T(8,128)} %copy-done.115, f32[8,8,512]{2,1,0:T(8,128)} %copy-done.118, f32[8,8,512]{2,1,0:T(8,128)} %concatenate.73.par_ref, f32[8,1024,20]{2,1,0:T(8,128)} %copy.430.cols_ref, bf16[128,1024]{1,0:T(8,128)(2,1)} %copy.418.bt_ref), custom_call_target="tpu_custom_call" | custom-call | flops 14680064000 | bytes 16777216 | tf_op jit(solution)/shard_map/local_state/pallas_call | solution.py:784
  370.7 11.0 %collective-permute-done.19 = bf16[8,128,256]{2,1,0:T(8,128)(2,1)S(1)} collective-permute-done((bf16[8,128,256]{2,1,0:T(8,128)(2,1)}, bf16[8,128,256]{2,1,0:T(8,128)(2,1)S(1)}, u32[]{:S(2)}, u32[]{:S(2)}) %collective-permute-start.19) | collective-permute-done | bytes 524320 | tf_op jit(solution)/shard_map/ppermute | solution.py:535
  386.3 4.9 fusion.refs_0_
  391.8 6.2 collective-permute-done.20
  399.2 23.5 %forward_scan.3 = (bf16[8,1024,512]{2,1,0:T(8,128)(2,1)}, f32[1024,1]{1,0:T(8,128)}, f32[8,5,128,256]{3,2,1,0:T(8,128)}) custom-call(f32[8,1024,512]{2,1,0:T(8,128)} %copy-done.115, f32[8,1024,256]{2,1,0:T(8,128)} %get-tuple-element.52.u_ref, f32[8,8,512]{2,1,0:T(8,128)} %concatenate.73.par_ref, ...), custom_call_target="tpu_custom_call", output_to_operand_aliasing={{0}: (9, {})} | custom-call | flops 35651584000 | bytes 20971520 | tf_op jit(solution)/shard_map/forward_scan/pallas_call | solution.py:786
  424.0 25.8 %convolution_convert_fusion.2.refs_1_ = bf16[8,512,2048]{2,1,0:T(8,128)(2,1)} fusion(bf16[8,1024,512]{2,1,0:T(8,128)(2,1)} %get-tuple-element.56.gated_ref.gained_ref, bf16[1024,2048]{1,0:T(8,128)(2,1)} %fusion.refs_0_, f32[1024]{0:T(1024)S(1)} %get-tuple-element.219), kind=kOutput, calls=%fused_computation.3 | convolution fusion | flops 17194549248 | bytes 29364224 | tf_op jit(solution)/shard_map/td,mtc->mcd/dot_general | solution.py:802
  452.2 27.0 %multiply_reduce_fusion = (f32[1024]{0:T(1024)S(1)}, f32[8,1024,512]{2,1,0:T(8,128)}) fusion(bf16[8,1024,512]{2,1,0:T(8,128)(2,1)} %get-tuple-element.56.gated_ref.gained_ref, bf16[8,2048,512]{2,1,0:T(8,128)(2,1)} %bitcast.303, bf16[1024,2048]{1,0:T(8,128)(2,1)} %after.50), kind=kOutput, calls=%fused_computation | convolution fusion | flops 17192452096 | bytes 46141440 | tf_op jit(solution)/shard_map/td,mdc->mtc/dot_general | solution.py:807
  481.5 16.6 %back_state.2 = (f32[8,128,256]{2,1,0:T(8,128)}, f32[8,8,256]{2,1,0:T(8,128)}) custom-call(f32[8,1024,512]{2,1,0:T(8,128)} %copy-done.114, f32[8,1024,512]{2,1,0:T(8,128)} %get-tuple-element.307.ngrad_ref, bf16[8,1024,512]{2,1,0:T(8,128)(2,1)} %get-tuple-element.56.gated_ref.gained_ref, f32[8,8,512]{2,1,0:T(8,128)} %concatenate.71.par_ref, ...), custom_call_target="tpu_custom_call" | custom-call | flops 16777216000 | bytes 29360128 | tf_op jit(solution)/shard_map/back_state/pallas_call | solution.py:814
  500.3 16.6 %back_state.3 = (f32[8,128,256]{2,1,0:T(8,128)}, f32[8,8,256]{2,1,0:T(8,128)}) custom-call(f32[8,1024,512]{2,1,0:T(8,128)} %copy-done.115, f32[8,1024,512]{2,1,0:T(8,128)} %get-tuple-element.307.ngrad_ref, bf16[8,1024,512]{2,1,0:T(8,128)(2,1)} %get-tuple-element.56.gated_ref.gained_ref, f32[8,8,512]{2,1,0:T(8,128)} %concatenate.73.par_ref, ...), custom_call_target="tpu_custom_call" | custom-call | flops 16777216000 | bytes 29360128 | tf_op jit(solution)/shard_map/back_state/pallas_call | solution.py:814
  521.9 24.4 %fusion.5.refs_1_.refs_2_ = bf16[1024,2048]{1,0:T(8,128)(2,1)} fusion(bf16[1024,2048]{1,0:T(8,128)(2,1)} %param.19, bf16[8,1024,512]{2,1,0:T(8,128)(2,1)} %get-tuple-element.56.gated_ref.gained_ref, bf16[8,2048,512]{2,1,0:T(8,128)(2,1)} %after.53, f32[1024]{0:T(1024)S(1)} %get-tuple-element.219, f32[1024]{0:T(1024)S(1)} %copy-done.84), kind=kOutput, calls=%fused_computation.16 | convolution fusion | flops 17190354944 | bytes 33562624 | tf_op jit(solution)/shard_map/mtc,mdc->td/dot_general | solution.py:821
  557.6 18.1 %collective-permute-done.25 = bf16[8,128,256]{2,1,0:T(8,128)(2,1)} collective-permute-done((bf16[8,128,256]{2,1,0:T(8,128)(2,1)}, bf16[8,128,256]{2,1,0:T(8,128)(2,1)}, u32[]{:S(2)}, u32[]{:S(2)}) %collective-permute-start.25) | collective-permute-done | bytes 524320 | tf_op jit(solution)/shard_map/ppermute | solution.py:535
  583.0 69.2 %backward_scan.2 = (bf16[8,1024,512]{2,1,0:T(8,128)(2,1)}, f32[8,16,512]{2,1,0:T(8,128)}, f32[8,8,512]{2,1,0:T(8,128)}, f32[8,8,256]{2,1,0:T(8,128)}, f32[8,1024,8]{2,1,0:T(8,128)}, /*index=5*/f32[1024,256]{1,0:T(8,128)}) custom-call(f32[8,1024,512]{2,1,0:T(8,128)} %copy-done.114, f32[8,1024,256]{2,1,0:T(8,128)} %get-tuple-element.48.u_ref, ...), custom_call_target="tpu_custom_call" | custom-call | flops 90177536000 | bytes 41943040 | tf_op jit(solution)/shard_map/backward_scan/pallas_call | solution.py:836
  661.9 24.8 %convolution_convert_fusion.1.refs_0_ = bf16[8,512,2048]{2,1,0:T(8,128)(2,1)} fusion(bf16[8,1024,512]{2,1,0:T(8,128)(2,1)} %fusion.67.refs_0_, bf16[1024,2048]{1,0:T(8,128)(2,1)} %param.19), kind=kOutput, calls=%fused_computation.2 | convolution fusion | flops 17188257792 | bytes 29360128 | tf_op jit(solution)/shard_map/td,mtc->mcd/dot_general | solution.py:852
  686.7 12.4 %reduce-scatter.8.cloned.1.call-done = bf16[1,512,512]{2,1,0:T(8,128)(2,1)} async-done(((bf16[4,512,512]{2,1,0:T(8,128)(2,1)}), bf16[1,512,512]{2,1,0:T(8,128)(2,1)}) %reduce-scatter.8.cloned.1.call-update) | async-done | bytes 524304 | tf_op jit(solution)/shard_map/reduce_scatter | solution.py:855
  702.2 11.5 %collective-permute-done.27.refs_0_ = bf16[8,128,256]{2,1,0:T(8,128)(2,1)S(1)} collective-permute-done((bf16[8,128,256]{2,1,0:T(8,128)(2,1)S(1)}, bf16[8,128,256]{2,1,0:T(8,128)(2,1)S(1)}, u32[]{:S(2)}, u32[]{:S(2)}) %collective-permute-start.27) | collective-permute-done | bytes 524320 | tf_op jit(solution)/shard_map/ppermute | solution.py:535
  717.4 71.9 %backward_scan.3 = (bf16[8,1024,512]{2,1,0:T(8,128)(2,1)}, f32[8,16,512]{2,1,0:T(8,128)}, f32[8,8,512]{2,1,0:T(8,128)}, f32[8,8,256]{2,1,0:T(8,128)}, f32[8,1024,8]{2,1,0:T(8,128)}, /*index=5*/f32[1024,256]{1,0:T(8,128)}) custom-call(f32[8,1024,512]{2,1,0:T(8,128)} %copy-done.115, f32[8,1024,256]{2,1,0:T(8,128)} %get-tuple-element.52.u_ref, ...), custom_call_target="tpu_custom_call" | custom-call | flops 90177536000 | bytes 41943040 | tf_op jit(solution)/shard_map/backward_scan/pallas_call | solution.py:836
  794.5 23.9 %convolution_convert_fusion.refs_0_ = bf16[8,512,2048]{2,1,0:T(8,128)(2,1)} fusion(bf16[8,1024,512]{2,1,0:T(8,128)(2,1)} %fusion.66.refs_0_, bf16[1024,2048]{1,0:T(8,128)(2,1)S(1)} %copy-done.117), kind=kOutput, calls=%fused_computation.1 | convolution fusion | flops 17188257792 | bytes 29360128 | tf_op jit(solution)/shard_map/td,mtc->mcd/dot_general | solution.py:852
  829.7 4.5 copy.451
  838.1 4.7 fusion.117
  856.9 4.8 fusion.57
  866.7 4.6 collective-permute-start.30
  877.0 4.0 collective-permute-start.35
  892.2 22.0 %convolution_bitcast_fusion.3.refs_1_ = f32[1024,2048]{1,0:T(8,128)} fusion(bf16[8,1024,512]{2,1,0:T(8,128)(2,1)S(1)} %copy-done.21, bf16[8,2048,512]{2,1,0:T(8,128)(2,1)} %after.39), kind=kOutput, calls=%fused_computation.18 | convolution fusion | flops 17179869184 | bytes 33554432 | tf_op jit(solution)/shard_map/mtc,mdc->td/dot_general | solution.py:923
  914.6 6.1 collective-permute-done.31
  938.2 6.8 collective-permute-done.32.refs_0_
  951.6 8.6 reduce-scatter.12.cloned.1.call-done
  965.6 21.6 %fusion.138 = f32[1024,2048,1]{1,0,2:T(8,128)S(1)} fusion(bf16[8,1024,512]{2,1,0:T(8,128)(2,1)} %after.72, bf16[8,2048,512]{2,1,0:T(8,128)(2,1)} %after.49), kind=kOutput, calls=%fused_computation.345 | convolution fusion | flops 17179869184 | bytes 33554432 | tf_op jit(solution)/shard_map/mtc,mdc->td/dot_general | solution.py:923
  987.2 7.0 fusion.2.refs_1_
  999.6 9.2 all_gather.39
  1022.4 5.4 inner_update.1
  (669 shorter events, 263.1 us)
Async XLA Ops:
  7.2 164.7 %all-gather.9.cloned.1.call-start = ((), (), s32[]{:S(2)}) async-start(), calls=%async_computation.10 | async-start | bytes 18874368 | tf_op jit(solution)/shard_map/all_gather | solution.py:770
  10.2 18.1 %collective-permute-start = (bf16[512,512]{1,0:T(8,128)(2,1)S(1)}, bf16[512,512]{1,0:T(8,128)(2,1)}, u32[]{:S(2)}, u32[]{:S(2)}) collective-permute-start(bf16[512,512]{1,0:T(8,128)(2,1)S(1)} %copy.391), channel_id=1, source_target_pairs={{0,8},{8,16},{16,24},{24,0},{1,9},{9,17},{17,25},{25,1},{2,10},{10... | collective-permute-start | bytes 1572872 | tf_op jit(solution)/shard_map/ppermute | solution.py:503
  13.2 36.7 %collective-permute-start.1 = (bf16[512,512]{1,0:T(8,128)(2,1)S(1)}, bf16[512,512]{1,0:T(8,128)(2,1)}, u32[]{:S(2)}, u32[]{:S(2)}) collective-permute-start(bf16[512,512]{1,0:T(8,128)(2,1)S(1)} %copy.391), channel_id=1, source_target_pairs={{0,16},{8,24},{16,0},{24,8},{1,17},{9,25},{17,1},{25,9},{2,18},{10... | collective-permute-start | bytes 1572872 | tf_op jit(solution)/shard_map/ppermute | solution.py:503
  15.8 35.2 %collective-permute-start.2 = (bf16[512,512]{1,0:T(8,128)(2,1)S(1)}, bf16[512,512]{1,0:T(8,128)(2,1)}, u32[]{:S(2)}, u32[]{:S(2)}) collective-permute-start(bf16[512,512]{1,0:T(8,128)(2,1)S(1)} %copy.391), channel_id=1, source_target_pairs={{0,24},{8,0},{16,8},{24,16},{1,25},{9,1},{17,9},{25,17},{2,26},{10... | collective-permute-start | bytes 1572872 | tf_op jit(solution)/shard_map/ppermute | solution.py:503
  53.4 262.3 %all-gather.11.cloned.1.call-start = ((), (), s32[]{:S(2)}) async-start(), calls=%async_computation.11 | async-start | bytes 18874368 | tf_op jit(solution)/shard_map/all_gather | solution.py:770
  66.1 23.0 %collective-permute-start.3 = (bf16[512,320]{1,0:T(8,128)(2,1)}, bf16[512,320]{1,0:T(8,128)(2,1)S(1)}, u32[]{:S(2)}, u32[]{:S(2)}) collective-permute-start(bf16[512,320]{1,0:T(8,128)(2,1)} %after.38), channel_id=1, source_target_pairs={{0,8},{8,16},{16,24},{24,0},{1,9},{9,17},{17,25},{25,1},{2,10},{10... | collective-permute-start | bytes 983048 | tf_op jit(solution)/shard_map/ppermute | solution.py:503
  76.8 28.8 %collective-permute-start.4 = (bf16[512,320]{1,0:T(8,128)(2,1)}, bf16[512,320]{1,0:T(8,128)(2,1)S(1)}, u32[]{:S(2)}, u32[]{:S(2)}) collective-permute-start(bf16[512,320]{1,0:T(8,128)(2,1)} %after.38), channel_id=1, source_target_pairs={{0,16},{8,24},{16,0},{24,8},{1,17},{9,25},{17,1},{25,9},{2,18},{10... | collective-permute-start | bytes 983048 | tf_op jit(solution)/shard_map/ppermute | solution.py:503
  80.7 25.0 %collective-permute-start.5 = (bf16[512,320]{1,0:T(8,128)(2,1)}, bf16[512,320]{1,0:T(8,128)(2,1)S(1)}, u32[]{:S(2)}, u32[]{:S(2)}) collective-permute-start(bf16[512,320]{1,0:T(8,128)(2,1)} %after.38), channel_id=1, source_target_pairs={{0,24},{8,0},{16,8},{24,16},{1,25},{9,1},{17,9},{25,17},{2,26},{10... | collective-permute-start | bytes 983048 | tf_op jit(solution)/shard_map/ppermute | solution.py:503
  106.9 36.2 %collective-permute-start.9 = (bf16[512,512]{1,0:T(8,128)(2,1)}, bf16[512,512]{1,0:T(8,128)(2,1)}, u32[]{:S(2)}, u32[]{:S(2)}) collective-permute-start(bf16[512,512]{1,0:T(8,128)(2,1)} %after.40), channel_id=1, source_target_pairs={{0,24},{8,0},{16,8},{24,16},{1,25},{9,1},{17,9},{25,17},{2,26},{10... | collective-permute-start | bytes 1572872 | tf_op jit(solution)/shard_map/ppermute | solution.py:503
  115.5 47.7 %collective-permute-start.8 = (bf16[512,512]{1,0:T(8,128)(2,1)}, bf16[512,512]{1,0:T(8,128)(2,1)}, u32[]{:S(2)}, u32[]{:S(2)}) collective-permute-start(bf16[512,512]{1,0:T(8,128)(2,1)} %after.40), channel_id=1, source_target_pairs={{0,16},{8,24},{16,0},{24,8},{1,17},{9,25},{17,1},{25,9},{2,18},{10... | collective-permute-start | bytes 1572872 | tf_op jit(solution)/shard_map/ppermute | solution.py:503
  117.2 46.0 %collective-permute-start.7 = (bf16[512,512]{1,0:T(8,128)(2,1)}, bf16[512,512]{1,0:T(8,128)(2,1)}, u32[]{:S(2)}, u32[]{:S(2)}) collective-permute-start(bf16[512,512]{1,0:T(8,128)(2,1)} %after.40), channel_id=1, source_target_pairs={{0,8},{8,16},{16,24},{24,0},{1,9},{9,17},{17,25},{25,1},{2,10},{10... | collective-permute-start | bytes 1572872 | tf_op jit(solution)/shard_map/ppermute | solution.py:503
  167.9 284.4 %all-gather.13.cloned.1.call-start = ((), (), s32[]{:S(2)}) async-start(), calls=%async_computation.12 | async-start | bytes 18874368 | tf_op jit(solution)/shard_map/all_gather | solution.py:782
  168.8 32.2 %collective-permute-start.12 = (bf16[512,512]{1,0:T(8,128)(2,1)}, bf16[512,512]{1,0:T(8,128)(2,1)}, u32[]{:S(2)}, u32[]{:S(2)}) collective-permute-start(bf16[512,512]{1,0:T(8,128)(2,1)} %after.44), channel_id=1, source_target_pairs={{0,24},{8,0},{16,8},{24,16},{1,25},{9,1},{17,9},{25,17},{2,26},{10... | collective-permute-start | bytes 1572872 | tf_op jit(solution)/shard_map/ppermute | solution.py:503
  168.8 46.7 %collective-permute-start.11 = (bf16[512,512]{1,0:T(8,128)(2,1)}, bf16[512,512]{1,0:T(8,128)(2,1)}, u32[]{:S(2)}, u32[]{:S(2)}) collective-permute-start(bf16[512,512]{1,0:T(8,128)(2,1)} %after.44), channel_id=1, source_target_pairs={{0,16},{8,24},{16,0},{24,8},{1,17},{9,25},{17,1},{25,9},{2,18},{10... | collective-permute-start | bytes 1572872 | tf_op jit(solution)/shard_map/ppermute | solution.py:503
  169.5 46.0 %collective-permute-start.10 = (bf16[512,512]{1,0:T(8,128)(2,1)}, bf16[512,512]{1,0:T(8,128)(2,1)}, u32[]{:S(2)}, u32[]{:S(2)}) collective-permute-start(bf16[512,512]{1,0:T(8,128)(2,1)} %after.44), channel_id=1, source_target_pairs={{0,8},{8,16},{16,24},{24,0},{1,9},{9,17},{17,25},{25,1},{2,10},{10... | collective-permute-start | bytes 1572872 | tf_op jit(solution)/shard_map/ppermute | solution.py:503
  195.2 5.8 collective-permute-start.6
  220.1 432.2 %reduce-scatter.6.cloned.1.call-start = ((), (), s32[]{:S(2)}) async-start(), calls=%async_computation.5 | async-start | bytes 18874368 | tf_op jit(solution)/shard_map/reduce_scatter | solution.py:805
  220.2 119.1 %copy-start.54 = (f32[8,8,256]{2,1,0:T(8,128)}, f32[8,8,256]{2,1,0:T(8,128)S(1)}, u32[]{:S(2)}) copy-start(f32[8,8,256]{2,1,0:T(8,128)S(1)} %get-tuple-element.260) | copy-start | bytes 196612
  221.0 3.9 collective-permute-start.13
  246.0 4.6 collective-permute-start.14
  252.9 14.4 %collective-permute-start.15 = (bf16[8,128,256]{2,1,0:T(8,128)(2,1)}, bf16[8,128,256]{2,1,0:T(8,128)(2,1)}, u32[]{:S(2)}, u32[]{:S(2)}) collective-permute-start(bf16[8,128,256]{2,1,0:T(8,128)(2,1)} %fusion.50), channel_id=1, source_target_pairs={{0,2},{1,3},{2,0},{3,1},{4,6},{5,7},{6,4},{7,5},{8,10},{9,11},{10,... | collective-permute-start | bytes 1572872 | tf_op jit(solution)/shard_map/ppermute | solution.py:535
  269.6 19.7 %collective-permute-start.16 = (bf16[8,128,256]{2,1,0:T(8,128)(2,1)}, bf16[8,128,256]{2,1,0:T(8,128)(2,1)S(1)}, u32[]{:S(2)}, u32[]{:S(2)}) collective-permute-start(bf16[8,128,256]{2,1,0:T(8,128)(2,1)} %fusion.18), channel_id=1, source_target_pairs={{0,4},{1,5},{2,6},{3,7},{4,0},{5,1},{6,2},{7,3},{8,12},{9,13},{10,... | collective-permute-start | bytes 1572872 | tf_op jit(solution)/shard_map/ppermute | solution.py:535
  337.8 8.5 collective-permute-start.17
  363.1 2.0 collective-permute-start.18
  367.3 14.3 %collective-permute-start.19 = (bf16[8,128,256]{2,1,0:T(8,128)(2,1)}, bf16[8,128,256]{2,1,0:T(8,128)(2,1)S(1)}, u32[]{:S(2)}, u32[]{:S(2)}) collective-permute-start(bf16[8,128,256]{2,1,0:T(8,128)(2,1)} %fusion.49), channel_id=1, source_target_pairs={{0,2},{1,3},{2,0},{3,1},{4,6},{5,7},{6,4},{7,5},{8,10},{9,11},{10,... | collective-permute-start | bytes 1572872 | tf_op jit(solution)/shard_map/ppermute | solution.py:535
  382.7 15.2 %collective-permute-start.20 = (bf16[8,128,256]{2,1,0:T(8,128)(2,1)}, bf16[8,128,256]{2,1,0:T(8,128)(2,1)S(1)}, u32[]{:S(2)}, u32[]{:S(2)}) collective-permute-start(bf16[8,128,256]{2,1,0:T(8,128)(2,1)} %fusion.23), channel_id=1, source_target_pairs={{0,4},{1,5},{2,6},{3,7},{4,0},{5,1},{6,2},{7,3},{8,12},{9,13},{10,... | collective-permute-start | bytes 1572872 | tf_op jit(solution)/shard_map/ppermute | solution.py:535
  449.8 249.4 %reduce-scatter.8.cloned.1.call-start = ((), (), s32[]{:S(2)}) async-start(), calls=%async_computation.6 | async-start | bytes 2621440 | tf_op jit(solution)/shard_map/reduce_scatter | solution.py:855
  500.3 19.0 %collective-permute-start.21 = (bf16[8,128,256]{2,1,0:T(8,128)(2,1)}, bf16[8,128,256]{2,1,0:T(8,128)(2,1)}, u32[]{:S(2)}, u32[]{:S(2)}) collective-permute-start(bf16[8,128,256]{2,1,0:T(8,128)(2,1)} %convert_element_type.200), channel_id=1, source_target_pairs={{0,1},{1,0},{2,3},{3,2},{4,5},{5,4},{6,7},{7,6},{8,9},{9,8},{10,11... | collective-permute-start | bytes 1572872 | tf_op jit(solution)/shard_map/ppermute | solution.py:535
  519.0 27.4 %collective-permute-start.24 = (bf16[8,128,256]{2,1,0:T(8,128)(2,1)}, bf16[8,128,256]{2,1,0:T(8,128)(2,1)}, u32[]{:S(2)}, u32[]{:S(2)}) collective-permute-start(bf16[8,128,256]{2,1,0:T(8,128)(2,1)} %convert_element_type.206), channel_id=1, source_target_pairs={{0,1},{1,0},{2,3},{3,2},{4,5},{5,4},{6,7},{7,6},{8,9},{9,8},{10,11... | collective-permute-start | bytes 1572872 | tf_op jit(solution)/shard_map/ppermute | solution.py:535
  521.6 30.9 %collective-permute-start.22 = (bf16[8,128,256]{2,1,0:T(8,128)(2,1)}, bf16[8,128,256]{2,1,0:T(8,128)(2,1)}, u32[]{:S(2)}, u32[]{:S(2)}) collective-permute-start(bf16[8,128,256]{2,1,0:T(8,128)(2,1)} %fusion.48), channel_id=1, source_target_pairs={{0,2},{1,3},{2,0},{3,1},{4,6},{5,7},{6,4},{7,5},{8,10},{9,11},{10,... | collective-permute-start | bytes 1572872 | tf_op jit(solution)/shard_map/ppermute | solution.py:535
  549.6 26.0 %collective-permute-start.25 = (bf16[8,128,256]{2,1,0:T(8,128)(2,1)}, bf16[8,128,256]{2,1,0:T(8,128)(2,1)}, u32[]{:S(2)}, u32[]{:S(2)}) collective-permute-start(bf16[8,128,256]{2,1,0:T(8,128)(2,1)} %fusion.47), channel_id=1, source_target_pairs={{0,2},{1,3},{2,0},{3,1},{4,6},{5,7},{6,4},{7,5},{8,10},{9,11},{10,... | collective-permute-start | bytes 1572872 | tf_op jit(solution)/shard_map/ppermute | solution.py:535
  554.8 25.8 %collective-permute-start.23 = (bf16[8,128,256]{2,1,0:T(8,128)(2,1)}, bf16[8,128,256]{2,1,0:T(8,128)(2,1)S(1)}, u32[]{:S(2)}, u32[]{:S(2)}) collective-permute-start(bf16[8,128,256]{2,1,0:T(8,128)(2,1)} %fusion.28), channel_id=1, source_target_pairs={{0,4},{1,5},{2,6},{3,7},{4,0},{5,1},{6,2},{7,3},{8,12},{9,13},{10,... | collective-permute-start | bytes 1572872 | tf_op jit(solution)/shard_map/ppermute | solution.py:535
  657.6 162.0 %reduce-scatter.10.cloned.1.call-start = ((), (), s32[]{:S(2)}) async-start(), calls=%async_computation.7 | async-start | bytes 18874368 | tf_op jit(solution)/shard_map/reduce_scatter | solution.py:857
  657.6 3.5 collective-permute-start.26
  699.2 261.1 %reduce-scatter.12.cloned.1.call-start = ((), (), s32[]{:S(2)}) async-start(), calls=%async_computation.8 | async-start | bytes 18874368 | tf_op jit(solution)/shard_map/reduce_scatter | solution.py:857
  700.2 13.5 %collective-permute-start.27 = (bf16[8,128,256]{2,1,0:T(8,128)(2,1)S(1)}, bf16[8,128,256]{2,1,0:T(8,128)(2,1)S(1)}, u32[]{:S(2)}, u32[]{:S(2)}) collective-permute-start(bf16[8,128,256]{2,1,0:T(8,128)(2,1)S(1)} %copy-done.59), channel_id=1, source_target_pairs={{0,4},{1,5},{2,6},{3,7},{4,0},{5,1},{6,2},{7,3},{8,12},{9,13},{10,... | collective-permute-start | bytes 1572872 | tf_op jit(solution)/shard_map/ppermute | solution.py:535
  789.3 3.5 collective-permute-start.28
  819.7 199.5 %reduce-scatter.14.cloned.1.call-start = ((), (), s32[]{:S(2)}) async-start(), calls=%async_computation.9 | async-start | bytes 2621440 | tf_op jit(solution)/shard_map/reduce_scatter | solution.py:939
  845.5 10.1 collective-permute-start.29
  866.7 17.5 %collective-permute-start.30 = (f32[2,2,43,2048]{3,1,2,0:T(2,128)}, f32[2,2,43,2048]{3,1,2,0:T(2,128)}, u32[]{:S(2)}, u32[]{:S(2)}) collective-permute-start(f32[2,2,43,2048]{3,1,2,0:T(2,128)} %bitcast.289), channel_id=1, source_target_pairs={{0,1},{1,0},{2,3},{3,2},{4,5},{5,4},{6,7},{7,6},{8,9},{9,8},{10,11... | collective-permute-start | bytes 4227080 | tf_op jit(solution)/shard_map/ppermute | solution.py:488
  877.0 52.8 %collective-permute-start.33 = (bf16[512,512]{1,0:T(8,128)(2,1)}, bf16[512,512]{1,0:T(8,128)(2,1)}, u32[]{:S(2)}, u32[]{:S(2)}) collective-permute-start(bf16[512,512]{1,0:T(8,128)(2,1)} %get-tuple-element.229), channel_id=1, source_target_pairs={{0,8},{8,16},{16,24},{24,0},{1,9},{9,17},{17,25},{25,1},{2,10},{10... | collective-permute-start | bytes 1572872 | tf_op jit(solution)/shard_map/ppermute | solution.py:518
  877.0 52.8 %collective-permute-start.35 = (bf16[512,512]{1,0:T(8,128)(2,1)}, bf16[512,512]{1,0:T(8,128)(2,1)}, u32[]{:S(2)}, u32[]{:S(2)}) collective-permute-start(bf16[512,512]{1,0:T(8,128)(2,1)} %get-tuple-element.230), channel_id=1, source_target_pairs={{0,24},{8,0},{16,8},{24,16},{1,25},{9,1},{17,9},{25,17},{2,26},{10... | collective-permute-start | bytes 1572872 | tf_op jit(solution)/shard_map/ppermute | solution.py:518
  881.0 48.8 %collective-permute-start.34 = (bf16[512,512]{1,0:T(8,128)(2,1)}, bf16[512,512]{1,0:T(8,128)(2,1)}, u32[]{:S(2)}, u32[]{:S(2)}) collective-permute-start(bf16[512,512]{1,0:T(8,128)(2,1)} %get-tuple-element.231), channel_id=1, source_target_pairs={{0,16},{8,24},{16,0},{24,8},{1,17},{9,25},{17,1},{25,9},{2,18},{10... | collective-permute-start | bytes 1572872 | tf_op jit(solution)/shard_map/ppermute | solution.py:518
  890.6 30.1 %collective-permute-start.31 = (f32[2,43,2048]{2,0,1:T(2,128)S(1)}, f32[2,43,2048]{2,0,1:T(2,128)S(1)}, u32[]{:S(2)}, u32[]{:S(2)}) collective-permute-start(f32[2,43,2048]{2,0,1:T(2,128)S(1)} %bitcast.333), channel_id=1, source_target_pairs={{0,2},{1,3},{2,0},{3,1},{4,6},{5,7},{6,4},{7,5},{8,10},{9,11},{10,... | collective-permute-start | bytes 2113544 | tf_op jit(solution)/shard_map/ppermute | solution.py:488
  925.3 19.7 %collective-permute-start.32 = (f32[43,2048]{1,0:T(8,128)}, f32[43,2048]{1,0:T(8,128)}, u32[]{:S(2)}, u32[]{:S(2)}) collective-permute-start(f32[43,2048]{1,0:T(8,128)} %dynamic-slice_bitcast_fusion.3), channel_id=1, source_target_pairs={{0,4},{1,5},{2,6},{3,7},{4,0},{5,1},{6,2},{7,3},{8,12},{9,13},{10,... | collective-permute-start | bytes 1056776 | tf_op jit(solution)/shard_map/ppermute | solution.py:488
  946.2 48.0 %collective-permute-start.36 = (f32[52,512]{1,0:T(8,128)S(1)}, f32[52,512]{1,0:T(8,128)S(1)}, u32[]{:S(2)}, u32[]{:S(2)}) collective-permute-start(f32[52,512]{1,0:T(8,128)S(1)} %get-tuple-element.274), channel_id=1, source_target_pairs={{0,8},{8,16},{16,24},{24,0},{1,9},{9,17},{17,25},{25,1},{2,10},{10... | collective-permute-start | bytes 319496 | tf_op jit(solution)/shard_map/ppermute | solution.py:952
  947.7 47.1 %collective-permute-start.37 = (f32[52,512]{1,0:T(8,128)S(1)}, f32[52,512]{1,0:T(8,128)S(1)}, u32[]{:S(2)}, u32[]{:S(2)}) collective-permute-start(f32[52,512]{1,0:T(8,128)S(1)} %get-tuple-element.275), channel_id=1, source_target_pairs={{0,16},{8,24},{16,0},{24,8},{1,17},{9,25},{17,1},{25,9},{2,18},{10... | collective-permute-start | bytes 319496 | tf_op jit(solution)/shard_map/ppermute | solution.py:952
  949.9 45.6 %collective-permute-start.38 = (f32[52,512]{1,0:T(8,128)S(1)}, f32[52,512]{1,0:T(8,128)S(1)}, u32[]{:S(2)}, u32[]{:S(2)}) collective-permute-start(f32[52,512]{1,0:T(8,128)S(1)} %get-tuple-element.276), channel_id=1, source_target_pairs={{0,24},{8,0},{16,8},{24,16},{1,25},{9,1},{17,9},{25,17},{2,26},{10... | collective-permute-start | bytes 319496 | tf_op jit(solution)/shard_map/ppermute | solution.py:952
  (119 other events, 1299.3 us)
Sparse Core Ops, SparseCore 0:
  53.5 100.2 all-gather.8
  168.0 87.7 all-gather.10
  258.2 101.9 all-gather.12
  449.9 135.8 reduce-scatter.5
  657.7 41.3 reduce-scatter.7
  703.0 116.5 reduce-scatter.9
  823.6 136.6 reduce-scatter.11
  965.7 43.8 reduce-scatter.13
